TPU v7x, 32 devices: a whole 2x2x4 slice. The times are simulated.
32 devices in a mesh: dp: 2 (over core), seq: 4 (over y, x), tensor: 4 (over z).
Axes of the slice: x: 2, y: 2, z: 4, core: 2. Of those that a mesh axis runs over, the one named last changes fastest.
Arguments:
- hidden: bfloat16 [4096, 7168], P(('dp', 'seq')), may hold values from -34 to 34
- grad_out: bfloat16 [4096, 4096], P(('dp', 'seq'), 'tensor'), may hold values from -24 to 24
- master_weight: float32 [7168, 4096], P(('dp', 'seq'), 'tensor'), may hold values from -6 to 6
- row_prev: float32 [7168], P(('dp', 'seq')), may hold values from 0.01 to 0.3
- col_prev: float32 [4096], P('tensor'), may hold values from 0.01 to 0.3
Outputs:
- new_weight: bfloat16 [7168, 4096], P('dp', 'tensor')
- update: float32 [7168, 4096], P(('dp', 'seq'), 'tensor')
- new_rows: float32 [7168], P(('dp', 'seq'))
- new_cols: float32 [4096], P('tensor')
All inputs are finite; a program needn't handle non-finite values.
Results may differ from a plain program's by a relative error of at most 0.0004.
Values may be sent and summed in bfloat16 or wider, within the bound.
No kernel may reach another device: no remote copies, remote signals or barrier semaphores. Data moves between devices by JAX's collectives and lax.ppermute only.
A program may use at most 128 MiB of HBM per device.

v0:
```python
import jax
import jax.numpy as jnp
from jax import lax
from jax.sharding import PartitionSpec as P

D = 4096
FF_WIN = 7168


decay_rate = 0.8
learn_rate = 0.05
small_term = 1e-06


def per_device(hidden, grad_out, master_weight, row_prev, col_prev):
    grads = lax.psum_scatter(
        lax.dot_general(
            hidden, grad_out, (((0,), (0,)), ((), ())), preferred_element_type=jnp.float32
        ),
        ("dp", "seq"),
        scatter_dimension=0,
        tiled=True,
    )
    squares = grads * grads + small_term
    col_total = lax.psum(jnp.sum(squares, axis=0), ("dp", "seq"))
    row_total = lax.psum(jnp.sum(squares, axis=1), "tensor")
    new_rows = decay_rate * row_prev + (1.0 - decay_rate) * row_total / D
    new_cols = decay_rate * col_prev + (1.0 - decay_rate) * col_total / FF_WIN
    second = new_rows[:, None] * new_cols[None, :]
    raw = grads / jnp.sqrt(second)
    raw_total = lax.psum(jnp.sum(raw * raw), ("dp", "seq", "tensor"))
    size = jnp.sqrt(raw_total / (FF_WIN * D))
    update = raw / jnp.maximum(1.0, size)
    fresh = (master_weight - learn_rate * update).astype(jnp.bfloat16)
    new_weight = lax.all_gather(fresh, "seq", axis=0, tiled=True)
    return (new_weight, update, new_rows, new_cols)


def solution(mesh):
    return jax.shard_map(
        per_device,
        mesh=mesh,
        in_specs=(
            P(("dp", "seq"), None),
            P(("dp", "seq"), "tensor"),
            P(("dp", "seq"), "tensor"),
            P(("dp", "seq")),
            P("tensor"),
        ),
        out_specs=(P("dp", "tensor"), P(("dp", "seq"), "tensor"), P(("dp", "seq")), P("tensor")),
        check_vma=False,
    )
```

profile of v0, /device:TPU:0, one launch (start us, length us, event | category | flops | bytes accessed | tf_op | source)
XLA Modules:
  0.0 378.6 jit_solution(17348877985578557813)
XLA Ops:
  7.2 0.0 copy-start
  7.2 0.0 reduce-scatter.2.cloned.1.call-start
  7.2 1.2 copy-done
  8.4 16.7 %fusion.4 = f32[7168,1024]{1,0:T(8,128)} fusion(bf16[512,7168]{1,0:T(8,128)(2,1)} %param.5, bf16[512,1024]{1,0:T(8,128)(2,1)S(1)} %copy-done), kind=kOutput, calls=%fused_computation.9 | convolution fusion | flops 7516192768 | bytes 37748736 | tf_op jit(solution)/shard_map/dot_general | solution.py:17
  25.1 0.0 reduce-scatter.2.cloned.1.call-update
  25.1 0.0 copy-start.3
  25.1 0.0 copy-start.4
  25.1 0.0 all-gather.2.cloned.1.call-start
  25.2 181.5 %reduce-scatter.2.cloned.1.call-done = f32[896,1024]{1,0:T(8,128)} async-done(((f32[7168,1024]{1,0:T(8,128)}), f32[896,1024]{1,0:T(8,128)}) %reduce-scatter.2.cloned.1.call-update) | async-done | bytes 3670032 | tf_op jit(solution)/shard_map/reduce_scatter | solution.py:16
  206.7 2.6 fusion.1
  209.4 11.7 %psum.21 = f32[896]{0:T(1024)S(1)} all-reduce(f32[896]{0:T(1024)S(1)} %get-tuple-element.4), channel_id=1, replica_groups=mesh['dp'=2,'seq'=4,'tensor'=4] {'tensor'}, use_global_device_ids=true, to_apply=%region_2.0 | all-reduce | flops 896 | bytes 7168 | tf_op jit(solution)/shard_map/psum | solution.py:26
  221.1 14.1 %psum.22 = f32[1024]{0:T(1024)S(1)} all-reduce(f32[1024]{0:T(1024)S(1)} %get-tuple-element.5), channel_id=1, replica_groups=mesh['dp'=2,'seq'=4,'tensor'=4] {'dp','seq'}, use_global_device_ids=true, to_apply=%region_4.0 | all-reduce | flops 1024 | bytes 8192 | tf_op jit(solution)/shard_map/psum | solution.py:25
  235.1 0.0 copy-done.3
  235.1 0.0 copy-done.4
  235.2 0.0 copy-start.1
  235.2 0.0 copy-start.2
  235.2 3.9 %multiply_reduce_fusion = f32[]{:T(128)} fusion(f32[896,1024]{1,0:T(8,128)} %reduce-scatter.2.cloned.1.call-done, f32[1024]{0:T(1024)S(1)} %multiply_add_fusion.1, f32[896]{0:T(1024)S(1)} %multiply_add_fusion.2), kind=kLoop, calls=%fused_computation.1 | loop fusion | flops 3670015 | bytes 3677700 | tf_op jit(solution)/shard_map/reduce_sum | solution.py:31
  239.1 37.9 %psum.23 = f32[]{:T(128)} all-reduce(f32[]{:T(128)} %multiply_reduce_fusion), channel_id=1, replica_groups=mesh['dp'=2,'seq'=4,'tensor'=4] {'dp','seq','tensor'}, use_global_device_ids=true, to_apply=%region_6.0 | all-reduce | flops 1 | bytes 8 | tf_op jit(solution)/shard_map/psum | solution.py:31
  277.7 6.5 %subtract_convert_fusion = (bf16[896,1024]{1,0:T(8,128)(2,1)}, f32[896,1024]{1,0:T(8,128)}) fusion(f32[896,1024]{1,0:T(8,128)} %param.7, f32[]{:T(128)S(6)} %max_shard_map.3, f32[896,1024]{1,0:T(8,128)} %reduce-scatter.2.cloned.1.call-done, f32[1024]{0:T(1024)S(1)} %multiply_add_fusion.1, f32[896]{0:T(1024)S(1)} %multiply_add_fusion.2), kind=kLoop, calls=%fused_computation | loop fusion | flops 5505024 | bytes 12852740 | tf_op jit(solution)/shard_map/convert_element_type | solution.py:34
  284.2 0.0 copy-done.1
  284.2 0.0 copy-done.2
  284.2 0.0 all-gather.2.cloned.1.call-update
  284.2 80.6 %all-gather.2.cloned.1.call-done = bf16[3584,1024]{1,0:T(8,128)(2,1)} async-done(((bf16[896,1024]{1,0:T(8,128)(2,1)}), bf16[3584,1024]{1,0:T(8,128)(2,1)}) %all-gather.2.cloned.1.call-update) | async-done | bytes 7340048 | tf_op jit(solution)/shard_map/all_gather | solution.py:35
  364.8 7.0 %copy.10 = bf16[3584,1024]{1,0:T(8,128)(2,1)} copy(bf16[3584,1024]{1,0:T(8,128)(2,1)} %all-gather.2.cloned.1.call-done) | data formatting | bytes 14680064
  (2 shorter events, 0.0 us)
Async XLA Ops:
  7.2 1.2 copy-start
  7.2 199.5 %reduce-scatter.2.cloned.1.call-start = ((), (), s32[]{:S(2)}) async-start(), calls=%async_computation.1 | async-start | bytes 33030144 | tf_op jit(solution)/shard_map/reduce_scatter | solution.py:16
  25.1 210.0 %copy-start.3 = (f32[896]{0:T(1024)S(1)}, f32[896]{0:T(1024)}, u32[]{:S(2)}) copy-start(f32[896]{0:T(1024)} %param.8) | copy-start | bytes 10756
  25.1 210.0 %copy-start.4 = (f32[1024]{0:T(1024)S(1)}, f32[1024]{0:T(1024)}, u32[]{:S(2)}) copy-start(f32[1024]{0:T(1024)} %param.9) | copy-start | bytes 12292
  25.1 339.7 %all-gather.2.cloned.1.call-start = ((), (), s32[]{:S(2)}) async-start(), calls=%async_computation.2 | async-start | bytes 9175040 | tf_op jit(solution)/shard_map/all_gather | solution.py:35
  235.2 49.0 %copy-start.1 = (f32[896]{0:T(1024)}, f32[896]{0:T(1024)S(1)}, u32[]{:S(2)}) copy-start(f32[896]{0:T(1024)S(1)} %multiply_add_fusion.2) | copy-start | bytes 10756
  235.2 49.0 %copy-start.2 = (f32[1024]{0:T(1024)}, f32[1024]{0:T(1024)S(1)}, u32[]{:S(2)}) copy-start(f32[1024]{0:T(1024)S(1)} %multiply_add_fusion.1) | copy-start | bytes 12292
Sparse Core Ops, SparseCore 0:
  25.2 181.4 reduce-scatter.1
  284.4 80.3 all-gather.1
where the time goes:
time: 379 us
  waiting for transfers between devices  262 us (69%)
  blocking collectives  63.7 us (17%)
  matrix products  16.7 us (4%)
  between operations  14.8 us (4%)
  other arithmetic  13.1 us (3%)
  local copies, waits for them, and re-layouts  8.18 us (2%)
    reduce_scatter x1, waiting for transfers between devices, per_device(): lax.psum_scatter(lax.dot_general(hidden, grad_out, (((0,), (0,)), ((), ()...  182 us
    all_gather x1, waiting for transfers between devices, per_device(): new_weight = lax.all_gather(fresh, 'seq', axis=0, tiled=True)  80.6 us
    psum x1, blocking collectives, per_device(): raw_total = lax.psum(jnp.sum(raw * raw), ('dp', 'seq', 'tensor'))  37.9 us
    dot_general x1, matrix products, per_device(): lax.dot_general(hidden, grad_out, (((0,), (0,)), ((), ())), preferred_ele...  16.7 us
    psum x1, blocking collectives, per_device(): col_total = lax.psum(jnp.sum(squares, axis=0), ('dp', 'seq'))  14.1 us
    psum x1, blocking collectives, per_device(): row_total = lax.psum(jnp.sum(squares, axis=1), 'tensor')  11.7 us
    unnamed x11, local copies, waits for them, and re-layouts  8.18 us
  transfers between devices with their start and end apart: 2, of which 2 were waited for; matrix products, arithmetic and copies ran while one was open for 0% of the time, Pallas kernels for 0%

commit v1 on v0

v1 whole, which is shorter than its diff:
```python
import functools
import math

import jax
import jax.numpy as jnp
import numpy as np
from jax import lax
from jax.experimental import pallas as pl
from jax.experimental.pallas import tpu as pltpu
from jax.sharding import PartitionSpec as P

decay_rate = 0.8
learn_rate = 0.05
small_term = 1e-06

POWER = 11
TOP = 2.0 ** (125.0 / POWER)
TAIL = 16
VMEM_LIMIT = 16 * 2**20


def chunk_of(rows):
    return 128 if rows % 128 == 0 else rows


def encode(x):
    top = jnp.max(jnp.abs(x), axis=0, keepdims=True)
    scale = jnp.maximum(top * 1.004, 1e-30).astype(jnp.bfloat16).astype(jnp.float32)
    u = x * (TOP / scale)
    u2 = u * u
    u4 = u2 * u2
    return (u4 * u4 * u2 * u).astype(jnp.bfloat16), scale


def decode(code, scale):
    code = code.astype(jnp.float32)
    size = jnp.abs(code)
    u = jnp.exp(jnp.log(jnp.maximum(size, 1e-37)) * (1.0 / POWER)) * (scale * (1.0 / TOP))
    return jnp.where(size > 1e-37, jnp.where(code > 0, u, -u), 0.0)


def write_scales(ref, scales):
    rows, cols = ref.shape
    at = lax.broadcasted_iota(jnp.int32, (TAIL, cols), 0)
    tail = jnp.zeros((TAIL, cols), jnp.float32)
    for j, scale in enumerate(scales):
        tail = jnp.where(at == j, scale, tail)
    ref[rows - TAIL :] = tail.astype(jnp.bfloat16)


def read_scales(ref):
    return ref[ref.shape[0] - TAIL :].astype(jnp.float32)


def pieces_of(rows):
    n = rows // 128
    cuts = sorted({0, (n + 2) // 4, (n + 1) // 2, n})
    return [slice(a * 128, b * 128) for a, b in zip(cuts, cuts[1:])]


def product_kernel(layout, entry, coded, *refs):
    copied, n_hs, n_base = layout
    refs = list(refs)
    take = lambda k: [refs.pop(0) for _ in range(k)]
    source, hs = take(2 * copied), take(n_hs)
    gs, bases, outs = take(n_hs + copied), take(n_base), take(2)
    arriving = {}
    if copied:
        (table, hidden), (held, sems) = source, refs
        start = pl.multiple_of(table[entry], 128)
        for k, at in enumerate(pieces_of(held.shape[1])):
            there = pl.ds(pl.multiple_of(start + at.start, 128), at.stop - at.start)
            copy = pltpu.make_async_copy(hidden.at[:, there], held.at[:, at], sems.at[k])
            copy.start()
            arriving[at.start] = copy
        hs = [held] + hs
    rows, cols = hs[0].shape[1], gs[0].shape[1]
    half, chunk = cols // 2, chunk_of(rows)
    scales = [[], []]
    for j in range(rows // chunk):
        at = slice(j * chunk, (j + 1) * chunk)
        if at.start in arriving:
            arriving[at.start].wait()
        total = None
        for h, g in zip(hs, gs):
            term = lax.dot_general(
                h[:, at], g[...], (((0,), (0,)), ((), ())), preferred_element_type=jnp.float32
            )
            total = term if total is None else total + term
        for part in (0, 1):
            x = total[:, part * half : (part + 1) * half]
            if bases:
                x = x + bases[part][at]
            if coded[part]:
                outs[part][at], scale = encode(x)
                scales[part].append(scale)
            else:
                outs[part][at] = x
    for part in (0, 1):
        if coded[part]:
            write_scales(outs[part], scales[part])


def slice_kernel(entries, table, hidden, *refs):
    outs, sems = refs[: len(entries)], refs[len(entries)]
    copies = []
    for k, out in enumerate(outs):
        at = pl.ds(pl.multiple_of(table[entries[k]], 128), out.shape[1])
        copies.append(pltpu.make_async_copy(hidden.at[:, at], out, sems.at[k]))
    for copy in copies:
        copy.start()
    for copy in copies:
        copy.wait()


def relay_kernel(n, base, *refs):
    messages, out = refs[:n], refs[n]
    rows = base.shape[0]
    chunk = chunk_of(rows)
    tails = [read_scales(m) for m in messages]
    scales = []
    for j in range(rows // chunk):
        at = slice(j * chunk, (j + 1) * chunk)
        total = base[at]
        for m, tail in zip(messages, tails):
            total = total + decode(m[at], tail[j : j + 1])
        out[at], scale = encode(total)
        scales.append(scale)
    write_scales(out, scales)


def gather_kernel(n, base, *refs):
    messages, out = refs[:n], refs[n]
    rows = base.shape[0]
    chunk = chunk_of(rows)
    tails = [read_scales(m) for m in messages]
    for j in range(rows // chunk):
        at = slice(j * chunk, (j + 1) * chunk)
        total = base[at]
        for m, tail in zip(messages, tails):
            total = total + decode(m[at], tail[j : j + 1])
        out[at] = total


def final_kernel(counts, *refs):
    bases, refs = refs[:2], refs[2:]
    messages = refs[: counts[0]], refs[counts[0] : sum(counts)]
    out, row_out, col_out = refs[sum(counts) :]
    rows, half = bases[0].shape
    chunk = chunk_of(rows)
    tails = [[read_scales(m) for m in group] for group in messages]
    col_sums = [jnp.zeros((1, half), jnp.float32)] * 2
    for j in range(rows // chunk):
        at = slice(j * chunk, (j + 1) * chunk)
        row_sum = jnp.zeros((chunk, 128), jnp.float32)
        for part in (0, 1):
            total = bases[part][at]
            for m, tail in zip(messages[part], tails[part]):
                total = total + decode(m[at], tail[j : j + 1])
            out[at, part * half : (part + 1) * half] = total
            squares = total * total
            col_sums[part] = col_sums[part] + jnp.sum(squares, axis=0, keepdims=True)
            for k in range(half // 128):
                row_sum = row_sum + squares[:, k * 128 : (k + 1) * 128]
        row_out[j : j + 1] = jnp.sum(row_sum.T, axis=0, keepdims=True)
    for part in (0, 1):
        col_out[:, part * half : (part + 1) * half] = col_sums[part]


def as_column(row):
    return jnp.broadcast_to(row, (128, row.shape[1])).T


def rows_kernel(n, all_cols, grads, row_prev, col_part, *refs):
    parts, (rows_out, by_row_out, both_out) = refs[:n], refs[n:]
    total = sum(p[...] for p in parts[1:]) + parts[0][...] if n > 1 else parts[0][...]
    total = total + small_term * all_cols
    new_rows = decay_rate * row_prev[...] + (1.0 - decay_rate) * total / all_cols
    rows_out[...] = new_rows
    by_row_out[...] = 1.0 / jnp.sqrt(new_rows)
    inverse = 1.0 / new_rows
    n_chunks, chunk = new_rows.shape
    cols = grads.shape[1]
    sums = [jnp.zeros((1, 128), jnp.float32)] * (cols // 128)
    for j in range(n_chunks):
        weight = as_column(inverse[j : j + 1])
        for k in range(cols // 128):
            g = grads[j * chunk : (j + 1) * chunk, k * 128 : (k + 1) * 128]
            sums[k] = sums[k] + jnp.sum(g * g * weight, axis=0, keepdims=True)
    both_out[0:1] = col_part[...]
    for k in range(cols // 128):
        both_out[1:2, k * 128 : (k + 1) * 128] = sums[k]


def cols_kernel(n, all_rows, col_prev, *refs):
    parts, (cols_out, by_col_out, total_out) = refs[:n], refs[n:]
    both = sum(p[...] for p in parts[1:]) + parts[0][...] if n > 1 else parts[0][...]
    total = both[0:1] + small_term * all_rows
    new_cols = decay_rate * col_prev[...] + (1.0 - decay_rate) * total / all_rows
    cols_out[...] = new_cols
    by_col_out[...] = 1.0 / jnp.sqrt(new_cols)
    share = jnp.sum(both[1:2] / new_cols, axis=1, keepdims=True)
    total_out[...] = jnp.broadcast_to(share, total_out.shape)


def factors(elements, parts, by_row, by_col):
    total = parts[0][0:1, 0:1]
    for part in parts[1:]:
        total = total + part[0:1, 0:1]
    clip = jnp.maximum(1.0, jnp.sqrt(total / elements))
    return by_row[...] / clip, by_col[...]


def fresh_kernel(n, elements, grads, weight, row_factor, col_factor, *refs):
    parts, outs = refs[:n], refs[n:]
    by_row, by_col = factors(elements, parts, row_factor, col_factor)
    n_chunks, chunk = by_row.shape
    cols = grads.shape[1]
    for j in range(n_chunks):
        column = as_column(by_row[j : j + 1])
        for k in range(cols // 128):
            at = slice(j * chunk, (j + 1) * chunk), slice(k * 128, (k + 1) * 128)
            update = grads[at] * column * by_col[:, k * 128 : (k + 1) * 128]
            fresh = (weight[at] - learn_rate * update).astype(jnp.bfloat16)
            split = outs[0].shape[0]
            low, high = j * chunk, (j + 1) * chunk
            if low < split:
                outs[0][low : min(high, split), at[1]] = fresh[: min(high, split) - low]
            if high > split:
                first = max(low, split)
                outs[1][first - split : high - split, at[1]] = fresh[first - low :]


def update_kernel(n, elements, grads, row_factor, col_factor, *refs):
    parts, out = refs[:n], refs[n]
    by_row, by_col = factors(elements, parts, row_factor, col_factor)
    n_chunks, chunk = by_row.shape
    for j in range(n_chunks):
        column = as_column(by_row[j : j + 1])
        for k in range(grads.shape[1] // 128):
            at = slice(j * chunk, (j + 1) * chunk), slice(k * 128, (k + 1) * 128)
            out[at] = grads[at] * column * by_col[:, k * 128 : (k + 1) * 128]


def place_kernel(entries, table, *refs):
    pieces, out, sems = refs[: len(entries)], refs[-2], refs[-1]
    copies = []
    for k, piece in enumerate(pieces):
        at = pl.ds(pl.multiple_of(table[entries[k]], 16), piece.shape[0])
        copies.append(pltpu.make_async_copy(piece, out.at[at], sems.at[k]))
    for copy in copies:
        copy.start()
    for copy in copies:
        copy.wait()


SCALARS = pl.BlockSpec(memory_space=pltpu.SMEM)
FAR = pl.BlockSpec(memory_space=pltpu.HBM)
ANYWHERE = pl.BlockSpec(memory_space=pl.ANY)
NEAR = pl.BlockSpec(memory_space=pltpu.VMEM)


def call(kernel, out_shape, *args, flops=0, specs=None, moved=None, **more):
    outs = out_shape if isinstance(out_shape, (tuple, list)) else [out_shape]
    if moved is None:
        moved = sum(x.size * x.dtype.itemsize for x in [*args, *outs])
    return pl.pallas_call(
        kernel,
        out_shape=out_shape,
        in_specs=specs or [NEAR] * len(args),
        compiler_params=pltpu.CompilerParams(vmem_limit_bytes=VMEM_LIMIT),
        cost_estimate=pl.CostEstimate(flops=flops, bytes_accessed=moved, transcendentals=0),
        **more,
    )(*args)


def shape_of(*dims, dtype=jnp.float32):
    return jax.ShapeDtypeStruct(dims, dtype)


def slices(hidden, table, entries, rows):
    n = len(entries)
    if rows % 128:
        return [lax.dynamic_slice_in_dim(hidden, table[e], rows, axis=1) for e in entries]
    shapes = [shape_of(hidden.shape[0], rows, dtype=hidden.dtype)] * n
    return call(
        functools.partial(slice_kernel, entries),
        shapes,
        table,
        hidden,
        specs=[SCALARS, FAR],
        moved=4 * n * hidden.shape[0] * rows,
        scratch_shapes=[pltpu.SemaphoreType.DMA((n,))],
    )


def product(hidden, table, entry, rows, peers, gs, coded, bases=(), light=False):
    half = gs[0].shape[1] // 2
    shapes = [
        shape_of(rows + TAIL, half, dtype=jnp.bfloat16) if c else shape_of(rows, half) for c in coded
    ]
    copied = entry is not None and rows % 128 == 0
    hs, source, scratch = list(peers), [], []
    if copied:
        source = [table, hidden]
        held = pltpu.VMEM((hidden.shape[0], rows), hidden.dtype)
        scratch = [held, pltpu.SemaphoreType.DMA((len(pieces_of(rows)),))]
    elif entry is not None:
        hs = slices(hidden, table, [entry], rows) + hs
    flops = sum(2 * g.size * rows for g in gs)
    rest = [*hs, *gs, *bases]
    moved = sum(x.size * x.dtype.itemsize for x in rest + shapes)
    if light:
        flops, moved = 0, 1
    return call(
        functools.partial(product_kernel, (int(copied), len(hs), len(bases)), entry, coded),
        shapes,
        *source,
        *rest,
        flops=flops,
        specs=[SCALARS, FAR][: len(source)] + [NEAR] * len(rest),
        moved=moved,
        scratch_shapes=scratch,
    )


def relay(base, messages):
    rows, half = base.shape
    shape = shape_of(rows + TAIL, half, dtype=jnp.bfloat16)
    return call(functools.partial(relay_kernel, len(messages)), shape, base, *messages)


def gather(base, messages):
    if not messages:
        return base
    shape = shape_of(*base.shape)
    return call(functools.partial(gather_kernel, len(messages)), shape, base, *messages)


def final(bases, first, second):
    rows, half = bases[0].shape
    chunk = chunk_of(rows)
    shapes = [shape_of(rows, 2 * half), shape_of(rows // chunk, chunk), shape_of(1, 2 * half)]
    kernel = functools.partial(final_kernel, (len(first), len(second)))
    return call(kernel, shapes, *bases, *first, *second)


def place(pieces, table, entries, out):
    n = len(pieces)
    old = [] if isinstance(out, jax.ShapeDtypeStruct) else [out]
    return call(
        functools.partial(place_kernel, entries),
        jax.ShapeDtypeStruct(out.shape, out.dtype),
        table,
        *pieces,
        *old,
        specs=[SCALARS] + [NEAR] * n + [ANYWHERE] * len(old),
        moved=sum(4 * p.size for p in pieces),
        out_specs=ANYWHERE,
        scratch_shapes=[pltpu.SemaphoreType.DMA((n,))],
        input_output_aliases={n + 1: 0} if old else {},
    )


def after(x, *others):
    return lax.optimization_barrier((x, others))[0]


def grid_of(seq):
    hi = int(math.isqrt(seq))
    while seq % hi:
        hi -= 1
    return hi, seq // hi


def solution(mesh):
    n_dp, n_seq, n_tensor = (mesh.shape[name] for name in ("dp", "seq", "tensor"))
    n_hi, n_lo = grid_of(n_seq)
    his, los = range(1, n_hi), range(1, n_lo)

    def shift(x, hi=0, lo=0):
        pairs = [
            (a * n_lo + b, (a + hi) % n_hi * n_lo + (b + lo) % n_lo)
            for a in range(n_hi)
            for b in range(n_lo)
        ]
        return lax.ppermute(x, "seq", pairs)

    def turn(x, axis, n, step):
        return lax.ppermute(x, axis, [(a, (a + step) % n) for a in range(n)])

    def exchange(parts, axis, n, step=None):
        step = step or (lambda x, d: turn(x, axis, n, d))
        if axis is not None and n & (n - 1) == 0:
            d = 1
            while d < n:
                x = sum(parts[1:], parts[0])
                parts = [x, lax.ppermute(x, axis, [(a, a ^ d) for a in range(n)])]
                d *= 2
            return parts
        if n == 1:
            return parts
        x = sum(parts[1:], parts[0])
        return [x] + [step(x, d) for d in range(1, n)]

    def per_device(hidden, grad_out, master_weight, row_prev, col_prev):
        rows, cols = master_weight.shape

        def settle(x):
            return x if rows % 128 else pltpu.with_memory_space_constraint(x, pltpu.HBM)

        given, hidden = hidden, settle(hidden)
        all_rows, all_cols = rows * n_dp * n_seq, cols * n_tensor
        dp, seq = lax.axis_index("dp"), lax.axis_index("seq")
        my_hi, my_lo = seq // n_lo, seq % n_lo

        part_rows = rows // 2
        cells = np.array([(p, hi, lo) for p in range(n_dp) for hi in range(n_hi) for lo in range(n_lo)])
        places = np.array([(hi, lo, k) for hi in range(n_hi) for lo in range(n_lo) for k in (0, 1)])

        def block_of(hi, lo):
            return lax.rem(my_hi + hi, n_hi) * n_lo + lax.rem(my_lo + lo, n_lo)

        p, hi, lo = (jnp.asarray(x, jnp.int32) for x in cells.T)
        columns = (lax.rem(dp + p, n_dp) * n_seq + block_of(hi, lo)) * rows
        hi, lo, k = (jnp.asarray(x, jnp.int32) for x in places.T)
        table = block_of(n_hi - hi, n_lo - lo) * rows + k * part_rows
        table = jnp.concatenate([columns, table])

        def start_of(p, hi, lo):
            return (p * n_hi + hi) * n_lo + lo

        def row_of(part, hi, lo):
            return len(cells) + (hi * n_lo + lo) * 2 + part

        def peers_of(group, source):
            found = {at: [] for at in group}
            for p in range(1, n_dp if group else 1):
                entries = [start_of(p, *at) for at in group]
                for at, block in zip(group, slices(source, table, entries, rows)):
                    found[at].append(turn(block, "dp", n_dp, p))
            return found

        gs = [grad_out] + [turn(grad_out, "dp", n_dp, p) for p in range(1, n_dp)]
        far_group = [(hi, lo) for hi in his for lo in los]
        near_group = [(0, lo) for lo in los] + [(hi, 0) for hi in his] + [(0, 0)]
        blocks = peers_of(far_group, hidden)

        far, sent = [{}, {}], []
        for hi, lo in far_group:
            bases = product(hidden, table, start_of(0, hi, lo), rows, [], gs[:1], (False, False))
            if n_dp > 1:
                coded = product(None, None, None, rows, blocks[hi, lo], gs[1:], (True, True), bases)
            else:
                coded = [relay(x, []) for x in bases]
            sent += coded
            far[0][hi, lo] = shift(coded[0], lo=lo)
            far[1][hi, lo] = shift(coded[1], hi=hi)

        hidden = settle(after(given, *sent))
        blocks = peers_of(near_group, hidden)

        def whole_product(hi, lo, coded):
            entry = start_of(0, hi, lo)
            return product(hidden, table, entry, rows, blocks[hi, lo], gs, coded, light=True)

        near, base = [{}, {}], [{}, {}]
        for lo in los:
            first, base[1][lo] = whole_product(0, lo, (True, False))
            near[0][lo] = shift(first, lo=lo)
        for hi in his:
            base[0][hi], second = whole_product(hi, 0, (False, True))
            near[1][hi] = shift(second, hi=hi)
        own = whole_product(0, 0, (False, False))
        last = [{}, {}]
        for hi in his:
            message = relay(base[0][hi], [far[0][hi, lo] for lo in los])
            last[0][hi] = shift(message, hi=hi)
        for lo in los:
            message = relay(base[1][lo], [far[1][hi, lo] for hi in his])
            last[1][lo] = shift(message, lo=lo)
        own = [gather(own[part], list(near[part].values())) for part in (0, 1)]
        grads, row_part, col_part = final(own, list(last[0].values()), list(last[1].values()))

        chunks = row_part.shape
        parts = exchange([row_part], "tensor", n_tensor)
        new_rows, by_row, both = call(
            functools.partial(rows_kernel, len(parts), all_cols),
            [shape_of(*chunks), shape_of(*chunks), shape_of(2, cols)],
            grads,
            row_prev.reshape(chunks),
            col_part,
            *parts,
        )
        parts = exchange([both], "dp", n_dp)
        parts = exchange(parts, None, n_lo, lambda x, d: shift(x, lo=d))
        parts = exchange(parts, None, n_hi, lambda x, d: shift(x, hi=d))
        new_cols, by_col, share = call(
            functools.partial(cols_kernel, len(parts), all_rows),
            [shape_of(1, cols), shape_of(1, cols), shape_of(1, 128)],
            col_prev.reshape(1, cols),
            *parts,
        )
        parts = exchange([share], "tensor", n_tensor)
        elements = all_rows * all_cols

        pair = call(
            functools.partial(fresh_kernel, len(parts), elements),
            [shape_of(part_rows, cols, dtype=jnp.bfloat16)] * 2,
            grads,
            master_weight,
            by_row,
            by_col,
            *parts,
        )
        along_lo, along_hi = {}, {}
        for lo in los:
            along_lo[0, lo] = shift(pair[0], lo=lo)
        for hi in his:
            along_hi[1, hi] = shift(pair[1], hi=hi)
        for lo in los:
            along_lo[1, lo] = shift(pair[1], lo=lo)
        for hi in his:
            along_hi[0, hi] = shift(pair[0], hi=hi)

        onward = []
        for hi in his:
            for lo in los:
                onward.append((shift(along_lo[0, lo], hi=hi), row_of(0, hi, lo)))
                onward.append((shift(along_hi[1, hi], lo=lo), row_of(1, hi, lo)))
        update = call(
            functools.partial(update_kernel, len(parts), elements),
            shape_of(rows, cols),
            after(grads, *along_lo.values()),
            by_row,
            by_col,
            *parts,
        )

        whole = jax.ShapeDtypeStruct((rows * n_seq, cols), jnp.bfloat16)
        new_weight = place(pair, table, [row_of(part, 0, 0) for part in (0, 1)], whole)
        pieces = [(x, row_of(part, 0, lo)) for (part, lo), x in along_lo.items()]
        pieces += [(x, row_of(part, hi, 0)) for (part, hi), x in along_hi.items()]
        for group in (pieces, onward):
            if group:
                new_weight = place([x for x, _ in group], table, [e for _, e in group], new_weight)
        return (new_weight, update, new_rows.reshape(rows), new_cols.reshape(cols))

    return jax.shard_map(
        per_device,
        mesh=mesh,
        in_specs=(
            P(("dp", "seq"), None),
            P(("dp", "seq"), "tensor"),
            P(("dp", "seq"), "tensor"),
            P(("dp", "seq")),
            P("tensor"),
        ),
        out_specs=(P("dp", "tensor"), P(("dp", "seq"), "tensor"), P(("dp", "seq")), P("tensor")),
        check_vma=False,
    )
```

time: 379 us -> 164 us (0.43)
  waiting for transfers between devices: 262 us -> 94.9 us
  blocking collectives: 63.7 us -> 0 us
  Pallas kernels: 0 us -> 40 us
  starting transfers between devices: 0.08 us -> 26.6 us
  matrix products: 16.7 us -> 0 us
  between operations: 14.8 us -> 0.97 us
  other arithmetic: 13.1 us -> 0.84 us
  local copies, waits for them, and re-layouts: 8.18 us -> 0.02 us
    reduce_scatter x1 -> x0, waiting for transfers between devices: 182 us -> none  [per_device(): lax.psum_scatter(lax.dot_general(hidden, grad_out, (((0,), (0,)), ((), ()...]
    ppermute x0 -> x24, waiting for transfers between devices: none -> 94.9 us  [the longest x14 81.5 us: shift(): return lax.ppermute(x, 'seq', pairs)]
    all_gather x1 -> x0, waiting for transfers between devices: 80.6 us -> none  [per_device(): new_weight = lax.all_gather(fresh, 'seq', axis=0, tiled=True)]
    psum x3 -> x0, blocking collectives: 63.7 us -> none  [the longest x1 37.9 us: per_device(): raw_total = lax.psum(jnp.sum(raw * raw), ('dp', 'seq', 'tensor'))]
    pallas_call x0 -> x19, Pallas kernels: none -> 40 us  [call(): pl.pallas_call(kernel, out_shape=out_shape, in_specs=specs or [NEAR] * le...]
    ppermute x0 -> x24, starting transfers between devices: none -> 26.6 us  [the longest x14 17 us: shift(): return lax.ppermute(x, 'seq', pairs)]
    dot_general x1 -> x0, matrix products: 16.7 us -> none  [per_device(): lax.dot_general(hidden, grad_out, (((0,), (0,)), ((), ())), preferred_ele...]
    unnamed x11 -> x8, local copies, waits for them, and re-layouts: 8.18 us -> 0.02 us
  transfers between devices with their start and end apart: 2 -> 24, of which waited for: 2 -> 15; matrix products, arithmetic and copies ran while one was open for 0% -> 1% of each run, Pallas kernels for 0% -> 19%
where the time goes in v1:
time: 164 us; the launch traced here: 163 us
  waiting for transfers between devices  94.9 us (58%)
  Pallas kernels  40 us (24%)
  starting transfers between devices  26.6 us (16%)
    ppermute x14, waiting for transfers between devices, shift(): return lax.ppermute(x, 'seq', pairs)  81.5 us
    pallas_call x19, Pallas kernels, call(): pl.pallas_call(kernel, out_shape=out_shape, in_specs=specs or [NEAR] * le...  40 us
    ppermute x14, starting transfers between devices, shift(): return lax.ppermute(x, 'seq', pairs)  17 us
    ppermute x5, waiting for transfers between devices, exchange(): parts = [x, lax.ppermute(x, axis, [(a, a ^ d) for a in range(n)])]  8.96 us
    ppermute x5, starting transfers between devices, exchange(): parts = [x, lax.ppermute(x, axis, [(a, a ^ d) for a in range(n)])]  8.37 us
    ppermute x5, waiting for transfers between devices, turn(): return lax.ppermute(x, axis, [(a, (a + step) % n) for a in range(n)])  4.44 us
  transfers between devices with their start and end apart: 24, of which 15 were waited for; matrix products, arithmetic and copies ran while one was open for 1% of the time, Pallas kernels for 19%

profile of v1, /device:TPU:0, one launch (start us, length us, event | category | flops | bytes accessed | tf_op | source)
XLA Modules:
  0.0 163.2 jit_solution(4968035858099636206)
XLA Ops:
  3.8 3.1 %shard_map.139 = (f32[896,512]{1,0:T(8,128)S(1)}, f32[896,512]{1,0:T(8,128)S(1)}) custom-call(s32[16]{0:T(128)S(1)} %pad_add_fusion.table.refs_0_, bf16[512,7168]{1,0:T(8,128)(2,1)} %refs_1_.4, bf16[512,1024]{1,0:T(8,128)(2,1)S(1)} %copy-done), custom_call_target="tpu_custom_call" | custom-call | flops 939524096 | bytes 4718592 | tf_op jit(solution)/shard_map/pallas_call | solution.py:267
  6.9 2.3 %shard_map.140 = (bf16[912,512]{1,0:T(8,128)(2,1)S(1)}, bf16[912,512]{1,0:T(8,128)(2,1)S(1)}) custom-call(bf16[512,896]{1,0:T(8,128)(2,1)S(1)} %collective-permute-done.refs_0_, bf16[512,1024]{1,0:T(8,128)(2,1)S(1)} %collective-permute-done.1.refs_1_.refs_4_, f32[896,512]{1,0:T(8,128)S(1)} %get-tuple-element.30.refs_2_, f32[896,512]{1,0:T(8,128)S(1)} %get-tuple-element.31.refs_3_), custom_call_target="tpu_custom_call" | custom-call | flops 939524096 | bytes 7503872 | tf_op jit(solution)/shard_map/pallas_call | solution.py:267
  9.3 3.0 %collective-permute-start.7 = (bf16[912,512]{1,0:T(8,128)(2,1)S(1)}, bf16[912,512]{1,0:T(8,128)(2,1)S(1)}, u32[]{:S(2)}, u32[]{:S(2)}) collective-permute-start(bf16[912,512]{1,0:T(8,128)(2,1)S(1)} %get-tuple-element.32), channel_id=1, source_target_pairs={{0,4},{4,0},{8,12},{12,8},{1,5},{5,1},{9,13},{13,9},{2,6},{6,2},{1... | collective-permute-start | bytes 2801672 | tf_op jit(solution)/shard_map/ppermute | solution.py:387
  13.8 2.3 %shard_map.141 = (bf16[512,896]{1,0:T(8,128)(2,1)S(1)}, bf16[512,896]{1,0:T(8,128)(2,1)S(1)}, bf16[512,896]{1,0:T(8,128)(2,1)S(1)}) custom-call(s32[16]{0:T(128)S(1)} %pad_add_fusion.table.refs_0_, bf16[512,7168]{1,0:T(8,128)(2,1)} %refs_1_.4), custom_call_target="tpu_custom_call" | custom-call | bytes 5505024 | tf_op jit(solution)/shard_map/pallas_call | solution.py:267
  18.7 4.5 %shard_map.145 = (f32[896,512]{1,0:T(8,128)S(1)}, bf16[912,512]{1,0:T(8,128)(2,1)S(1)}) custom-call(s32[16]{0:T(128)S(1)} %pad_add_fusion.table.refs_0_, bf16[512,7168]{1,0:T(8,128)(2,1)} %refs_1_.4, bf16[512,896]{1,0:T(8,128)(2,1)S(1)} %collective-permute-done.5.refs_2_, bf16[512,1024]{1,0:T(8,128)(2,1)S(1)} %copy-done, ...), custom_call_target="tpu_custom_call" | custom-call | bytes 1 | tf_op jit(solution)/shard_map/pallas_call | solution.py:267
  23.8 4.3 %shard_map.143 = (bf16[912,512]{1,0:T(8,128)(2,1)S(1)}, f32[896,512]{1,0:T(8,128)S(1)}) custom-call(s32[16]{0:T(128)S(1)} %pad_add_fusion.table.refs_0_, bf16[512,7168]{1,0:T(8,128)(2,1)} %refs_1_.4, bf16[512,896]{1,0:T(8,128)(2,1)S(1)} %collective-permute-done.3.refs_2_, bf16[512,1024]{1,0:T(8,128)(2,1)S(1)} %copy-done, ...), custom_call_target="tpu_custom_call" | custom-call | bytes 1 | tf_op jit(solution)/shard_map/pallas_call | solution.py:267
  28.2 5.6 %collective-permute-done.7.refs_0_ = bf16[912,512]{1,0:T(8,128)(2,1)S(1)} collective-permute-done((bf16[912,512]{1,0:T(8,128)(2,1)S(1)}, bf16[912,512]{1,0:T(8,128)(2,1)S(1)}, u32[]{:S(2)}, u32[]{:S(2)}) %collective-permute-start.7) | collective-permute-done | bytes 933920 | tf_op jit(solution)/shard_map/ppermute | solution.py:387
  35.2 2.2 %collective-permute-start.8 = (bf16[912,512]{1,0:T(8,128)(2,1)S(1)}, bf16[912,512]{1,0:T(8,128)(2,1)S(1)}, u32[]{:S(2)}, u32[]{:S(2)}) collective-permute-start(bf16[912,512]{1,0:T(8,128)(2,1)S(1)} %shard_map.147), channel_id=1, source_target_pairs={{0,8},{4,12},{8,0},{12,4},{1,9},{5,13},{9,1},{13,5},{2,10},{6,14},... | collective-permute-start | bytes 2801672 | tf_op jit(solution)/shard_map/ppermute | solution.py:387
  40.6 2.5 %collective-permute-done.2.refs_2_ = bf16[512,896]{1,0:T(8,128)(2,1)S(1)} collective-permute-done((bf16[512,896]{1,0:T(8,128)(2,1)S(1)}, bf16[512,896]{1,0:T(8,128)(2,1)S(1)}, u32[]{:S(2)}, u32[]{:S(2)}) %collective-permute-start.2) | collective-permute-done | bytes 917536 | tf_op jit(solution)/shard_map/ppermute | solution.py:390
  43.1 4.0 %shard_map.142 = (f32[896,512]{1,0:T(8,128)S(1)}, f32[896,512]{1,0:T(8,128)S(1)}) custom-call(s32[16]{0:T(128)S(1)} %pad_add_fusion.table.refs_0_, bf16[512,7168]{1,0:T(8,128)(2,1)} %refs_1_.4, bf16[512,896]{1,0:T(8,128)(2,1)S(1)} %collective-permute-done.2.refs_2_, bf16[512,1024]{1,0:T(8,128)(2,1)S(1)} %copy-done, ...), custom_call_target="tpu_custom_call" | custom-call | bytes 1 | tf_op jit(solution)/shard_map/pallas_call | solution.py:267
  47.1 8.8 %collective-permute-done.6.refs_0_ = bf16[912,512]{1,0:T(8,128)(2,1)S(1)} collective-permute-done((bf16[912,512]{1,0:T(8,128)(2,1)S(1)}, bf16[912,512]{1,0:T(8,128)(2,1)S(1)}, u32[]{:S(2)}, u32[]{:S(2)}) %collective-permute-start.6) | collective-permute-done | bytes 933920 | tf_op jit(solution)/shard_map/ppermute | solution.py:387
  57.7 16.9 %collective-permute-done.8.refs_2_ = bf16[912,512]{1,0:T(8,128)(2,1)S(1)} collective-permute-done((bf16[912,512]{1,0:T(8,128)(2,1)S(1)}, bf16[912,512]{1,0:T(8,128)(2,1)S(1)}, u32[]{:S(2)}, u32[]{:S(2)}) %collective-permute-start.8) | collective-permute-done | bytes 933920 | tf_op jit(solution)/shard_map/ppermute | solution.py:387
  74.7 2.6 %shard_map.149 = (f32[896,1024]{1,0:T(8,128)S(1)}, f32[7,128]{1,0:T(8,128)S(1)}, f32[1,1024]{1,0:T(1,128)S(1)}) custom-call(f32[896,512]{1,0:T(8,128)S(1)} %shard_map.144.refs_0_, f32[896,512]{1,0:T(8,128)S(1)} %shard_map.146.refs_1_, bf16[912,512]{1,0:T(8,128)(2,1)S(1)} %collective-permute-done.8.refs_2_, bf16[912,512]{1,0:T(8,128)(2,1)S(1)} %collective-permute-done.10.refs_3_), custom_call_target="tpu_custom_call" | custom-call | bytes 9215488 | tf_op jit(solution)/shard_map/pallas_call | solution.py:267
  78.9 2.0 %collective-permute-done.11 = f32[7,128]{1,0:T(8,128)S(1)} collective-permute-done((f32[7,128]{1,0:T(8,128)S(1)}, f32[7,128]{1,0:T(8,128)S(1)}, u32[]{:S(2)}, u32[]{:S(2)}) %collective-permute-start.11) | collective-permute-done | bytes 3616 | tf_op jit(solution)/shard_map/ppermute | solution.py:398
  80.9 2.6 %collective-permute-start.12 = (f32[7,128]{1,0:T(8,128)S(1)}, f32[7,128]{1,0:T(8,128)S(1)}, u32[]{:S(2)}, u32[]{:S(2)}) collective-permute-start(f32[7,128]{1,0:T(8,128)S(1)} %add.68.refs_0_), channel_id=1, source_target_pairs={{0,2},{1,3},{2,0},{3,1},{4,6},{5,7},{6,4},{7,5},{8,10},{9,11},{10,... | collective-permute-start | bytes 10760 | tf_op jit(solution)/shard_map/ppermute | solution.py:398
  87.6 3.3 %collective-permute-done.14 = f32[2,1024]{1,0:T(2,128)S(1)} collective-permute-done((f32[2,1024]{1,0:T(2,128)S(1)}, f32[2,1024]{1,0:T(2,128)S(1)}, u32[]{:S(2)}, u32[]{:S(2)}) %collective-permute-start.14) | collective-permute-done | bytes 8224 | tf_op jit(solution)/shard_map/ppermute | solution.py:387
  92.4 2.1 %collective-permute-done.15.refs_1_ = f32[2,1024]{1,0:T(2,128)S(1)} collective-permute-done((f32[2,1024]{1,0:T(2,128)S(1)}, f32[2,1024]{1,0:T(2,128)S(1)}, u32[]{:S(2)}, u32[]{:S(2)}) %collective-permute-start.15) | collective-permute-done | bytes 8224 | tf_op jit(solution)/shard_map/ppermute | solution.py:387
  96.7 2.0 %collective-permute-done.16 = f32[1,128]{1,0:T(1,128)S(1)} collective-permute-done((f32[1,128]{1,0:T(1,128)S(1)}, f32[1,128]{1,0:T(1,128)S(1)}, u32[]{:S(2)}, u32[]{:S(2)}) %collective-permute-start.16) | collective-permute-done | bytes 544 | tf_op jit(solution)/shard_map/ppermute | solution.py:398
  98.7 2.6 %collective-permute-start.17 = (f32[1,128]{1,0:T(1,128)S(1)}, f32[1,128]{1,0:T(1,128)S(1)}, u32[]{:S(2)}, u32[]{:S(2)}) collective-permute-start(f32[1,128]{1,0:T(1,128)S(1)} %add.71.refs_0_), channel_id=1, source_target_pairs={{0,2},{1,3},{2,0},{3,1},{4,6},{5,7},{6,4},{7,5},{8,10},{9,11},{10,... | collective-permute-start | bytes 1544 | tf_op jit(solution)/shard_map/ppermute | solution.py:398
  108.0 19.2 %collective-permute-done.18.refs_0_ = bf16[448,1024]{1,0:T(8,128)(2,1)S(1)} collective-permute-done((bf16[448,1024]{1,0:T(8,128)(2,1)S(1)}, bf16[448,1024]{1,0:T(8,128)(2,1)S(1)}, u32[]{:S(2)}, u32[]{:S(2)}) %collective-permute-start.18) | collective-permute-done | bytes 917536 | tf_op jit(solution)/shard_map/ppermute | solution.py:387
  131.1 15.8 %collective-permute-done.22.refs_1_ = bf16[448,1024]{1,0:T(8,128)(2,1)S(1)} collective-permute-done((bf16[448,1024]{1,0:T(8,128)(2,1)S(1)}, bf16[448,1024]{1,0:T(8,128)(2,1)S(1)}, u32[]{:S(2)}, u32[]{:S(2)}) %collective-permute-start.22) | collective-permute-done | bytes 917536 | tf_op jit(solution)/shard_map/ppermute | solution.py:387
  146.9 2.3 %shard_map.156 = f32[896,1024]{1,0:T(8,128)} custom-call(f32[896,1024]{1,0:T(8,128)S(1)} %get-tuple-element.53.grads, f32[7,128]{1,0:T(8,128)S(1)} %get-tuple-element.47.row_factor, f32[1,1024]{1,0:T(1,128)S(1)} %get-tuple-element.49.col_factor, f32[1,128]{1,0:T(1,128)S(1)} %add.71.refs_0_, f32[1,128]{1,0:T(1,128)S(1)} %collective-permute-done.17.refs_1_), custom_call_target="tpu_custom_call" | custom-call | bytes 7348736 | tf_op jit(solution)/shard_map/pallas_call | solution.py:267
  149.2 2.4 %shard_map.154.refs_2_ = bf16[3584,1024]{1,0:T(8,128)(2,1)} custom-call(s32[16]{0:T(128)S(1)} %pad_add_fusion.table.refs_0_, bf16[448,1024]{1,0:T(8,128)(2,1)S(1)} %collective-permute-done.18.refs_0_, bf16[448,1024]{1,0:T(8,128)(2,1)S(1)} %collective-permute-done.22.refs_1_, ...), custom_call_target="tpu_custom_call", output_to_operand_aliasing={{}: (5, {})} | custom-call | bytes 7340032 | tf_op jit(solution)/shard_map/pallas_call | solution.py:267
  151.6 9.7 %collective-permute-done.19.refs_0_ = bf16[448,1024]{1,0:T(8,128)(2,1)S(1)} collective-permute-done((bf16[448,1024]{1,0:T(8,128)(2,1)S(1)}, bf16[448,1024]{1,0:T(8,128)(2,1)S(1)}, u32[]{:S(2)}, u32[]{:S(2)}) %collective-permute-start.19) | collective-permute-done | bytes 917536 | tf_op jit(solution)/shard_map/ppermute | solution.py:387
  (57 shorter events, 36.2 us)
Async XLA Ops:
  0.6 6.3 %collective-permute-start.1 = (bf16[512,1024]{1,0:T(8,128)(2,1)}, bf16[512,1024]{1,0:T(8,128)(2,1)S(1)}, u32[]{:S(2)}, u32[]{:S(2)}) collective-permute-start(bf16[512,1024]{1,0:T(8,128)(2,1)} %refs_3_.5), channel_id=1, source_target_pairs={{0,16},{16,0},{1,17},{17,1},{2,18},{18,2},{3,19},{19,3},{4,20},{20... | collective-permute-start | bytes 3145736 | tf_op jit(solution)/shard_map/ppermute | solution.py:390
  3.7 3.2 %collective-permute-start = (bf16[512,896]{1,0:T(8,128)(2,1)S(1)}, bf16[512,896]{1,0:T(8,128)(2,1)S(1)}, u32[]{:S(2)}, u32[]{:S(2)}) collective-permute-start(bf16[512,896]{1,0:T(8,128)(2,1)S(1)} %shard_map.138), channel_id=1, source_target_pairs={{0,16},{16,0},{1,17},{17,1},{2,18},{18,2},{3,19},{19,3},{4,20},{20... | collective-permute-start | bytes 2752520 | tf_op jit(solution)/shard_map/ppermute | solution.py:390
  9.3 24.5 %collective-permute-start.7 = (bf16[912,512]{1,0:T(8,128)(2,1)S(1)}, bf16[912,512]{1,0:T(8,128)(2,1)S(1)}, u32[]{:S(2)}, u32[]{:S(2)}) collective-permute-start(bf16[912,512]{1,0:T(8,128)(2,1)S(1)} %get-tuple-element.32), channel_id=1, source_target_pairs={{0,4},{4,0},{8,12},{12,8},{1,5},{5,1},{9,13},{13,9},{2,6},{6,2},{1... | collective-permute-start | bytes 2801672 | tf_op jit(solution)/shard_map/ppermute | solution.py:387
  12.3 25.1 %collective-permute-start.9 = (bf16[912,512]{1,0:T(8,128)(2,1)S(1)}, bf16[912,512]{1,0:T(8,128)(2,1)S(1)}, u32[]{:S(2)}, u32[]{:S(2)}) collective-permute-start(bf16[912,512]{1,0:T(8,128)(2,1)S(1)} %get-tuple-element.33), channel_id=1, source_target_pairs={{0,8},{4,12},{8,0},{12,4},{1,9},{5,13},{9,1},{13,5},{2,10},{6,14},... | collective-permute-start | bytes 2801672 | tf_op jit(solution)/shard_map/ppermute | solution.py:387
  16.1 2.5 %collective-permute-start.5 = (bf16[512,896]{1,0:T(8,128)(2,1)S(1)}, bf16[512,896]{1,0:T(8,128)(2,1)S(1)}, u32[]{:S(2)}, u32[]{:S(2)}) collective-permute-start(bf16[512,896]{1,0:T(8,128)(2,1)S(1)} %get-tuple-element.40), channel_id=1, source_target_pairs={{0,16},{16,0},{1,17},{17,1},{2,18},{18,2},{3,19},{19,3},{4,20},{20... | collective-permute-start | bytes 2752520 | tf_op jit(solution)/shard_map/ppermute | solution.py:390
  16.2 7.6 %collective-permute-start.3 = (bf16[512,896]{1,0:T(8,128)(2,1)S(1)}, bf16[512,896]{1,0:T(8,128)(2,1)S(1)}, u32[]{:S(2)}, u32[]{:S(2)}) collective-permute-start(bf16[512,896]{1,0:T(8,128)(2,1)S(1)} %get-tuple-element.37), channel_id=1, source_target_pairs={{0,16},{16,0},{1,17},{17,1},{2,18},{18,2},{3,19},{19,3},{4,20},{20... | collective-permute-start | bytes 2752520 | tf_op jit(solution)/shard_map/ppermute | solution.py:390
  23.2 32.7 %collective-permute-start.6 = (bf16[912,512]{1,0:T(8,128)(2,1)S(1)}, bf16[912,512]{1,0:T(8,128)(2,1)S(1)}, u32[]{:S(2)}, u32[]{:S(2)}) collective-permute-start(bf16[912,512]{1,0:T(8,128)(2,1)S(1)} %get-tuple-element.41), channel_id=1, source_target_pairs={{0,8},{4,12},{8,0},{12,4},{1,9},{5,13},{9,1},{13,5},{2,10},{6,14},... | collective-permute-start | bytes 2801672 | tf_op jit(solution)/shard_map/ppermute | solution.py:387
  28.1 28.7 %collective-permute-start.4 = (bf16[912,512]{1,0:T(8,128)(2,1)S(1)}, bf16[912,512]{1,0:T(8,128)(2,1)S(1)}, u32[]{:S(2)}, u32[]{:S(2)}) collective-permute-start(bf16[912,512]{1,0:T(8,128)(2,1)S(1)} %get-tuple-element.38), channel_id=1, source_target_pairs={{0,4},{4,0},{8,12},{12,8},{1,5},{5,1},{9,13},{13,9},{2,6},{6,2},{1... | collective-permute-start | bytes 2801672 | tf_op jit(solution)/shard_map/ppermute | solution.py:387
  35.2 39.4 %collective-permute-start.8 = (bf16[912,512]{1,0:T(8,128)(2,1)S(1)}, bf16[912,512]{1,0:T(8,128)(2,1)S(1)}, u32[]{:S(2)}, u32[]{:S(2)}) collective-permute-start(bf16[912,512]{1,0:T(8,128)(2,1)S(1)} %shard_map.147), channel_id=1, source_target_pairs={{0,8},{4,12},{8,0},{12,4},{1,9},{5,13},{9,1},{13,5},{2,10},{6,14},... | collective-permute-start | bytes 2801672 | tf_op jit(solution)/shard_map/ppermute | solution.py:387
  39.1 35.6 %collective-permute-start.10 = (bf16[912,512]{1,0:T(8,128)(2,1)S(1)}, bf16[912,512]{1,0:T(8,128)(2,1)S(1)}, u32[]{:S(2)}, u32[]{:S(2)}) collective-permute-start(bf16[912,512]{1,0:T(8,128)(2,1)S(1)} %shard_map.148), channel_id=1, source_target_pairs={{0,4},{4,0},{8,12},{12,8},{1,5},{5,1},{9,13},{13,9},{2,6},{6,2},{1... | collective-permute-start | bytes 2801672 | tf_op jit(solution)/shard_map/ppermute | solution.py:387
  40.6 2.5 %collective-permute-start.2 = (bf16[512,896]{1,0:T(8,128)(2,1)S(1)}, bf16[512,896]{1,0:T(8,128)(2,1)S(1)}, u32[]{:S(2)}, u32[]{:S(2)}) collective-permute-start(bf16[512,896]{1,0:T(8,128)(2,1)S(1)} %get-tuple-element.35), channel_id=1, source_target_pairs={{0,16},{16,0},{1,17},{17,1},{2,18},{18,2},{3,19},{19,3},{4,20},{20... | collective-permute-start | bytes 2752520 | tf_op jit(solution)/shard_map/ppermute | solution.py:390
  77.2 3.7 %collective-permute-start.11 = (f32[7,128]{1,0:T(8,128)S(1)}, f32[7,128]{1,0:T(8,128)S(1)}, u32[]{:S(2)}, u32[]{:S(2)}) collective-permute-start(f32[7,128]{1,0:T(8,128)S(1)} %get-tuple-element.46), channel_id=1, source_target_pairs={{0,1},{1,0},{2,3},{3,2},{4,5},{5,4},{6,7},{7,6},{8,9},{9,8},{10,11... | collective-permute-start | bytes 10760 | tf_op jit(solution)/shard_map/ppermute | solution.py:398
  80.9 4.5 %collective-permute-start.12 = (f32[7,128]{1,0:T(8,128)S(1)}, f32[7,128]{1,0:T(8,128)S(1)}, u32[]{:S(2)}, u32[]{:S(2)}) collective-permute-start(f32[7,128]{1,0:T(8,128)S(1)} %add.68.refs_0_), channel_id=1, source_target_pairs={{0,2},{1,3},{2,0},{3,1},{4,6},{5,7},{6,4},{7,5},{8,10},{9,11},{10,... | collective-permute-start | bytes 10760 | tf_op jit(solution)/shard_map/ppermute | solution.py:398
  86.0 1.2 collective-permute-start.13
  87.2 3.7 %collective-permute-start.14 = (f32[2,1024]{1,0:T(2,128)S(1)}, f32[2,1024]{1,0:T(2,128)S(1)}, u32[]{:S(2)}, u32[]{:S(2)}) collective-permute-start(f32[2,1024]{1,0:T(2,128)S(1)} %add.69), channel_id=1, source_target_pairs={{0,4},{4,0},{8,12},{12,8},{1,5},{5,1},{9,13},{13,9},{2,6},{6,2},{1... | collective-permute-start | bytes 24584 | tf_op jit(solution)/shard_map/ppermute | solution.py:387
  90.9 3.7 %collective-permute-start.15 = (f32[2,1024]{1,0:T(2,128)S(1)}, f32[2,1024]{1,0:T(2,128)S(1)}, u32[]{:S(2)}, u32[]{:S(2)}) collective-permute-start(f32[2,1024]{1,0:T(2,128)S(1)} %add.70.refs_0_), channel_id=1, source_target_pairs={{0,8},{4,12},{8,0},{12,4},{1,9},{5,13},{9,1},{13,5},{2,10},{6,14},... | collective-permute-start | bytes 24584 | tf_op jit(solution)/shard_map/ppermute | solution.py:387
  95.1 3.5 %collective-permute-start.16 = (f32[1,128]{1,0:T(1,128)S(1)}, f32[1,128]{1,0:T(1,128)S(1)}, u32[]{:S(2)}, u32[]{:S(2)}) collective-permute-start(f32[1,128]{1,0:T(1,128)S(1)} %get-tuple-element.50), channel_id=1, source_target_pairs={{0,1},{1,0},{2,3},{3,2},{4,5},{5,4},{6,7},{7,6},{8,9},{9,8},{10,11... | collective-permute-start | bytes 1544 | tf_op jit(solution)/shard_map/ppermute | solution.py:398
  98.7 4.4 %collective-permute-start.17 = (f32[1,128]{1,0:T(1,128)S(1)}, f32[1,128]{1,0:T(1,128)S(1)}, u32[]{:S(2)}, u32[]{:S(2)}) collective-permute-start(f32[1,128]{1,0:T(1,128)S(1)} %add.71.refs_0_), channel_id=1, source_target_pairs={{0,2},{1,3},{2,0},{3,1},{4,6},{5,7},{6,4},{7,5},{8,10},{9,11},{10,... | collective-permute-start | bytes 1544 | tf_op jit(solution)/shard_map/ppermute | solution.py:398
  103.9 23.4 %collective-permute-start.18 = (bf16[448,1024]{1,0:T(8,128)(2,1)S(1)}, bf16[448,1024]{1,0:T(8,128)(2,1)S(1)}, u32[]{:S(2)}, u32[]{:S(2)}) collective-permute-start(bf16[448,1024]{1,0:T(8,128)(2,1)S(1)} %get-tuple-element.51.refs_0_), channel_id=1, source_target_pairs={{0,4},{4,0},{8,12},{12,8},{1,5},{5,1},{9,13},{13,9},{2,6},{6,2},{1... | collective-permute-start | bytes 2752520 | tf_op jit(solution)/shard_map/ppermute | solution.py:387
  104.3 24.5 %collective-permute-start.20 = (bf16[448,1024]{1,0:T(8,128)(2,1)S(1)}, bf16[448,1024]{1,0:T(8,128)(2,1)S(1)}, u32[]{:S(2)}, u32[]{:S(2)}) collective-permute-start(bf16[448,1024]{1,0:T(8,128)(2,1)S(1)} %get-tuple-element.52.refs_1_), channel_id=1, source_target_pairs={{0,8},{4,12},{8,0},{12,4},{1,9},{5,13},{9,1},{13,5},{2,10},{6,14},... | collective-permute-start | bytes 2752520 | tf_op jit(solution)/shard_map/ppermute | solution.py:387
  106.0 40.9 %collective-permute-start.22 = (bf16[448,1024]{1,0:T(8,128)(2,1)S(1)}, bf16[448,1024]{1,0:T(8,128)(2,1)S(1)}, u32[]{:S(2)}, u32[]{:S(2)}) collective-permute-start(bf16[448,1024]{1,0:T(8,128)(2,1)S(1)} %get-tuple-element.52.refs_1_), channel_id=1, source_target_pairs={{0,4},{4,0},{8,12},{12,8},{1,5},{5,1},{9,13},{13,9},{2,6},{6,2},{1... | collective-permute-start | bytes 2752520 | tf_op jit(solution)/shard_map/ppermute | solution.py:387
  107.5 41.7 %collective-permute-start.23 = (bf16[448,1024]{1,0:T(8,128)(2,1)S(1)}, bf16[448,1024]{1,0:T(8,128)(2,1)S(1)}, u32[]{:S(2)}, u32[]{:S(2)}) collective-permute-start(bf16[448,1024]{1,0:T(8,128)(2,1)S(1)} %get-tuple-element.51.refs_0_), channel_id=1, source_target_pairs={{0,8},{4,12},{8,0},{12,4},{1,9},{5,13},{9,1},{13,5},{2,10},{6,14},... | collective-permute-start | bytes 2752520 | tf_op jit(solution)/shard_map/ppermute | solution.py:387
  127.2 34.1 %collective-permute-start.19 = (bf16[448,1024]{1,0:T(8,128)(2,1)S(1)}, bf16[448,1024]{1,0:T(8,128)(2,1)S(1)}, u32[]{:S(2)}, u32[]{:S(2)}) collective-permute-start(bf16[448,1024]{1,0:T(8,128)(2,1)S(1)} %collective-permute-done.18.refs_0_), channel_id=1, source_target_pairs={{0,8},{4,12},{8,0},{12,4},{1,9},{5,13},{9,1},{13,5},{2,10},{6,14},... | collective-permute-start | bytes 2752520 | tf_op jit(solution)/shard_map/ppermute | solution.py:387
  128.8 32.5 %collective-permute-start.21 = (bf16[448,1024]{1,0:T(8,128)(2,1)S(1)}, bf16[448,1024]{1,0:T(8,128)(2,1)S(1)}, u32[]{:S(2)}, u32[]{:S(2)}) collective-permute-start(bf16[448,1024]{1,0:T(8,128)(2,1)S(1)} %collective-permute-done.20.refs_2_), channel_id=1, source_target_pairs={{0,4},{4,0},{8,12},{12,8},{1,5},{5,1},{9,13},{13,9},{2,6},{6,2},{1... | collective-permute-start | bytes 2752520 | tf_op jit(solution)/shard_map/ppermute | solution.py:387
  (4 other events, 56.4 us)

commit v2 on v1

--- a/solution.py
+++ b/solution.py
@@ -3,7 +3,6 @@
 
 import jax
 import jax.numpy as jnp
-import numpy as np
 from jax import lax
 from jax.experimental import pallas as pl
 from jax.experimental.pallas import tpu as pltpu
@@ -52,39 +51,26 @@
     return ref[ref.shape[0] - TAIL :].astype(jnp.float32)
 
 
-def pieces_of(rows):
-    n = rows // 128
-    cuts = sorted({0, (n + 2) // 4, (n + 1) // 2, n})
-    return [slice(a * 128, b * 128) for a, b in zip(cuts, cuts[1:])]
-
-
-def product_kernel(layout, entry, coded, *refs):
-    copied, n_hs, n_base = layout
+def product_kernel(layout, start_of, coded, *refs):
+    placed, n_hs, n_base = layout
     refs = list(refs)
     take = lambda k: [refs.pop(0) for _ in range(k)]
-    source, hs = take(2 * copied), take(n_hs)
-    gs, bases, outs = take(n_hs + copied), take(n_base), take(2)
-    arriving = {}
-    if copied:
-        (table, hidden), (held, sems) = source, refs
-        start = pl.multiple_of(table[entry], 128)
-        for k, at in enumerate(pieces_of(held.shape[1])):
-            there = pl.ds(pl.multiple_of(start + at.start, 128), at.stop - at.start)
-            copy = pltpu.make_async_copy(hidden.at[:, there], held.at[:, at], sems.at[k])
-            copy.start()
-            arriving[at.start] = copy
-        hs = [held] + hs
-    rows, cols = hs[0].shape[1], gs[0].shape[1]
+    hs, gs, bases, outs = take(n_hs), take(n_hs), take(n_base), refs
+    cols = gs[0].shape[1]
+    rows = outs[0].shape[0] - (TAIL if coded[0] else 0)
     half, chunk = cols // 2, chunk_of(rows)
+    first = [start_of() if k == 0 and placed else 0 for k in range(n_hs)]
     scales = [[], []]
     for j in range(rows // chunk):
         at = slice(j * chunk, (j + 1) * chunk)
-        if at.start in arriving:
-            arriving[at.start].wait()
         total = None
-        for h, g in zip(hs, gs):
+        for k, (h, g) in enumerate(zip(hs, gs)):
+            if k == 0 and placed:
+                block = h[:, pl.ds(pl.multiple_of(first[k] + j * chunk, chunk), chunk)]
+            else:
+                block = h[:, at]
             term = lax.dot_general(
-                h[:, at], g[...], (((0,), (0,)), ((), ())), preferred_element_type=jnp.float32
+                block, g[...], (((0,), (0,)), ((), ())), preferred_element_type=jnp.float32
             )
             total = term if total is None else total + term
         for part in (0, 1):
@@ -101,16 +87,23 @@
             write_scales(outs[part], scales[part])
 
 
-def slice_kernel(entries, table, hidden, *refs):
-    outs, sems = refs[: len(entries)], refs[len(entries)]
+LOADS = 4
+
+
+def load_kernel(starts_of, hidden, held, *refs):
+    outs, sems = refs[:-1], refs[-1]
+    step = hidden.shape[0] // LOADS
     copies = []
-    for k, out in enumerate(outs):
-        at = pl.ds(pl.multiple_of(table[entries[k]], 128), out.shape[1])
-        copies.append(pltpu.make_async_copy(hidden.at[:, at], out, sems.at[k]))
-    for copy in copies:
-        copy.start()
-    for copy in copies:
-        copy.wait()
+    for k in range(LOADS):
+        at = pl.ds(k * step, step)
+        copies.append(pltpu.make_async_copy(hidden.at[at], held.at[at], sems.at[k]))
+        copies[k].start()
+    starts = [pl.multiple_of(start_of(), 128) for start_of in starts_of]
+    for k in range(LOADS):
+        copies[k].wait()
+        for start, out in zip(starts, outs):
+            at = slice(k * step, (k + 1) * step)
+            out[at] = held[at, pl.ds(start, out.shape[1])]
 
 
 def relay_kernel(n, base, *refs):
@@ -242,11 +235,11 @@
             out[at] = grads[at] * column * by_col[:, k * 128 : (k + 1) * 128]
 
 
-def place_kernel(entries, table, *refs):
-    pieces, out, sems = refs[: len(entries)], refs[-2], refs[-1]
+def place_kernel(rows_of, *refs):
+    pieces, out, sems = refs[: len(rows_of)], refs[-2], refs[-1]
     copies = []
     for k, piece in enumerate(pieces):
-        at = pl.ds(pl.multiple_of(table[entries[k]], 16), piece.shape[0])
+        at = pl.ds(pl.multiple_of(rows_of[k](), 16), piece.shape[0])
         copies.append(pltpu.make_async_copy(piece, out.at[at], sems.at[k]))
     for copy in copies:
         copy.start()
@@ -254,7 +247,6 @@
         copy.wait()
 
 
-SCALARS = pl.BlockSpec(memory_space=pltpu.SMEM)
 FAR = pl.BlockSpec(memory_space=pltpu.HBM)
 ANYWHERE = pl.BlockSpec(memory_space=pl.ANY)
 NEAR = pl.BlockSpec(memory_space=pltpu.VMEM)
@@ -278,49 +270,44 @@
     return jax.ShapeDtypeStruct(dims, dtype)
 
 
-def slices(hidden, table, entries, rows):
-    n = len(entries)
-    if rows % 128:
-        return [lax.dynamic_slice_in_dim(hidden, table[e], rows, axis=1) for e in entries]
-    shapes = [shape_of(hidden.shape[0], rows, dtype=hidden.dtype)] * n
-    return call(
-        functools.partial(slice_kernel, entries),
-        shapes,
-        table,
-        hidden,
-        specs=[SCALARS, FAR],
-        moved=4 * n * hidden.shape[0] * rows,
-        scratch_shapes=[pltpu.SemaphoreType.DMA((n,))],
+def load(hidden, starts_of, rows):
+    if rows % 128 or hidden.shape[0] % (16 * LOADS):
+        return hidden, [lax.dynamic_slice_in_dim(hidden, f(), rows, axis=1) for f in starts_of]
+    shapes = [shape_of(hidden.shape[0], rows, dtype=hidden.dtype)] * len(starts_of)
+    held, *blocks = call(
+        functools.partial(load_kernel, starts_of),
+        [jax.ShapeDtypeStruct(hidden.shape, hidden.dtype)] + shapes,
+        pltpu.with_memory_space_constraint(hidden, pltpu.HBM),
+        specs=[FAR],
+        moved=4 * hidden.size,
+        scratch_shapes=[pltpu.SemaphoreType.DMA((LOADS,))],
     )
-
-
-def product(hidden, table, entry, rows, peers, gs, coded, bases=(), light=False):
+    return held, blocks
+
+
+def product(held, start_of, rows, peers, gs, coded, bases=(), light=False):
     half = gs[0].shape[1] // 2
     shapes = [
         shape_of(rows + TAIL, half, dtype=jnp.bfloat16) if c else shape_of(rows, half) for c in coded
     ]
-    copied = entry is not None and rows % 128 == 0
-    hs, source, scratch = list(peers), [], []
-    if copied:
-        source = [table, hidden]
-        held = pltpu.VMEM((hidden.shape[0], rows), hidden.dtype)
-        scratch = [held, pltpu.SemaphoreType.DMA((len(pieces_of(rows)),))]
-    elif entry is not None:
-        hs = slices(hidden, table, [entry], rows) + hs
+    placed = start_of is not None and rows % 128 == 0
+    hs = list(peers)
+    if placed:
+        hs = [held] + hs
+    elif start_of is not None:
+        hs = [lax.dynamic_slice_in_dim(held, start_of(), rows, axis=1)] + hs
     flops = sum(2 * g.size * rows for g in gs)
-    rest = [*hs, *gs, *bases]
-    moved = sum(x.size * x.dtype.itemsize for x in rest + shapes)
+    moved = sum(x.size * x.dtype.itemsize for x in [*gs, *bases, *shapes])
     if light:
         flops, moved = 0, 1
     return call(
-        functools.partial(product_kernel, (int(copied), len(hs), len(bases)), entry, coded),
+        functools.partial(product_kernel, (placed, len(hs), len(bases)), start_of, coded),
         shapes,
-        *source,
-        *rest,
+        *hs,
+        *gs,
+        *bases,
         flops=flops,
-        specs=[SCALARS, FAR][: len(source)] + [NEAR] * len(rest),
         moved=moved,
-        scratch_shapes=scratch,
     )
 
 
@@ -345,20 +332,19 @@
     return call(kernel, shapes, *bases, *first, *second)
 
 
-def place(pieces, table, entries, out):
+def place(pieces, rows_of, out):
     n = len(pieces)
     old = [] if isinstance(out, jax.ShapeDtypeStruct) else [out]
     return call(
-        functools.partial(place_kernel, entries),
+        functools.partial(place_kernel, rows_of),
         jax.ShapeDtypeStruct(out.shape, out.dtype),
-        table,
         *pieces,
         *old,
-        specs=[SCALARS] + [NEAR] * n + [ANYWHERE] * len(old),
+        specs=[NEAR] * n + [ANYWHERE] * len(old),
         moved=sum(4 * p.size for p in pieces),
         out_specs=ANYWHERE,
         scratch_shapes=[pltpu.SemaphoreType.DMA((n,))],
-        input_output_aliases={n + 1: 0} if old else {},
+        input_output_aliases={n: 0} if old else {},
     )
 
 
@@ -406,63 +392,44 @@
     def per_device(hidden, grad_out, master_weight, row_prev, col_prev):
         rows, cols = master_weight.shape
 
-        def settle(x):
-            return x if rows % 128 else pltpu.with_memory_space_constraint(x, pltpu.HBM)
-
-        given, hidden = hidden, settle(hidden)
+        part_rows = rows // 2
         all_rows, all_cols = rows * n_dp * n_seq, cols * n_tensor
-        dp, seq = lax.axis_index("dp"), lax.axis_index("seq")
-        my_hi, my_lo = seq // n_lo, seq % n_lo
-
-        part_rows = rows // 2
-        cells = np.array([(p, hi, lo) for p in range(n_dp) for hi in range(n_hi) for lo in range(n_lo)])
-        places = np.array([(hi, lo, k) for hi in range(n_hi) for lo in range(n_lo) for k in (0, 1)])
 
         def block_of(hi, lo):
-            return lax.rem(my_hi + hi, n_hi) * n_lo + lax.rem(my_lo + lo, n_lo)
-
-        p, hi, lo = (jnp.asarray(x, jnp.int32) for x in cells.T)
-        columns = (lax.rem(dp + p, n_dp) * n_seq + block_of(hi, lo)) * rows
-        hi, lo, k = (jnp.asarray(x, jnp.int32) for x in places.T)
-        table = block_of(n_hi - hi, n_lo - lo) * rows + k * part_rows
-        table = jnp.concatenate([columns, table])
+            seq = lax.axis_index("seq")
+            mine = lax.div(seq, n_lo), lax.rem(seq, n_lo)
+            return lax.rem(mine[0] + hi, n_hi) * n_lo + lax.rem(mine[1] + lo, n_lo)
 
         def start_of(p, hi, lo):
-            return (p * n_hi + hi) * n_lo + lo
+            return lambda: (
+                lax.rem(lax.axis_index("dp") + p, n_dp) * n_seq + block_of(hi, lo)
+            ) * rows
 
         def row_of(part, hi, lo):
-            return len(cells) + (hi * n_lo + lo) * 2 + part
-
-        def peers_of(group, source):
-            found = {at: [] for at in group}
-            for p in range(1, n_dp if group else 1):
-                entries = [start_of(p, *at) for at in group]
-                for at, block in zip(group, slices(source, table, entries, rows)):
-                    found[at].append(turn(block, "dp", n_dp, p))
-            return found
+            return lambda: block_of(n_hi - hi, n_lo - lo) * rows + part * part_rows
 
         gs = [grad_out] + [turn(grad_out, "dp", n_dp, p) for p in range(1, n_dp)]
         far_group = [(hi, lo) for hi in his for lo in los]
         near_group = [(0, lo) for lo in los] + [(hi, 0) for hi in his] + [(0, 0)]
-        blocks = peers_of(far_group, hidden)
-
-        far, sent = [{}, {}], []
+        keys = [(p, at) for at in far_group + near_group for p in range(1, n_dp)]
+        held, sent = load(hidden, [start_of(p, *at) for p, at in keys], rows)
+        blocks = {at: [] for at in far_group + near_group}
+        for (p, at), block in zip(keys, sent):
+            blocks[at].append(turn(block, "dp", n_dp, p))
+
+        far = [{}, {}]
         for hi, lo in far_group:
-            bases = product(hidden, table, start_of(0, hi, lo), rows, [], gs[:1], (False, False))
+            bases = product(held, start_of(0, hi, lo), rows, [], gs[:1], (False, False))
             if n_dp > 1:
-                coded = product(None, None, None, rows, blocks[hi, lo], gs[1:], (True, True), bases)
+                coded = product(None, None, rows, blocks[hi, lo], gs[1:], (True, True), bases)
             else:
                 coded = [relay(x, []) for x in bases]
-            sent += coded
             far[0][hi, lo] = shift(coded[0], lo=lo)
             far[1][hi, lo] = shift(coded[1], hi=hi)
 
-        hidden = settle(after(given, *sent))
-        blocks = peers_of(near_group, hidden)
-
         def whole_product(hi, lo, coded):
-            entry = start_of(0, hi, lo)
-            return product(hidden, table, entry, rows, blocks[hi, lo], gs, coded, light=True)
+            peers = blocks[hi, lo]
+            return product(held, start_of(0, hi, lo), rows, peers, gs, coded, light=True)
 
         near, base = [{}, {}], [{}, {}]
         for lo in los:
@@ -538,12 +505,12 @@
         )
 
         whole = jax.ShapeDtypeStruct((rows * n_seq, cols), jnp.bfloat16)
-        new_weight = place(pair, table, [row_of(part, 0, 0) for part in (0, 1)], whole)
+        new_weight = place(pair, [row_of(part, 0, 0) for part in (0, 1)], whole)
         pieces = [(x, row_of(part, 0, lo)) for (part, lo), x in along_lo.items()]
         pieces += [(x, row_of(part, hi, 0)) for (part, hi), x in along_hi.items()]
         for group in (pieces, onward):
             if group:
-                new_weight = place([x for x, _ in group], table, [e for _, e in group], new_weight)
+                new_weight = place([x for x, _ in group], [f for _, f in group], new_weight)
         return (new_weight, update, new_rows.reshape(rows), new_cols.reshape(cols))
 
     return jax.shard_map(

time: 164 us -> 164 us (level)
  waiting for transfers between devices: 94.9 us -> 107 us
  Pallas kernels: 40 us -> 30.1 us
    ppermute x14, waiting for transfers between devices: 81.5 us -> 93 us  [shift(): return lax.ppermute(x, 'seq', pairs)]
    pallas_call x19 -> x18, Pallas kernels: 40 us -> 30.1 us  [call(): pl.pallas_call(kernel, out_shape=out_shape, in_specs=specs or [NEAR] * le...]
  transfers between devices with their start and end apart: 24 -> 24, of which waited for: 15 -> 18; matrix products, arithmetic and copies ran while one was open for 1% -> 0% of each run, Pallas kernels for 19% -> 14%
where the time goes in v2:
time: 164 us
  waiting for transfers between devices  107 us (65%)
  Pallas kernels  30.1 us (18%)
  starting transfers between devices  25.1 us (15%)
    ppermute x14, waiting for transfers between devices, shift(): return lax.ppermute(x, 'seq', pairs)  93 us
    pallas_call x18, Pallas kernels, call(): pl.pallas_call(kernel, out_shape=out_shape, in_specs=specs or [NEAR] * le...  30.1 us
    ppermute x14, starting transfers between devices, shift(): return lax.ppermute(x, 'seq', pairs)  15.4 us
    ppermute x5, waiting for transfers between devices, exchange(): parts = [x, lax.ppermute(x, axis, [(a, a ^ d) for a in range(n)])]  8.9 us
    ppermute x5, starting transfers between devices, exchange(): parts = [x, lax.ppermute(x, axis, [(a, a ^ d) for a in range(n)])]  8.43 us
    ppermute x5, waiting for transfers between devices, turn(): return lax.ppermute(x, axis, [(a, (a + step) % n) for a in range(n)])  5.6 us
  transfers between devices with their start and end apart: 24, of which 18 were waited for; matrix products, arithmetic and copies ran while one was open for 0% of the time, Pallas kernels for 14%

profile of v2, /device:TPU:0, one launch (start us, length us, event | category | flops | bytes accessed | tf_op | source)
XLA Modules:
  0.0 163.6 jit_solution(10740160275038043070)
XLA Ops:
  1.2 3.3 %shard_map.84 = (bf16[512,7168]{1,0:T(8,128)(2,1)S(1)}, bf16[512,896]{1,0:T(8,128)(2,1)S(1)}, bf16[512,896]{1,0:T(8,128)(2,1)S(1)}, bf16[512,896]{1,0:T(8,128)(2,1)S(1)}, bf16[512,896]{1,0:T(8,128)(2,1)S(1)}) custom-call(bf16[512,7168]{1,0:T(8,128)(2,1)} %hidden.1), custom_call_target="tpu_custom_call" | custom-call | bytes 14680064 | tf_op jit(solution)/shard_map/pallas_call | solution.py:259
  7.0 2.2 %shard_map.91 = (bf16[912,512]{1,0:T(8,128)(2,1)S(1)}, bf16[912,512]{1,0:T(8,128)(2,1)S(1)}) custom-call(bf16[512,896]{1,0:T(8,128)(2,1)S(1)} %collective-permute-done.6.refs_0_, bf16[512,1024]{1,0:T(8,128)(2,1)S(1)} %collective-permute-done.1.refs_3_.refs_1_, f32[896,512]{1,0:T(8,128)S(1)} %get-tuple-element.41.refs_2_, ...), custom_call_target="tpu_custom_call" | custom-call | flops 939524096 | bytes 6586368 | tf_op jit(solution)/shard_map/pallas_call | solution.py:259
  9.1 2.7 %collective-permute-start.9 = (bf16[912,512]{1,0:T(8,128)(2,1)S(1)}, bf16[912,512]{1,0:T(8,128)(2,1)S(1)}, u32[]{:S(2)}, u32[]{:S(2)}) collective-permute-start(bf16[912,512]{1,0:T(8,128)(2,1)S(1)} %get-tuple-element.45), channel_id=1, source_target_pairs={{0,8},{4,12},{8,0},{12,4},{1,9},{5,13},{9,1},{13,5},{2,10},{6,14},... | collective-permute-start | bytes 2801672 | tf_op jit(solution)/shard_map/ppermute | solution.py:373
  13.9 2.0 %collective-permute-done.4.refs_1_ = bf16[512,896]{1,0:T(8,128)(2,1)S(1)} collective-permute-done((bf16[512,896]{1,0:T(8,128)(2,1)S(1)}, bf16[512,896]{1,0:T(8,128)(2,1)S(1)}, u32[]{:S(2)}, u32[]{:S(2)}) %collective-permute-start.4) | collective-permute-done | bytes 917536 | tf_op jit(solution)/shard_map/ppermute | solution.py:376
  15.8 2.6 %shard_map.88 = (f32[896,512]{1,0:T(8,128)S(1)}, bf16[912,512]{1,0:T(8,128)(2,1)S(1)}) custom-call(bf16[512,7168]{1,0:T(8,128)(2,1)S(1)} %get-tuple-element.31.refs_0_, bf16[512,896]{1,0:T(8,128)(2,1)S(1)} %collective-permute-done.4.refs_1_, bf16[512,1024]{1,0:T(8,128)(2,1)S(1)} %copy-done, bf16[512,1024]{1,0:T(8,128)(2,1)S(1)} %collective-permute-done.1.refs_3_.refs_1_), custom_call_target="tpu_custom_call" | custom-call | bytes 1 | tf_op jit(solution)/shard_map/pallas_call | solution.py:259
  19.0 2.6 %shard_map.86 = (bf16[912,512]{1,0:T(8,128)(2,1)S(1)}, f32[896,512]{1,0:T(8,128)S(1)}) custom-call(bf16[512,7168]{1,0:T(8,128)(2,1)S(1)} %get-tuple-element.31.refs_0_, bf16[512,896]{1,0:T(8,128)(2,1)S(1)} %collective-permute-done.2.refs_1_, bf16[512,1024]{1,0:T(8,128)(2,1)S(1)} %copy-done, bf16[512,1024]{1,0:T(8,128)(2,1)S(1)} %collective-permute-done.1.refs_3_.refs_1_), custom_call_target="tpu_custom_call" | custom-call | bytes 1 | tf_op jit(solution)/shard_map/pallas_call | solution.py:259
  21.8 11.5 %collective-permute-done.9.refs_0_ = bf16[912,512]{1,0:T(8,128)(2,1)S(1)} collective-permute-done((bf16[912,512]{1,0:T(8,128)(2,1)S(1)}, bf16[912,512]{1,0:T(8,128)(2,1)S(1)}, u32[]{:S(2)}, u32[]{:S(2)}) %collective-permute-start.9) | collective-permute-done | bytes 933920 | tf_op jit(solution)/shard_map/ppermute | solution.py:373
  34.9 2.0 %collective-permute-start.10 = (bf16[912,512]{1,0:T(8,128)(2,1)S(1)}, bf16[912,512]{1,0:T(8,128)(2,1)S(1)}, u32[]{:S(2)}, u32[]{:S(2)}) collective-permute-start(bf16[912,512]{1,0:T(8,128)(2,1)S(1)} %shard_map.93), channel_id=1, source_target_pairs={{0,4},{4,0},{8,12},{12,8},{1,5},{5,1},{9,13},{13,9},{2,6},{6,2},{1... | collective-permute-start | bytes 2801672 | tf_op jit(solution)/shard_map/ppermute | solution.py:373
  40.1 2.5 %collective-permute-done.refs_1_ = bf16[512,896]{1,0:T(8,128)(2,1)S(1)} collective-permute-done((bf16[512,896]{1,0:T(8,128)(2,1)S(1)}, bf16[512,896]{1,0:T(8,128)(2,1)S(1)}, u32[]{:S(2)}, u32[]{:S(2)}) %collective-permute-start) | collective-permute-done | bytes 917536 | tf_op jit(solution)/shard_map/ppermute | solution.py:376
  42.6 2.1 %shard_map.85 = (f32[896,512]{1,0:T(8,128)S(1)}, f32[896,512]{1,0:T(8,128)S(1)}) custom-call(bf16[512,7168]{1,0:T(8,128)(2,1)S(1)} %get-tuple-element.31.refs_0_, bf16[512,896]{1,0:T(8,128)(2,1)S(1)} %collective-permute-done.refs_1_, bf16[512,1024]{1,0:T(8,128)(2,1)S(1)} %copy-done, bf16[512,1024]{1,0:T(8,128)(2,1)S(1)} %collective-permute-done.1.refs_3_.refs_1_), custom_call_target="tpu_custom_call" | custom-call | bytes 1 | tf_op jit(solution)/shard_map/pallas_call | solution.py:259
  44.7 8.7 %collective-permute-done.5.refs_0_ = bf16[912,512]{1,0:T(8,128)(2,1)S(1)} collective-permute-done((bf16[912,512]{1,0:T(8,128)(2,1)S(1)}, bf16[912,512]{1,0:T(8,128)(2,1)S(1)}, u32[]{:S(2)}, u32[]{:S(2)}) %collective-permute-start.5) | collective-permute-done | bytes 933920 | tf_op jit(solution)/shard_map/ppermute | solution.py:373
  56.4 18.2 %collective-permute-done.10.refs_3_ = bf16[912,512]{1,0:T(8,128)(2,1)S(1)} collective-permute-done((bf16[912,512]{1,0:T(8,128)(2,1)S(1)}, bf16[912,512]{1,0:T(8,128)(2,1)S(1)}, u32[]{:S(2)}, u32[]{:S(2)}) %collective-permute-start.10) | collective-permute-done | bytes 933920 | tf_op jit(solution)/shard_map/ppermute | solution.py:373
  74.6 2.6 %shard_map.94 = (f32[896,1024]{1,0:T(8,128)S(1)}, f32[7,128]{1,0:T(8,128)S(1)}, f32[1,1024]{1,0:T(1,128)S(1)}) custom-call(f32[896,512]{1,0:T(8,128)S(1)} %shard_map.87.refs_0_, f32[896,512]{1,0:T(8,128)S(1)} %shard_map.89.refs_1_, bf16[912,512]{1,0:T(8,128)(2,1)S(1)} %collective-permute-done.8.refs_2_, bf16[912,512]{1,0:T(8,128)(2,1)S(1)} %collective-permute-done.10.refs_3_), custom_call_target="tpu_custom_call" | custom-call | bytes 9215488 | tf_op jit(solution)/shard_map/pallas_call | solution.py:259
  78.8 2.0 %collective-permute-done.11 = f32[7,128]{1,0:T(8,128)S(1)} collective-permute-done((f32[7,128]{1,0:T(8,128)S(1)}, f32[7,128]{1,0:T(8,128)S(1)}, u32[]{:S(2)}, u32[]{:S(2)}) %collective-permute-start.11) | collective-permute-done | bytes 3616 | tf_op jit(solution)/shard_map/ppermute | solution.py:384
  80.8 2.6 %collective-permute-start.12 = (f32[7,128]{1,0:T(8,128)S(1)}, f32[7,128]{1,0:T(8,128)S(1)}, u32[]{:S(2)}, u32[]{:S(2)}) collective-permute-start(f32[7,128]{1,0:T(8,128)S(1)} %add.12.refs_0_), channel_id=1, source_target_pairs={{0,2},{1,3},{2,0},{3,1},{4,6},{5,7},{6,4},{7,5},{8,10},{9,11},{10,... | collective-permute-start | bytes 10760 | tf_op jit(solution)/shard_map/ppermute | solution.py:384
  83.4 1.9 %collective-permute-done.12.refs_1_ = f32[7,128]{1,0:T(8,128)S(1)} collective-permute-done((f32[7,128]{1,0:T(8,128)S(1)}, f32[7,128]{1,0:T(8,128)S(1)}, u32[]{:S(2)}, u32[]{:S(2)}) %collective-permute-start.12) | collective-permute-done | bytes 3616 | tf_op jit(solution)/shard_map/ppermute | solution.py:384
  88.6 2.2 %collective-permute-done.14 = f32[2,1024]{1,0:T(2,128)S(1)} collective-permute-done((f32[2,1024]{1,0:T(2,128)S(1)}, f32[2,1024]{1,0:T(2,128)S(1)}, u32[]{:S(2)}, u32[]{:S(2)}) %collective-permute-start.14) | collective-permute-done | bytes 8224 | tf_op jit(solution)/shard_map/ppermute | solution.py:373
  91.1 3.3 %collective-permute-done.15.refs_1_ = f32[2,1024]{1,0:T(2,128)S(1)} collective-permute-done((f32[2,1024]{1,0:T(2,128)S(1)}, f32[2,1024]{1,0:T(2,128)S(1)}, u32[]{:S(2)}, u32[]{:S(2)}) %collective-permute-start.15) | collective-permute-done | bytes 8224 | tf_op jit(solution)/shard_map/ppermute | solution.py:373
  96.6 2.0 %collective-permute-done.16 = f32[1,128]{1,0:T(1,128)S(1)} collective-permute-done((f32[1,128]{1,0:T(1,128)S(1)}, f32[1,128]{1,0:T(1,128)S(1)}, u32[]{:S(2)}, u32[]{:S(2)}) %collective-permute-start.16) | collective-permute-done | bytes 544 | tf_op jit(solution)/shard_map/ppermute | solution.py:384
  98.5 2.6 %collective-permute-start.17 = (f32[1,128]{1,0:T(1,128)S(1)}, f32[1,128]{1,0:T(1,128)S(1)}, u32[]{:S(2)}, u32[]{:S(2)}) collective-permute-start(f32[1,128]{1,0:T(1,128)S(1)} %add.15.refs_0_), channel_id=1, source_target_pairs={{0,2},{1,3},{2,0},{3,1},{4,6},{5,7},{6,4},{7,5},{8,10},{9,11},{10,... | collective-permute-start | bytes 1544 | tf_op jit(solution)/shard_map/ppermute | solution.py:384
  107.9 19.2 %collective-permute-done.18.refs_0_ = bf16[448,1024]{1,0:T(8,128)(2,1)S(1)} collective-permute-done((bf16[448,1024]{1,0:T(8,128)(2,1)S(1)}, bf16[448,1024]{1,0:T(8,128)(2,1)S(1)}, u32[]{:S(2)}, u32[]{:S(2)}) %collective-permute-start.18) | collective-permute-done | bytes 917536 | tf_op jit(solution)/shard_map/ppermute | solution.py:373
  130.4 16.4 %collective-permute-done.22.refs_1_ = bf16[448,1024]{1,0:T(8,128)(2,1)S(1)} collective-permute-done((bf16[448,1024]{1,0:T(8,128)(2,1)S(1)}, bf16[448,1024]{1,0:T(8,128)(2,1)S(1)}, u32[]{:S(2)}, u32[]{:S(2)}) %collective-permute-start.22) | collective-permute-done | bytes 917536 | tf_op jit(solution)/shard_map/ppermute | solution.py:373
  146.8 2.3 %shard_map.101 = f32[896,1024]{1,0:T(8,128)} custom-call(f32[896,1024]{1,0:T(8,128)S(1)} %get-tuple-element.55.grads, f32[7,128]{1,0:T(8,128)S(1)} %get-tuple-element.49.row_factor, f32[1,1024]{1,0:T(1,128)S(1)} %get-tuple-element.51.col_factor, f32[1,128]{1,0:T(1,128)S(1)} %add.15.refs_0_, f32[1,128]{1,0:T(1,128)S(1)} %collective-permute-done.17.refs_1_), custom_call_target="tpu_custom_call" | custom-call | bytes 7348736 | tf_op jit(solution)/shard_map/pallas_call | solution.py:259
  150.9 11.3 %collective-permute-done.19.refs_0_ = bf16[448,1024]{1,0:T(8,128)(2,1)S(1)} collective-permute-done((bf16[448,1024]{1,0:T(8,128)(2,1)S(1)}, bf16[448,1024]{1,0:T(8,128)(2,1)S(1)}, u32[]{:S(2)}, u32[]{:S(2)}) %collective-permute-start.19) | collective-permute-done | bytes 917536 | tf_op jit(solution)/shard_map/ppermute | solution.py:373
  (54 shorter events, 34.0 us)
Async XLA Ops:
  0.6 6.3 %collective-permute-start.1 = (bf16[512,1024]{1,0:T(8,128)(2,1)}, bf16[512,1024]{1,0:T(8,128)(2,1)S(1)}, u32[]{:S(2)}, u32[]{:S(2)}) collective-permute-start(bf16[512,1024]{1,0:T(8,128)(2,1)} %refs_1_.1), channel_id=1, source_target_pairs={{0,16},{16,0},{1,17},{17,1},{2,18},{18,2},{3,19},{19,3},{4,20},{20... | collective-permute-start | bytes 3145736 | tf_op jit(solution)/shard_map/ppermute | solution.py:376
  4.4 2.5 %collective-permute-start.6 = (bf16[512,896]{1,0:T(8,128)(2,1)S(1)}, bf16[512,896]{1,0:T(8,128)(2,1)S(1)}, u32[]{:S(2)}, u32[]{:S(2)}) collective-permute-start(bf16[512,896]{1,0:T(8,128)(2,1)S(1)} %get-tuple-element.40), channel_id=1, source_target_pairs={{0,16},{16,0},{1,17},{17,1},{2,18},{18,2},{3,19},{19,3},{4,20},{20... | collective-permute-start | bytes 2752520 | tf_op jit(solution)/shard_map/ppermute | solution.py:376
  9.1 24.3 %collective-permute-start.9 = (bf16[912,512]{1,0:T(8,128)(2,1)S(1)}, bf16[912,512]{1,0:T(8,128)(2,1)S(1)}, u32[]{:S(2)}, u32[]{:S(2)}) collective-permute-start(bf16[912,512]{1,0:T(8,128)(2,1)S(1)} %get-tuple-element.45), channel_id=1, source_target_pairs={{0,8},{4,12},{8,0},{12,4},{1,9},{5,13},{9,1},{13,5},{2,10},{6,14},... | collective-permute-start | bytes 2801672 | tf_op jit(solution)/shard_map/ppermute | solution.py:373
  11.8 25.0 %collective-permute-start.7 = (bf16[912,512]{1,0:T(8,128)(2,1)S(1)}, bf16[912,512]{1,0:T(8,128)(2,1)S(1)}, u32[]{:S(2)}, u32[]{:S(2)}) collective-permute-start(bf16[912,512]{1,0:T(8,128)(2,1)S(1)} %get-tuple-element.43), channel_id=1, source_target_pairs={{0,4},{4,0},{8,12},{12,8},{1,5},{5,1},{9,13},{13,9},{2,6},{6,2},{1... | collective-permute-start | bytes 2801672 | tf_op jit(solution)/shard_map/ppermute | solution.py:373
  13.3 2.5 %collective-permute-start.4 = (bf16[512,896]{1,0:T(8,128)(2,1)S(1)}, bf16[512,896]{1,0:T(8,128)(2,1)S(1)}, u32[]{:S(2)}, u32[]{:S(2)}) collective-permute-start(bf16[512,896]{1,0:T(8,128)(2,1)S(1)} %get-tuple-element.37), channel_id=1, source_target_pairs={{0,16},{16,0},{1,17},{17,1},{2,18},{18,2},{3,19},{19,3},{4,20},{20... | collective-permute-start | bytes 2752520 | tf_op jit(solution)/shard_map/ppermute | solution.py:376
  13.3 5.7 %collective-permute-start.2 = (bf16[512,896]{1,0:T(8,128)(2,1)S(1)}, bf16[512,896]{1,0:T(8,128)(2,1)S(1)}, u32[]{:S(2)}, u32[]{:S(2)}) collective-permute-start(bf16[512,896]{1,0:T(8,128)(2,1)S(1)} %get-tuple-element.34), channel_id=1, source_target_pairs={{0,16},{16,0},{1,17},{17,1},{2,18},{18,2},{3,19},{19,3},{4,20},{20... | collective-permute-start | bytes 2752520 | tf_op jit(solution)/shard_map/ppermute | solution.py:376
  18.5 34.9 %collective-permute-start.5 = (bf16[912,512]{1,0:T(8,128)(2,1)S(1)}, bf16[912,512]{1,0:T(8,128)(2,1)S(1)}, u32[]{:S(2)}, u32[]{:S(2)}) collective-permute-start(bf16[912,512]{1,0:T(8,128)(2,1)S(1)} %get-tuple-element.38), channel_id=1, source_target_pairs={{0,8},{4,12},{8,0},{12,4},{1,9},{5,13},{9,1},{13,5},{2,10},{6,14},... | collective-permute-start | bytes 2801672 | tf_op jit(solution)/shard_map/ppermute | solution.py:373
  21.7 33.8 %collective-permute-start.3 = (bf16[912,512]{1,0:T(8,128)(2,1)S(1)}, bf16[912,512]{1,0:T(8,128)(2,1)S(1)}, u32[]{:S(2)}, u32[]{:S(2)}) collective-permute-start(bf16[912,512]{1,0:T(8,128)(2,1)S(1)} %get-tuple-element.35), channel_id=1, source_target_pairs={{0,4},{4,0},{8,12},{12,8},{1,5},{5,1},{9,13},{13,9},{2,6},{6,2},{1... | collective-permute-start | bytes 2801672 | tf_op jit(solution)/shard_map/ppermute | solution.py:373
  34.9 39.7 %collective-permute-start.10 = (bf16[912,512]{1,0:T(8,128)(2,1)S(1)}, bf16[912,512]{1,0:T(8,128)(2,1)S(1)}, u32[]{:S(2)}, u32[]{:S(2)}) collective-permute-start(bf16[912,512]{1,0:T(8,128)(2,1)S(1)} %shard_map.93), channel_id=1, source_target_pairs={{0,4},{4,0},{8,12},{12,8},{1,5},{5,1},{9,13},{13,9},{2,6},{6,2},{1... | collective-permute-start | bytes 2801672 | tf_op jit(solution)/shard_map/ppermute | solution.py:373
  38.5 36.0 %collective-permute-start.8 = (bf16[912,512]{1,0:T(8,128)(2,1)S(1)}, bf16[912,512]{1,0:T(8,128)(2,1)S(1)}, u32[]{:S(2)}, u32[]{:S(2)}) collective-permute-start(bf16[912,512]{1,0:T(8,128)(2,1)S(1)} %shard_map.92), channel_id=1, source_target_pairs={{0,8},{4,12},{8,0},{12,4},{1,9},{5,13},{9,1},{13,5},{2,10},{6,14},... | collective-permute-start | bytes 2801672 | tf_op jit(solution)/shard_map/ppermute | solution.py:373
  40.1 2.5 %collective-permute-start = (bf16[512,896]{1,0:T(8,128)(2,1)S(1)}, bf16[512,896]{1,0:T(8,128)(2,1)S(1)}, u32[]{:S(2)}, u32[]{:S(2)}) collective-permute-start(bf16[512,896]{1,0:T(8,128)(2,1)S(1)} %get-tuple-element.32), channel_id=1, source_target_pairs={{0,16},{16,0},{1,17},{17,1},{2,18},{18,2},{3,19},{19,3},{4,20},{20... | collective-permute-start | bytes 2752520 | tf_op jit(solution)/shard_map/ppermute | solution.py:376
  77.1 3.7 %collective-permute-start.11 = (f32[7,128]{1,0:T(8,128)S(1)}, f32[7,128]{1,0:T(8,128)S(1)}, u32[]{:S(2)}, u32[]{:S(2)}) collective-permute-start(f32[7,128]{1,0:T(8,128)S(1)} %get-tuple-element.48), channel_id=1, source_target_pairs={{0,1},{1,0},{2,3},{3,2},{4,5},{5,4},{6,7},{7,6},{8,9},{9,8},{10,11... | collective-permute-start | bytes 10760 | tf_op jit(solution)/shard_map/ppermute | solution.py:384
  80.8 4.5 %collective-permute-start.12 = (f32[7,128]{1,0:T(8,128)S(1)}, f32[7,128]{1,0:T(8,128)S(1)}, u32[]{:S(2)}, u32[]{:S(2)}) collective-permute-start(f32[7,128]{1,0:T(8,128)S(1)} %add.12.refs_0_), channel_id=1, source_target_pairs={{0,2},{1,3},{2,0},{3,1},{4,6},{5,7},{6,4},{7,5},{8,10},{9,11},{10,... | collective-permute-start | bytes 10760 | tf_op jit(solution)/shard_map/ppermute | solution.py:384
  85.9 1.2 collective-permute-start.13
  87.1 3.7 %collective-permute-start.14 = (f32[2,1024]{1,0:T(2,128)S(1)}, f32[2,1024]{1,0:T(2,128)S(1)}, u32[]{:S(2)}, u32[]{:S(2)}) collective-permute-start(f32[2,1024]{1,0:T(2,128)S(1)} %add.13), channel_id=1, source_target_pairs={{0,4},{4,0},{8,12},{12,8},{1,5},{5,1},{9,13},{13,9},{2,6},{6,2},{1... | collective-permute-start | bytes 24584 | tf_op jit(solution)/shard_map/ppermute | solution.py:373
  90.7 3.7 %collective-permute-start.15 = (f32[2,1024]{1,0:T(2,128)S(1)}, f32[2,1024]{1,0:T(2,128)S(1)}, u32[]{:S(2)}, u32[]{:S(2)}) collective-permute-start(f32[2,1024]{1,0:T(2,128)S(1)} %add.14.refs_0_), channel_id=1, source_target_pairs={{0,8},{4,12},{8,0},{12,4},{1,9},{5,13},{9,1},{13,5},{2,10},{6,14},... | collective-permute-start | bytes 24584 | tf_op jit(solution)/shard_map/ppermute | solution.py:373
  95.0 3.5 %collective-permute-start.16 = (f32[1,128]{1,0:T(1,128)S(1)}, f32[1,128]{1,0:T(1,128)S(1)}, u32[]{:S(2)}, u32[]{:S(2)}) collective-permute-start(f32[1,128]{1,0:T(1,128)S(1)} %get-tuple-element.52), channel_id=1, source_target_pairs={{0,1},{1,0},{2,3},{3,2},{4,5},{5,4},{6,7},{7,6},{8,9},{9,8},{10,11... | collective-permute-start | bytes 1544 | tf_op jit(solution)/shard_map/ppermute | solution.py:384
  98.5 4.4 %collective-permute-start.17 = (f32[1,128]{1,0:T(1,128)S(1)}, f32[1,128]{1,0:T(1,128)S(1)}, u32[]{:S(2)}, u32[]{:S(2)}) collective-permute-start(f32[1,128]{1,0:T(1,128)S(1)} %add.15.refs_0_), channel_id=1, source_target_pairs={{0,2},{1,3},{2,0},{3,1},{4,6},{5,7},{6,4},{7,5},{8,10},{9,11},{10,... | collective-permute-start | bytes 1544 | tf_op jit(solution)/shard_map/ppermute | solution.py:384
  103.8 23.4 %collective-permute-start.18 = (bf16[448,1024]{1,0:T(8,128)(2,1)S(1)}, bf16[448,1024]{1,0:T(8,128)(2,1)S(1)}, u32[]{:S(2)}, u32[]{:S(2)}) collective-permute-start(bf16[448,1024]{1,0:T(8,128)(2,1)S(1)} %get-tuple-element.53.refs_0_), channel_id=1, source_target_pairs={{0,4},{4,0},{8,12},{12,8},{1,5},{5,1},{9,13},{13,9},{2,6},{6,2},{1... | collective-permute-start | bytes 2752520 | tf_op jit(solution)/shard_map/ppermute | solution.py:373
  105.3 23.3 %collective-permute-start.20 = (bf16[448,1024]{1,0:T(8,128)(2,1)S(1)}, bf16[448,1024]{1,0:T(8,128)(2,1)S(1)}, u32[]{:S(2)}, u32[]{:S(2)}) collective-permute-start(bf16[448,1024]{1,0:T(8,128)(2,1)S(1)} %get-tuple-element.54.refs_1_), channel_id=1, source_target_pairs={{0,8},{4,12},{8,0},{12,4},{1,9},{5,13},{9,1},{13,5},{2,10},{6,14},... | collective-permute-start | bytes 2752520 | tf_op jit(solution)/shard_map/ppermute | solution.py:373
  105.8 41.0 %collective-permute-start.22 = (bf16[448,1024]{1,0:T(8,128)(2,1)S(1)}, bf16[448,1024]{1,0:T(8,128)(2,1)S(1)}, u32[]{:S(2)}, u32[]{:S(2)}) collective-permute-start(bf16[448,1024]{1,0:T(8,128)(2,1)S(1)} %get-tuple-element.54.refs_1_), channel_id=1, source_target_pairs={{0,4},{4,0},{8,12},{12,8},{1,5},{5,1},{9,13},{13,9},{2,6},{6,2},{1... | collective-permute-start | bytes 2752520 | tf_op jit(solution)/shard_map/ppermute | solution.py:373
  106.2 42.9 %collective-permute-start.23 = (bf16[448,1024]{1,0:T(8,128)(2,1)S(1)}, bf16[448,1024]{1,0:T(8,128)(2,1)S(1)}, u32[]{:S(2)}, u32[]{:S(2)}) collective-permute-start(bf16[448,1024]{1,0:T(8,128)(2,1)S(1)} %get-tuple-element.53.refs_0_), channel_id=1, source_target_pairs={{0,8},{4,12},{8,0},{12,4},{1,9},{5,13},{9,1},{13,5},{2,10},{6,14},... | collective-permute-start | bytes 2752520 | tf_op jit(solution)/shard_map/ppermute | solution.py:373
  127.1 35.1 %collective-permute-start.19 = (bf16[448,1024]{1,0:T(8,128)(2,1)S(1)}, bf16[448,1024]{1,0:T(8,128)(2,1)S(1)}, u32[]{:S(2)}, u32[]{:S(2)}) collective-permute-start(bf16[448,1024]{1,0:T(8,128)(2,1)S(1)} %collective-permute-done.18.refs_0_), channel_id=1, source_target_pairs={{0,8},{4,12},{8,0},{12,4},{1,9},{5,13},{9,1},{13,5},{2,10},{6,14},... | collective-permute-start | bytes 2752520 | tf_op jit(solution)/shard_map/ppermute | solution.py:373
  128.6 33.6 %collective-permute-start.21 = (bf16[448,1024]{1,0:T(8,128)(2,1)S(1)}, bf16[448,1024]{1,0:T(8,128)(2,1)S(1)}, u32[]{:S(2)}, u32[]{:S(2)}) collective-permute-start(bf16[448,1024]{1,0:T(8,128)(2,1)S(1)} %collective-permute-done.20.refs_2_), channel_id=1, source_target_pairs={{0,4},{4,0},{8,12},{12,8},{1,5},{5,1},{9,13},{13,9},{2,6},{6,2},{1... | collective-permute-start | bytes 2752520 | tf_op jit(solution)/shard_map/ppermute | solution.py:373
  (4 other events, 117.7 us)

commit v3 on v2

--- a/solution.py
+++ b/solution.py
@@ -87,23 +87,22 @@
             write_scales(outs[part], scales[part])
 
 
-LOADS = 4
-
-
-def load_kernel(starts_of, hidden, held, *refs):
-    outs, sems = refs[:-1], refs[-1]
-    step = hidden.shape[0] // LOADS
+def fetch_kernel(starts_of, hidden, grad_out, *refs):
+    outs, grad_held, sems = refs[:-2], refs[-2], refs[-1]
     copies = []
-    for k in range(LOADS):
-        at = pl.ds(k * step, step)
-        copies.append(pltpu.make_async_copy(hidden.at[at], held.at[at], sems.at[k]))
+    for k, (start_of, out) in enumerate(zip(starts_of, outs)):
+        at = pl.ds(pl.multiple_of(start_of(), 128), out.shape[1])
+        copies.append(pltpu.make_async_copy(hidden.at[:, at], out, sems.at[k]))
         copies[k].start()
-    starts = [pl.multiple_of(start_of(), 128) for start_of in starts_of]
-    for k in range(LOADS):
-        copies[k].wait()
-        for start, out in zip(starts, outs):
-            at = slice(k * step, (k + 1) * step)
-            out[at] = held[at, pl.ds(start, out.shape[1])]
+    copies.append(pltpu.make_async_copy(grad_out, grad_held, sems.at[len(outs)]))
+    copies[-1].start()
+    for copy in copies:
+        copy.wait()
+
+
+def cut_kernel(starts_of, hidden, *outs):
+    for start_of, out in zip(starts_of, outs):
+        out[...] = hidden[:, pl.ds(pl.multiple_of(start_of(), 128), out.shape[1])]
 
 
 def relay_kernel(n, base, *refs):
@@ -135,59 +134,74 @@
         out[at] = total
 
 
-def final_kernel(counts, *refs):
-    bases, refs = refs[:2], refs[2:]
-    messages = refs[: counts[0]], refs[counts[0] : sum(counts)]
-    out, row_out, col_out = refs[sum(counts) :]
-    rows, half = bases[0].shape
+def final_kernel(n, n_before, base, *refs):
+    messages, refs = refs[:n], refs[n:]
+    before, (out, row_out, col_out) = refs[:n_before], refs[n_before:]
+    rows, half = base.shape
     chunk = chunk_of(rows)
-    tails = [[read_scales(m) for m in group] for group in messages]
-    col_sums = [jnp.zeros((1, half), jnp.float32)] * 2
+    tails = [read_scales(m) for m in messages]
+    col_sum = jnp.zeros((1, half), jnp.float32)
     for j in range(rows // chunk):
         at = slice(j * chunk, (j + 1) * chunk)
         row_sum = jnp.zeros((chunk, 128), jnp.float32)
-        for part in (0, 1):
-            total = bases[part][at]
-            for m, tail in zip(messages[part], tails[part]):
-                total = total + decode(m[at], tail[j : j + 1])
-            out[at, part * half : (part + 1) * half] = total
-            squares = total * total
-            col_sums[part] = col_sums[part] + jnp.sum(squares, axis=0, keepdims=True)
-            for k in range(half // 128):
-                row_sum = row_sum + squares[:, k * 128 : (k + 1) * 128]
-        row_out[j : j + 1] = jnp.sum(row_sum.T, axis=0, keepdims=True)
+        total = base[at]
+        for m, tail in zip(messages, tails):
+            total = total + decode(m[at], tail[j : j + 1])
+        out[at] = total
+        squares = total * total
+        col_sum = col_sum + jnp.sum(squares, axis=0, keepdims=True)
+        for k in range(half // 128):
+            row_sum = row_sum + squares[:, k * 128 : (k + 1) * 128]
+        row_sum = jnp.sum(row_sum.T, axis=0, keepdims=True)
+        for row in before:
+            row_sum = row_sum + row[j : j + 1]
+        row_out[j : j + 1] = row_sum
+    col_out[...] = col_sum
+
+
+def columns_of(halves):
+    half = halves[0].shape[1]
     for part in (0, 1):
-        col_out[:, part * half : (part + 1) * half] = col_sums[part]
+        for k in range(0, half, 128):
+            yield halves[part], slice(k, k + 128), slice(part * half + k, part * half + k + 128)
 
 
 def as_column(row):
     return jnp.broadcast_to(row, (128, row.shape[1])).T
 
 
-def rows_kernel(n, all_cols, grads, row_prev, col_part, *refs):
+def tree_sum(terms):
+    while len(terms) > 1:
+        pairs = [sum(terms[k + 1 : k + 2], terms[k]) for k in range(0, len(terms), 2)]
+        terms = pairs
+    return terms[0]
+
+
+def rows_kernel(n, all_cols, low, high, row_prev, low_col, high_col, *refs):
     parts, (rows_out, by_row_out, both_out) = refs[:n], refs[n:]
-    total = sum(p[...] for p in parts[1:]) + parts[0][...] if n > 1 else parts[0][...]
+    total = tree_sum([p[...] for p in parts])
     total = total + small_term * all_cols
     new_rows = decay_rate * row_prev[...] + (1.0 - decay_rate) * total / all_cols
     rows_out[...] = new_rows
     by_row_out[...] = 1.0 / jnp.sqrt(new_rows)
     inverse = 1.0 / new_rows
     n_chunks, chunk = new_rows.shape
-    cols = grads.shape[1]
-    sums = [jnp.zeros((1, 128), jnp.float32)] * (cols // 128)
+    half = low.shape[1]
+    sums = [jnp.zeros((1, 128), jnp.float32)] * (2 * half // 128)
     for j in range(n_chunks):
         weight = as_column(inverse[j : j + 1])
-        for k in range(cols // 128):
-            g = grads[j * chunk : (j + 1) * chunk, k * 128 : (k + 1) * 128]
+        for k, (grads, at, _) in enumerate(columns_of((low, high))):
+            g = grads[j * chunk : (j + 1) * chunk, at]
             sums[k] = sums[k] + jnp.sum(g * g * weight, axis=0, keepdims=True)
-    both_out[0:1] = col_part[...]
-    for k in range(cols // 128):
-        both_out[1:2, k * 128 : (k + 1) * 128] = sums[k]
+    both_out[0:1, :half] = low_col[...]
+    both_out[0:1, half:] = high_col[...]
+    for k, (_, _, there) in enumerate(columns_of((low, high))):
+        both_out[1:2, there] = sums[k]
 
 
 def cols_kernel(n, all_rows, col_prev, *refs):
     parts, (cols_out, by_col_out, total_out) = refs[:n], refs[n:]
-    both = sum(p[...] for p in parts[1:]) + parts[0][...] if n > 1 else parts[0][...]
+    both = tree_sum([p[...] for p in parts])
     total = both[0:1] + small_term * all_rows
     new_cols = decay_rate * col_prev[...] + (1.0 - decay_rate) * total / all_rows
     cols_out[...] = new_cols
@@ -204,35 +218,33 @@
     return by_row[...] / clip, by_col[...]
 
 
-def fresh_kernel(n, elements, grads, weight, row_factor, col_factor, *refs):
+def fresh_kernel(n, elements, low, high, weight, row_factor, col_factor, *refs):
     parts, outs = refs[:n], refs[n:]
     by_row, by_col = factors(elements, parts, row_factor, col_factor)
     n_chunks, chunk = by_row.shape
-    cols = grads.shape[1]
+    split = outs[0].shape[0]
     for j in range(n_chunks):
         column = as_column(by_row[j : j + 1])
-        for k in range(cols // 128):
-            at = slice(j * chunk, (j + 1) * chunk), slice(k * 128, (k + 1) * 128)
-            update = grads[at] * column * by_col[:, k * 128 : (k + 1) * 128]
-            fresh = (weight[at] - learn_rate * update).astype(jnp.bfloat16)
-            split = outs[0].shape[0]
-            low, high = j * chunk, (j + 1) * chunk
-            if low < split:
-                outs[0][low : min(high, split), at[1]] = fresh[: min(high, split) - low]
-            if high > split:
-                first = max(low, split)
-                outs[1][first - split : high - split, at[1]] = fresh[first - low :]
-
-
-def update_kernel(n, elements, grads, row_factor, col_factor, *refs):
+        first, last = j * chunk, (j + 1) * chunk
+        for grads, here, there in columns_of((low, high)):
+            update = grads[first:last, here] * column * by_col[:, there]
+            fresh = (weight[first:last, there] - learn_rate * update).astype(jnp.bfloat16)
+            if first < split:
+                outs[0][first : min(last, split), there] = fresh[: min(last, split) - first]
+            if last > split:
+                cut = max(first, split)
+                outs[1][cut - split : last - split, there] = fresh[cut - first :]
+
+
+def update_kernel(n, elements, low, high, row_factor, col_factor, *refs):
     parts, out = refs[:n], refs[n]
     by_row, by_col = factors(elements, parts, row_factor, col_factor)
     n_chunks, chunk = by_row.shape
     for j in range(n_chunks):
         column = as_column(by_row[j : j + 1])
-        for k in range(grads.shape[1] // 128):
-            at = slice(j * chunk, (j + 1) * chunk), slice(k * 128, (k + 1) * 128)
-            out[at] = grads[at] * column * by_col[:, k * 128 : (k + 1) * 128]
+        for grads, here, there in columns_of((low, high)):
+            at = slice(j * chunk, (j + 1) * chunk)
+            out[at, there] = grads[at, here] * column * by_col[:, there]
 
 
 def place_kernel(rows_of, *refs):
@@ -270,19 +282,29 @@
     return jax.ShapeDtypeStruct(dims, dtype)
 
 
-def load(hidden, starts_of, rows):
-    if rows % 128 or hidden.shape[0] % (16 * LOADS):
-        return hidden, [lax.dynamic_slice_in_dim(hidden, f(), rows, axis=1) for f in starts_of]
+def fetch(hidden, grad_out, starts_of, rows):
+    if rows % 128 or not starts_of:
+        return cut(hidden, starts_of, rows), grad_out
+    far = lambda x: pltpu.with_memory_space_constraint(x, pltpu.HBM)
+    blocks = [shape_of(hidden.shape[0], rows, dtype=hidden.dtype)] * len(starts_of)
+    *blocks, grad_held = call(
+        functools.partial(fetch_kernel, starts_of),
+        blocks + [shape_of(*grad_out.shape, dtype=grad_out.dtype)],
+        far(hidden),
+        far(grad_out),
+        specs=[FAR, FAR],
+        moved=4 * (len(starts_of) * hidden.shape[0] * rows + grad_out.size),
+        scratch_shapes=[pltpu.SemaphoreType.DMA((len(starts_of) + 1,))],
+    )
+    return blocks, grad_held
+
+
+def cut(hidden, starts_of, rows):
+    if rows % 128 or not starts_of:
+        return [lax.dynamic_slice_in_dim(hidden, f(), rows, axis=1) for f in starts_of]
     shapes = [shape_of(hidden.shape[0], rows, dtype=hidden.dtype)] * len(starts_of)
-    held, *blocks = call(
-        functools.partial(load_kernel, starts_of),
-        [jax.ShapeDtypeStruct(hidden.shape, hidden.dtype)] + shapes,
-        pltpu.with_memory_space_constraint(hidden, pltpu.HBM),
-        specs=[FAR],
-        moved=4 * hidden.size,
-        scratch_shapes=[pltpu.SemaphoreType.DMA((LOADS,))],
-    )
-    return held, blocks
+    moved = 4 * len(starts_of) * hidden.shape[0] * rows
+    return call(functools.partial(cut_kernel, starts_of), shapes, hidden, moved=moved)
 
 
 def product(held, start_of, rows, peers, gs, coded, bases=(), light=False):
@@ -324,12 +346,12 @@
     return call(functools.partial(gather_kernel, len(messages)), shape, base, *messages)
 
 
-def final(bases, first, second):
-    rows, half = bases[0].shape
+def final(base, messages, before=()):
+    rows, half = base.shape
     chunk = chunk_of(rows)
-    shapes = [shape_of(rows, 2 * half), shape_of(rows // chunk, chunk), shape_of(1, 2 * half)]
-    kernel = functools.partial(final_kernel, (len(first), len(second)))
-    return call(kernel, shapes, *bases, *first, *second)
+    shapes = [shape_of(rows, half), shape_of(rows // chunk, chunk), shape_of(1, half)]
+    kernel = functools.partial(final_kernel, len(messages), len(before))
+    return call(kernel, shapes, base, *messages, *before)
 
 
 def place(pieces, rows_of, out):
@@ -408,18 +430,24 @@
         def row_of(part, hi, lo):
             return lambda: block_of(n_hi - hi, n_lo - lo) * rows + part * part_rows
 
-        gs = [grad_out] + [turn(grad_out, "dp", n_dp, p) for p in range(1, n_dp)]
+        gs = [turn(grad_out, "dp", n_dp, p) for p in range(1, n_dp)]
         far_group = [(hi, lo) for hi in his for lo in los]
         near_group = [(0, lo) for lo in los] + [(hi, 0) for hi in his] + [(0, 0)]
-        keys = [(p, at) for at in far_group + near_group for p in range(1, n_dp)]
-        held, sent = load(hidden, [start_of(p, *at) for p, at in keys], rows)
         blocks = {at: [] for at in far_group + near_group}
-        for (p, at), block in zip(keys, sent):
-            blocks[at].append(turn(block, "dp", n_dp, p))
+        for group in (far_group, near_group):
+            keys = [(p, at) for at in group for p in range(1, n_dp)]
+            starts = [start_of(p, *at) for p, at in keys]
+            if group is far_group:
+                sent, grad_out = fetch(hidden, grad_out, starts, rows)
+            else:
+                sent = cut(hidden, starts, rows)
+            for (p, at), block in zip(keys, sent):
+                blocks[at].append(turn(block, "dp", n_dp, p))
+        gs = [grad_out] + gs
 
         far = [{}, {}]
         for hi, lo in far_group:
-            bases = product(held, start_of(0, hi, lo), rows, [], gs[:1], (False, False))
+            bases = product(hidden, start_of(0, hi, lo), rows, [], gs[:1], (False, False))
             if n_dp > 1:
                 coded = product(None, None, rows, blocks[hi, lo], gs[1:], (True, True), bases)
             else:
@@ -429,7 +457,7 @@
 
         def whole_product(hi, lo, coded):
             peers = blocks[hi, lo]
-            return product(held, start_of(0, hi, lo), rows, peers, gs, coded, light=True)
+            return product(hidden, start_of(0, hi, lo), rows, peers, gs, coded, light=True)
 
         near, base = [{}, {}], [{}, {}]
         for lo in los:
@@ -447,21 +475,29 @@
             message = relay(base[1][lo], [far[1][hi, lo] for hi in his])
             last[1][lo] = shift(message, lo=lo)
         own = [gather(own[part], list(near[part].values())) for part in (0, 1)]
-        grads, row_part, col_part = final(own, list(last[0].values()), list(last[1].values()))
+        low, row_part, low_col = final(own[0], list(last[0].values()))
+        high, row_part, high_col = final(own[1], list(last[1].values()), [row_part])
 
         chunks = row_part.shape
         parts = exchange([row_part], "tensor", n_tensor)
         new_rows, by_row, both = call(
             functools.partial(rows_kernel, len(parts), all_cols),
             [shape_of(*chunks), shape_of(*chunks), shape_of(2, cols)],
-            grads,
+            low,
+            high,
             row_prev.reshape(chunks),
-            col_part,
+            low_col,
+            high_col,
             *parts,
         )
         parts = exchange([both], "dp", n_dp)
-        parts = exchange(parts, None, n_lo, lambda x, d: shift(x, lo=d))
-        parts = exchange(parts, None, n_hi, lambda x, d: shift(x, hi=d))
+        x = sum(parts[1:], parts[0])
+        if n_hi * n_lo <= 4:
+            steps = [(hi, lo) for hi in range(n_hi) for lo in range(n_lo) if hi or lo]
+            parts = [x] + [shift(x, hi=hi, lo=lo) for hi, lo in steps]
+        else:
+            parts = exchange([x], None, n_lo, lambda x, d: shift(x, lo=d))
+            parts = exchange(parts, None, n_hi, lambda x, d: shift(x, hi=d))
         new_cols, by_col, share = call(
             functools.partial(cols_kernel, len(parts), all_rows),
             [shape_of(1, cols), shape_of(1, cols), shape_of(1, 128)],
@@ -474,7 +510,8 @@
         pair = call(
             functools.partial(fresh_kernel, len(parts), elements),
             [shape_of(part_rows, cols, dtype=jnp.bfloat16)] * 2,
-            grads,
+            low,
+            high,
             master_weight,
             by_row,
             by_col,
@@ -498,7 +535,8 @@
         update = call(
             functools.partial(update_kernel, len(parts), elements),
             shape_of(rows, cols),
-            after(grads, *along_lo.values()),
+            after(low, *along_lo.values()),
+            high,
             by_row,
             by_col,
             *parts,
@@ -508,7 +546,7 @@
         new_weight = place(pair, [row_of(part, 0, 0) for part in (0, 1)], whole)
         pieces = [(x, row_of(part, 0, lo)) for (part, lo), x in along_lo.items()]
         pieces += [(x, row_of(part, hi, 0)) for (part, hi), x in along_hi.items()]
-        for group in (pieces, onward):
+        for group in [pieces, onward]:
             if group:
                 new_weight = place([x for x, _ in group], [f for _, f in group], new_weight)
         return (new_weight, update, new_rows.reshape(rows), new_cols.reshape(cols))

time: 164 us -> 163 us (level)
  waiting for transfers between devices: 107 us -> 104 us
  local copies, waits for them, and re-layouts: 0.02 us -> 1.89 us
  Pallas kernels: 30.1 us -> 28.3 us
    ppermute x14 -> x15, waiting for transfers between devices: 93 us -> 91.1 us  [shift(): return lax.ppermute(x, 'seq', pairs)]
    unnamed x8, local copies, waits for them, and re-layouts: 0.02 us -> 1.89 us
    pallas_call x18 -> x20, Pallas kernels: 30.1 us -> 28.3 us  [call(): pl.pallas_call(kernel, out_shape=out_shape, in_specs=specs or [NEAR] * le...]
    ppermute x14 -> x15, starting transfers between devices: 15.4 us -> 17.1 us  [shift(): return lax.ppermute(x, 'seq', pairs)]
  transfers between devices with their start and end apart: 24 -> 25, of which waited for: 18 -> 18; matrix products, arithmetic and copies ran while one was open for 0% -> 0% of each run, Pallas kernels for 14% -> 13%
where the time goes in v3:
time: 163 us; the launch traced here: 162 us
  waiting for transfers between devices  104 us (64%)
  Pallas kernels  28.3 us (17%)
  starting transfers between devices  26.7 us (16%)
  local copies, waits for them, and re-layouts  1.89 us (1%)
    ppermute x15, waiting for transfers between devices, shift(): return lax.ppermute(x, 'seq', pairs)  91.1 us
    pallas_call x20, Pallas kernels, call(): pl.pallas_call(kernel, out_shape=out_shape, in_specs=specs or [NEAR] * le...  28.3 us
    ppermute x15, starting transfers between devices, shift(): return lax.ppermute(x, 'seq', pairs)  17.1 us
    ppermute x5, waiting for transfers between devices, exchange(): parts = [x, lax.ppermute(x, axis, [(a, a ^ d) for a in range(n)])]  8.92 us
    ppermute x5, starting transfers between devices, exchange(): parts = [x, lax.ppermute(x, axis, [(a, a ^ d) for a in range(n)])]  8.4 us
    ppermute x5, waiting for transfers between devices, turn(): return lax.ppermute(x, axis, [(a, (a + step) % n) for a in range(n)])  4.44 us
  transfers between devices with their start and end apart: 25, of which 18 were waited for; matrix products, arithmetic and copies ran while one was open for 0% of the time, Pallas kernels for 13%

profile of v3, /device:TPU:0, one launch (start us, length us, event | category | flops | bytes accessed | tf_op | source)
XLA Modules:
  0.0 162.4 jit_solution(7548897040095007439)
XLA Ops:
  3.0 1.9 %copy-done = bf16[512,7168]{1,0:T(8,128)(2,1)S(1)} copy-done((bf16[512,7168]{1,0:T(8,128)(2,1)S(1)}, bf16[512,7168]{1,0:T(8,128)(2,1)}, u32[]{:S(2)}) %copy-start) | copy-done | bytes 7340056
  6.0 2.2 %shard_map.91 = (bf16[912,512]{1,0:T(8,128)(2,1)S(1)}, bf16[912,512]{1,0:T(8,128)(2,1)S(1)}) custom-call(bf16[512,896]{1,0:T(8,128)(2,1)S(1)} %collective-permute-done.5.refs_0_, bf16[512,1024]{1,0:T(8,128)(2,1)S(1)} %collective-permute-done.1.refs_3_.refs_1_, f32[896,512]{1,0:T(8,128)S(1)} %get-tuple-element.42.refs_2_, ...), custom_call_target="tpu_custom_call" | custom-call | flops 939524096 | bytes 6586368 | tf_op jit(solution)/shard_map/pallas_call | solution.py:271
  8.2 2.6 %collective-permute-start.6 = (bf16[912,512]{1,0:T(8,128)(2,1)S(1)}, bf16[912,512]{1,0:T(8,128)(2,1)S(1)}, u32[]{:S(2)}, u32[]{:S(2)}) collective-permute-start(bf16[912,512]{1,0:T(8,128)(2,1)S(1)} %get-tuple-element.44), channel_id=1, source_target_pairs={{0,4},{4,0},{8,12},{12,8},{1,5},{5,1},{9,13},{13,9},{2,6},{6,2},{1... | collective-permute-start | bytes 2801672 | tf_op jit(solution)/shard_map/ppermute | solution.py:395
  13.1 2.0 %collective-permute-done.2.refs_1_ = bf16[512,896]{1,0:T(8,128)(2,1)S(1)} collective-permute-done((bf16[512,896]{1,0:T(8,128)(2,1)S(1)}, bf16[512,896]{1,0:T(8,128)(2,1)S(1)}, u32[]{:S(2)}, u32[]{:S(2)}) %collective-permute-start.2) | collective-permute-done | bytes 917536 | tf_op jit(solution)/shard_map/ppermute | solution.py:398
  15.1 2.6 %shard_map.87 = (bf16[912,512]{1,0:T(8,128)(2,1)S(1)}, f32[896,512]{1,0:T(8,128)S(1)}) custom-call(bf16[512,7168]{1,0:T(8,128)(2,1)S(1)} %copy-done, bf16[512,896]{1,0:T(8,128)(2,1)S(1)} %collective-permute-done.2.refs_1_, bf16[512,1024]{1,0:T(8,128)(2,1)S(1)} %get-tuple-element.35.refs_2_.refs_1_, bf16[512,1024]{1,0:T(8,128)(2,1)S(1)} %collective-permute-done.1.refs_3_.refs_1_), custom_call_target="tpu_custom_call" | custom-call | bytes 1 | tf_op jit(solution)/shard_map/pallas_call | solution.py:271
  18.3 2.6 %shard_map.89 = (f32[896,512]{1,0:T(8,128)S(1)}, bf16[912,512]{1,0:T(8,128)(2,1)S(1)}) custom-call(bf16[512,7168]{1,0:T(8,128)(2,1)S(1)} %copy-done, bf16[512,896]{1,0:T(8,128)(2,1)S(1)} %collective-permute-done.4.refs_1_, bf16[512,1024]{1,0:T(8,128)(2,1)S(1)} %get-tuple-element.35.refs_2_.refs_1_, bf16[512,1024]{1,0:T(8,128)(2,1)S(1)} %collective-permute-done.1.refs_3_.refs_1_), custom_call_target="tpu_custom_call" | custom-call | bytes 1 | tf_op jit(solution)/shard_map/pallas_call | solution.py:271
  21.0 11.3 %collective-permute-done.6.refs_0_ = bf16[912,512]{1,0:T(8,128)(2,1)S(1)} collective-permute-done((bf16[912,512]{1,0:T(8,128)(2,1)S(1)}, bf16[912,512]{1,0:T(8,128)(2,1)S(1)}, u32[]{:S(2)}, u32[]{:S(2)}) %collective-permute-start.6) | collective-permute-done | bytes 933920 | tf_op jit(solution)/shard_map/ppermute | solution.py:395
  33.8 2.0 %collective-permute-start.7 = (bf16[912,512]{1,0:T(8,128)(2,1)S(1)}, bf16[912,512]{1,0:T(8,128)(2,1)S(1)}, u32[]{:S(2)}, u32[]{:S(2)}) collective-permute-start(bf16[912,512]{1,0:T(8,128)(2,1)S(1)} %shard_map.92), channel_id=1, source_target_pairs={{0,8},{4,12},{8,0},{12,4},{1,9},{5,13},{9,1},{13,5},{2,10},{6,14},... | collective-permute-start | bytes 2801672 | tf_op jit(solution)/shard_map/ppermute | solution.py:395
  39.1 2.5 %collective-permute-done.refs_1_ = bf16[512,896]{1,0:T(8,128)(2,1)S(1)} collective-permute-done((bf16[512,896]{1,0:T(8,128)(2,1)S(1)}, bf16[512,896]{1,0:T(8,128)(2,1)S(1)}, u32[]{:S(2)}, u32[]{:S(2)}) %collective-permute-start) | collective-permute-done | bytes 917536 | tf_op jit(solution)/shard_map/ppermute | solution.py:398
  41.5 2.1 %shard_map.86 = (f32[896,512]{1,0:T(8,128)S(1)}, f32[896,512]{1,0:T(8,128)S(1)}) custom-call(bf16[512,7168]{1,0:T(8,128)(2,1)S(1)} %copy-done, bf16[512,896]{1,0:T(8,128)(2,1)S(1)} %collective-permute-done.refs_1_, bf16[512,1024]{1,0:T(8,128)(2,1)S(1)} %get-tuple-element.35.refs_2_.refs_1_, bf16[512,1024]{1,0:T(8,128)(2,1)S(1)} %collective-permute-done.1.refs_3_.refs_1_), custom_call_target="tpu_custom_call" | custom-call | bytes 1 | tf_op jit(solution)/shard_map/pallas_call | solution.py:271
  43.7 8.7 %collective-permute-done.3.refs_0_ = bf16[912,512]{1,0:T(8,128)(2,1)S(1)} collective-permute-done((bf16[912,512]{1,0:T(8,128)(2,1)S(1)}, bf16[912,512]{1,0:T(8,128)(2,1)S(1)}, u32[]{:S(2)}, u32[]{:S(2)}) %collective-permute-start.3) | collective-permute-done | bytes 933920 | tf_op jit(solution)/shard_map/ppermute | solution.py:395
  55.2 18.4 %collective-permute-done.7.refs_0_ = bf16[912,512]{1,0:T(8,128)(2,1)S(1)} collective-permute-done((bf16[912,512]{1,0:T(8,128)(2,1)S(1)}, bf16[912,512]{1,0:T(8,128)(2,1)S(1)}, u32[]{:S(2)}, u32[]{:S(2)}) %collective-permute-start.7) | collective-permute-done | bytes 933920 | tf_op jit(solution)/shard_map/ppermute | solution.py:395
  77.7 2.0 %collective-permute-done.11 = f32[7,128]{1,0:T(8,128)S(1)} collective-permute-done((f32[7,128]{1,0:T(8,128)S(1)}, f32[7,128]{1,0:T(8,128)S(1)}, u32[]{:S(2)}, u32[]{:S(2)}) %collective-permute-start.11) | collective-permute-done | bytes 3616 | tf_op jit(solution)/shard_map/ppermute | solution.py:406
  79.8 2.6 %collective-permute-start.12 = (f32[7,128]{1,0:T(8,128)S(1)}, f32[7,128]{1,0:T(8,128)S(1)}, u32[]{:S(2)}, u32[]{:S(2)}) collective-permute-start(f32[7,128]{1,0:T(8,128)S(1)} %add.9.refs_0_), channel_id=1, source_target_pairs={{0,2},{1,3},{2,0},{3,1},{4,6},{5,7},{6,4},{7,5},{8,10},{9,11},{10,... | collective-permute-start | bytes 10760 | tf_op jit(solution)/shard_map/ppermute | solution.py:406
  82.3 1.9 %collective-permute-done.12.refs_1_ = f32[7,128]{1,0:T(8,128)S(1)} collective-permute-done((f32[7,128]{1,0:T(8,128)S(1)}, f32[7,128]{1,0:T(8,128)S(1)}, u32[]{:S(2)}, u32[]{:S(2)}) %collective-permute-start.12) | collective-permute-done | bytes 3616 | tf_op jit(solution)/shard_map/ppermute | solution.py:406
  90.1 2.6 %collective-permute-done.16.refs_3_ = f32[2,1024]{1,0:T(2,128)S(1)} collective-permute-done((f32[2,1024]{1,0:T(2,128)S(1)}, f32[2,1024]{1,0:T(2,128)S(1)}, u32[]{:S(2)}, u32[]{:S(2)}) %collective-permute-start.16) | collective-permute-done | bytes 8224 | tf_op jit(solution)/shard_map/ppermute | solution.py:395
  94.8 2.0 %collective-permute-done.17 = f32[1,128]{1,0:T(1,128)S(1)} collective-permute-done((f32[1,128]{1,0:T(1,128)S(1)}, f32[1,128]{1,0:T(1,128)S(1)}, u32[]{:S(2)}, u32[]{:S(2)}) %collective-permute-start.17) | collective-permute-done | bytes 544 | tf_op jit(solution)/shard_map/ppermute | solution.py:406
  96.8 2.6 %collective-permute-start.18 = (f32[1,128]{1,0:T(1,128)S(1)}, f32[1,128]{1,0:T(1,128)S(1)}, u32[]{:S(2)}, u32[]{:S(2)}) collective-permute-start(f32[1,128]{1,0:T(1,128)S(1)} %add.11.refs_0_), channel_id=1, source_target_pairs={{0,2},{1,3},{2,0},{3,1},{4,6},{5,7},{6,4},{7,5},{8,10},{9,11},{10,... | collective-permute-start | bytes 1544 | tf_op jit(solution)/shard_map/ppermute | solution.py:406
  99.4 1.8 %collective-permute-done.18.refs_1_ = f32[1,128]{1,0:T(1,128)S(1)} collective-permute-done((f32[1,128]{1,0:T(1,128)S(1)}, f32[1,128]{1,0:T(1,128)S(1)}, u32[]{:S(2)}, u32[]{:S(2)}) %collective-permute-start.18) | collective-permute-done | bytes 544 | tf_op jit(solution)/shard_map/ppermute | solution.py:406
  106.1 19.2 %collective-permute-done.19.refs_0_ = bf16[448,1024]{1,0:T(8,128)(2,1)S(1)} collective-permute-done((bf16[448,1024]{1,0:T(8,128)(2,1)S(1)}, bf16[448,1024]{1,0:T(8,128)(2,1)S(1)}, u32[]{:S(2)}, u32[]{:S(2)}) %collective-permute-start.19) | collective-permute-done | bytes 917536 | tf_op jit(solution)/shard_map/ppermute | solution.py:395
  128.6 16.4 %collective-permute-done.23.refs_1_ = bf16[448,1024]{1,0:T(8,128)(2,1)S(1)} collective-permute-done((bf16[448,1024]{1,0:T(8,128)(2,1)S(1)}, bf16[448,1024]{1,0:T(8,128)(2,1)S(1)}, u32[]{:S(2)}, u32[]{:S(2)}) %collective-permute-start.23) | collective-permute-done | bytes 917536 | tf_op jit(solution)/shard_map/ppermute | solution.py:395
  145.0 2.3 %shard_map.103 = f32[896,1024]{1,0:T(8,128)} custom-call(f32[896,512]{1,0:T(8,128)S(1)} %get-tuple-element.61.low, f32[896,512]{1,0:T(8,128)S(1)} %get-tuple-element.51.high, f32[7,128]{1,0:T(8,128)S(1)} %get-tuple-element.55.row_factor, f32[1,1024]{1,0:T(1,128)S(1)} %get-tuple-element.57.col_factor, f32[1,128]{1,0:T(1,128)S(1)} %add.11.refs_0_, ...), custom_call_target="tpu_custom_call" | custom-call | bytes 7348736 | tf_op jit(solution)/shard_map/pallas_call | solution.py:271
  147.3 1.9 %shard_map.101.refs_2_ = bf16[3584,1024]{1,0:T(8,128)(2,1)} custom-call(bf16[448,1024]{1,0:T(8,128)(2,1)S(1)} %collective-permute-done.19.refs_0_, bf16[448,1024]{1,0:T(8,128)(2,1)S(1)} %collective-permute-done.23.refs_1_, bf16[448,1024]{1,0:T(8,128)(2,1)S(1)} %collective-permute-done.21.refs_2_, ...), custom_call_target="tpu_custom_call", output_to_operand_aliasing={{}: (4, {})} | custom-call | bytes 7340032 | tf_op jit(solution)/shard_map/pallas_call | solution.py:271
  149.2 11.8 %collective-permute-done.20.refs_0_ = bf16[448,1024]{1,0:T(8,128)(2,1)S(1)} collective-permute-done((bf16[448,1024]{1,0:T(8,128)(2,1)S(1)}, bf16[448,1024]{1,0:T(8,128)(2,1)S(1)}, u32[]{:S(2)}, u32[]{:S(2)}) %collective-permute-start.20) | collective-permute-done | bytes 917536 | tf_op jit(solution)/shard_map/ppermute | solution.py:395
  (57 shorter events, 35.5 us)
Async XLA Ops:
  0.6 5.4 %collective-permute-start.1 = (bf16[512,1024]{1,0:T(8,128)(2,1)}, bf16[512,1024]{1,0:T(8,128)(2,1)S(1)}, u32[]{:S(2)}, u32[]{:S(2)}) collective-permute-start(bf16[512,1024]{1,0:T(8,128)(2,1)} %grad_out.1), channel_id=1, source_target_pairs={{0,16},{16,0},{1,17},{17,1},{2,18},{18,2},{3,19},{19,3},{4,20},{20... | collective-permute-start | bytes 3145736 | tf_op jit(solution)/shard_map/ppermute | solution.py:398
  2.8 3.2 %collective-permute-start.5 = (bf16[512,896]{1,0:T(8,128)(2,1)S(1)}, bf16[512,896]{1,0:T(8,128)(2,1)S(1)}, u32[]{:S(2)}, u32[]{:S(2)}) collective-permute-start(bf16[512,896]{1,0:T(8,128)(2,1)S(1)} %get-tuple-element.41), channel_id=1, source_target_pairs={{0,16},{16,0},{1,17},{17,1},{2,18},{18,2},{3,19},{19,3},{4,20},{20... | collective-permute-start | bytes 2752520 | tf_op jit(solution)/shard_map/ppermute | solution.py:398
  8.2 24.1 %collective-permute-start.6 = (bf16[912,512]{1,0:T(8,128)(2,1)S(1)}, bf16[912,512]{1,0:T(8,128)(2,1)S(1)}, u32[]{:S(2)}, u32[]{:S(2)}) collective-permute-start(bf16[912,512]{1,0:T(8,128)(2,1)S(1)} %get-tuple-element.44), channel_id=1, source_target_pairs={{0,4},{4,0},{8,12},{12,8},{1,5},{5,1},{9,13},{13,9},{2,6},{6,2},{1... | collective-permute-start | bytes 2801672 | tf_op jit(solution)/shard_map/ppermute | solution.py:395
  10.8 25.1 %collective-permute-start.9 = (bf16[912,512]{1,0:T(8,128)(2,1)S(1)}, bf16[912,512]{1,0:T(8,128)(2,1)S(1)}, u32[]{:S(2)}, u32[]{:S(2)}) collective-permute-start(bf16[912,512]{1,0:T(8,128)(2,1)S(1)} %get-tuple-element.49), channel_id=1, source_target_pairs={{0,8},{4,12},{8,0},{12,4},{1,9},{5,13},{9,1},{13,5},{2,10},{6,14},... | collective-permute-start | bytes 2801672 | tf_op jit(solution)/shard_map/ppermute | solution.py:395
  12.5 2.5 %collective-permute-start.2 = (bf16[512,896]{1,0:T(8,128)(2,1)S(1)}, bf16[512,896]{1,0:T(8,128)(2,1)S(1)}, u32[]{:S(2)}, u32[]{:S(2)}) collective-permute-start(bf16[512,896]{1,0:T(8,128)(2,1)S(1)} %get-tuple-element.37), channel_id=1, source_target_pairs={{0,16},{16,0},{1,17},{17,1},{2,18},{18,2},{3,19},{19,3},{4,20},{20... | collective-permute-start | bytes 2752520 | tf_op jit(solution)/shard_map/ppermute | solution.py:398
  12.6 5.7 %collective-permute-start.4 = (bf16[512,896]{1,0:T(8,128)(2,1)S(1)}, bf16[512,896]{1,0:T(8,128)(2,1)S(1)}, u32[]{:S(2)}, u32[]{:S(2)}) collective-permute-start(bf16[512,896]{1,0:T(8,128)(2,1)S(1)} %get-tuple-element.39), channel_id=1, source_target_pairs={{0,16},{16,0},{1,17},{17,1},{2,18},{18,2},{3,19},{19,3},{4,20},{20... | collective-permute-start | bytes 2752520 | tf_op jit(solution)/shard_map/ppermute | solution.py:398
  17.7 34.6 %collective-permute-start.3 = (bf16[912,512]{1,0:T(8,128)(2,1)S(1)}, bf16[912,512]{1,0:T(8,128)(2,1)S(1)}, u32[]{:S(2)}, u32[]{:S(2)}) collective-permute-start(bf16[912,512]{1,0:T(8,128)(2,1)S(1)} %get-tuple-element.38), channel_id=1, source_target_pairs={{0,4},{4,0},{8,12},{12,8},{1,5},{5,1},{9,13},{13,9},{2,6},{6,2},{1... | collective-permute-start | bytes 2801672 | tf_op jit(solution)/shard_map/ppermute | solution.py:395
  20.9 33.4 %collective-permute-start.8 = (bf16[912,512]{1,0:T(8,128)(2,1)S(1)}, bf16[912,512]{1,0:T(8,128)(2,1)S(1)}, u32[]{:S(2)}, u32[]{:S(2)}) collective-permute-start(bf16[912,512]{1,0:T(8,128)(2,1)S(1)} %get-tuple-element.47), channel_id=1, source_target_pairs={{0,8},{4,12},{8,0},{12,4},{1,9},{5,13},{9,1},{13,5},{2,10},{6,14},... | collective-permute-start | bytes 2801672 | tf_op jit(solution)/shard_map/ppermute | solution.py:395
  33.8 39.8 %collective-permute-start.7 = (bf16[912,512]{1,0:T(8,128)(2,1)S(1)}, bf16[912,512]{1,0:T(8,128)(2,1)S(1)}, u32[]{:S(2)}, u32[]{:S(2)}) collective-permute-start(bf16[912,512]{1,0:T(8,128)(2,1)S(1)} %shard_map.92), channel_id=1, source_target_pairs={{0,8},{4,12},{8,0},{12,4},{1,9},{5,13},{9,1},{13,5},{2,10},{6,14},... | collective-permute-start | bytes 2801672 | tf_op jit(solution)/shard_map/ppermute | solution.py:395
  37.3 37.6 %collective-permute-start.10 = (bf16[912,512]{1,0:T(8,128)(2,1)S(1)}, bf16[912,512]{1,0:T(8,128)(2,1)S(1)}, u32[]{:S(2)}, u32[]{:S(2)}) collective-permute-start(bf16[912,512]{1,0:T(8,128)(2,1)S(1)} %shard_map.95), channel_id=1, source_target_pairs={{0,4},{4,0},{8,12},{12,8},{1,5},{5,1},{9,13},{13,9},{2,6},{6,2},{1... | collective-permute-start | bytes 2801672 | tf_op jit(solution)/shard_map/ppermute | solution.py:395
  39.1 2.5 %collective-permute-start = (bf16[512,896]{1,0:T(8,128)(2,1)S(1)}, bf16[512,896]{1,0:T(8,128)(2,1)S(1)}, u32[]{:S(2)}, u32[]{:S(2)}) collective-permute-start(bf16[512,896]{1,0:T(8,128)(2,1)S(1)} %get-tuple-element.34), channel_id=1, source_target_pairs={{0,16},{16,0},{1,17},{17,1},{2,18},{18,2},{3,19},{19,3},{4,20},{20... | collective-permute-start | bytes 2752520 | tf_op jit(solution)/shard_map/ppermute | solution.py:398
  76.1 3.7 %collective-permute-start.11 = (f32[7,128]{1,0:T(8,128)S(1)}, f32[7,128]{1,0:T(8,128)S(1)}, u32[]{:S(2)}, u32[]{:S(2)}) collective-permute-start(f32[7,128]{1,0:T(8,128)S(1)} %get-tuple-element.54), channel_id=1, source_target_pairs={{0,1},{1,0},{2,3},{3,2},{4,5},{5,4},{6,7},{7,6},{8,9},{9,8},{10,11... | collective-permute-start | bytes 10760 | tf_op jit(solution)/shard_map/ppermute | solution.py:406
  79.8 4.5 %collective-permute-start.12 = (f32[7,128]{1,0:T(8,128)S(1)}, f32[7,128]{1,0:T(8,128)S(1)}, u32[]{:S(2)}, u32[]{:S(2)}) collective-permute-start(f32[7,128]{1,0:T(8,128)S(1)} %add.9.refs_0_), channel_id=1, source_target_pairs={{0,2},{1,3},{2,0},{3,1},{4,6},{5,7},{6,4},{7,5},{8,10},{9,11},{10,... | collective-permute-start | bytes 10760 | tf_op jit(solution)/shard_map/ppermute | solution.py:406
  86.0 3.7 %collective-permute-start.14 = (f32[2,1024]{1,0:T(2,128)S(1)}, f32[2,1024]{1,0:T(2,128)S(1)}, u32[]{:S(2)}, u32[]{:S(2)}) collective-permute-start(f32[2,1024]{1,0:T(2,128)S(1)} %add.10.refs_0_), channel_id=1, source_target_pairs={{0,4},{4,0},{8,12},{12,8},{1,5},{5,1},{9,13},{13,9},{2,6},{6,2},{1... | collective-permute-start | bytes 24584 | tf_op jit(solution)/shard_map/ppermute | solution.py:395
  86.4 3.7 %collective-permute-start.15 = (f32[2,1024]{1,0:T(2,128)S(1)}, f32[2,1024]{1,0:T(2,128)S(1)}, u32[]{:S(2)}, u32[]{:S(2)}) collective-permute-start(f32[2,1024]{1,0:T(2,128)S(1)} %add.10.refs_0_), channel_id=1, source_target_pairs={{0,8},{4,12},{8,0},{12,4},{1,9},{5,13},{9,1},{13,5},{2,10},{6,14},... | collective-permute-start | bytes 24584 | tf_op jit(solution)/shard_map/ppermute | solution.py:395
  88.1 4.5 %collective-permute-start.16 = (f32[2,1024]{1,0:T(2,128)S(1)}, f32[2,1024]{1,0:T(2,128)S(1)}, u32[]{:S(2)}, u32[]{:S(2)}) collective-permute-start(f32[2,1024]{1,0:T(2,128)S(1)} %add.10.refs_0_), channel_id=1, source_target_pairs={{0,12},{4,8},{8,4},{12,0},{1,13},{5,9},{9,5},{13,1},{2,14},{6,10},... | collective-permute-start | bytes 24584 | tf_op jit(solution)/shard_map/ppermute | solution.py:395
  93.3 3.5 %collective-permute-start.17 = (f32[1,128]{1,0:T(1,128)S(1)}, f32[1,128]{1,0:T(1,128)S(1)}, u32[]{:S(2)}, u32[]{:S(2)}) collective-permute-start(f32[1,128]{1,0:T(1,128)S(1)} %get-tuple-element.58), channel_id=1, source_target_pairs={{0,1},{1,0},{2,3},{3,2},{4,5},{5,4},{6,7},{7,6},{8,9},{9,8},{10,11... | collective-permute-start | bytes 1544 | tf_op jit(solution)/shard_map/ppermute | solution.py:406
  96.8 4.4 %collective-permute-start.18 = (f32[1,128]{1,0:T(1,128)S(1)}, f32[1,128]{1,0:T(1,128)S(1)}, u32[]{:S(2)}, u32[]{:S(2)}) collective-permute-start(f32[1,128]{1,0:T(1,128)S(1)} %add.11.refs_0_), channel_id=1, source_target_pairs={{0,2},{1,3},{2,0},{3,1},{4,6},{5,7},{6,4},{7,5},{8,10},{9,11},{10,... | collective-permute-start | bytes 1544 | tf_op jit(solution)/shard_map/ppermute | solution.py:406
  102.0 23.4 %collective-permute-start.19 = (bf16[448,1024]{1,0:T(8,128)(2,1)S(1)}, bf16[448,1024]{1,0:T(8,128)(2,1)S(1)}, u32[]{:S(2)}, u32[]{:S(2)}) collective-permute-start(bf16[448,1024]{1,0:T(8,128)(2,1)S(1)} %get-tuple-element.59.refs_0_), channel_id=1, source_target_pairs={{0,4},{4,0},{8,12},{12,8},{1,5},{5,1},{9,13},{13,9},{2,6},{6,2},{1... | collective-permute-start | bytes 2752520 | tf_op jit(solution)/shard_map/ppermute | solution.py:395
  103.5 23.3 %collective-permute-start.21 = (bf16[448,1024]{1,0:T(8,128)(2,1)S(1)}, bf16[448,1024]{1,0:T(8,128)(2,1)S(1)}, u32[]{:S(2)}, u32[]{:S(2)}) collective-permute-start(bf16[448,1024]{1,0:T(8,128)(2,1)S(1)} %get-tuple-element.60.refs_1_), channel_id=1, source_target_pairs={{0,8},{4,12},{8,0},{12,4},{1,9},{5,13},{9,1},{13,5},{2,10},{6,14},... | collective-permute-start | bytes 2752520 | tf_op jit(solution)/shard_map/ppermute | solution.py:395
  104.1 40.9 %collective-permute-start.23 = (bf16[448,1024]{1,0:T(8,128)(2,1)S(1)}, bf16[448,1024]{1,0:T(8,128)(2,1)S(1)}, u32[]{:S(2)}, u32[]{:S(2)}) collective-permute-start(bf16[448,1024]{1,0:T(8,128)(2,1)S(1)} %get-tuple-element.60.refs_1_), channel_id=1, source_target_pairs={{0,4},{4,0},{8,12},{12,8},{1,5},{5,1},{9,13},{13,9},{2,6},{6,2},{1... | collective-permute-start | bytes 2752520 | tf_op jit(solution)/shard_map/ppermute | solution.py:395
  104.4 42.9 %collective-permute-start.24 = (bf16[448,1024]{1,0:T(8,128)(2,1)S(1)}, bf16[448,1024]{1,0:T(8,128)(2,1)S(1)}, u32[]{:S(2)}, u32[]{:S(2)}) collective-permute-start(bf16[448,1024]{1,0:T(8,128)(2,1)S(1)} %get-tuple-element.59.refs_0_), channel_id=1, source_target_pairs={{0,8},{4,12},{8,0},{12,4},{1,9},{5,13},{9,1},{13,5},{2,10},{6,14},... | collective-permute-start | bytes 2752520 | tf_op jit(solution)/shard_map/ppermute | solution.py:395
  125.4 35.6 %collective-permute-start.20 = (bf16[448,1024]{1,0:T(8,128)(2,1)S(1)}, bf16[448,1024]{1,0:T(8,128)(2,1)S(1)}, u32[]{:S(2)}, u32[]{:S(2)}) collective-permute-start(bf16[448,1024]{1,0:T(8,128)(2,1)S(1)} %collective-permute-done.19.refs_0_), channel_id=1, source_target_pairs={{0,8},{4,12},{8,0},{12,4},{1,9},{5,13},{9,1},{13,5},{2,10},{6,14},... | collective-permute-start | bytes 2752520 | tf_op jit(solution)/shard_map/ppermute | solution.py:395
  126.8 34.2 %collective-permute-start.22 = (bf16[448,1024]{1,0:T(8,128)(2,1)S(1)}, bf16[448,1024]{1,0:T(8,128)(2,1)S(1)}, u32[]{:S(2)}, u32[]{:S(2)}) collective-permute-start(bf16[448,1024]{1,0:T(8,128)(2,1)S(1)} %collective-permute-done.21.refs_2_), channel_id=1, source_target_pairs={{0,4},{4,0},{8,12},{12,8},{1,5},{5,1},{9,13},{13,9},{2,6},{6,2},{1... | collective-permute-start | bytes 2752520 | tf_op jit(solution)/shard_map/ppermute | solution.py:395
  (5 other events, 39.6 us)

commit v4 on v3

--- a/solution.py
+++ b/solution.py
@@ -20,6 +20,12 @@
 
 def chunk_of(rows):
     return 128 if rows % 128 == 0 else rows
+
+
+def groups_of(rows):
+    n = rows // chunk_of(rows)
+    cuts = sorted({0, (n + 1) // 2, n})
+    return [(a * chunk_of(rows), b * chunk_of(rows)) for a, b in zip(cuts, cuts[1:])]
 
 
 def encode(x):
@@ -105,65 +111,64 @@
         out[...] = hidden[:, pl.ds(pl.multiple_of(start_of(), 128), out.shape[1])]
 
 
-def relay_kernel(n, base, *refs):
+def added_up(base, messages, group, begin):
+    chunk = chunk_of(base.shape[0])
+    tails = [read_scales(m) for m in messages]
+    for row in range(*group, chunk):
+        total = base[row : row + chunk]
+        j = (row - begin) // chunk
+        for m, tail in zip(messages, tails):
+            total = total + decode(m[row - begin : row - begin + chunk], tail[j : j + 1])
+        yield slice(row, row + chunk), total
+
+
+def relay_kernel(n, group, base, *refs):
     messages, out = refs[:n], refs[n]
-    rows = base.shape[0]
-    chunk = chunk_of(rows)
-    tails = [read_scales(m) for m in messages]
     scales = []
-    for j in range(rows // chunk):
-        at = slice(j * chunk, (j + 1) * chunk)
-        total = base[at]
-        for m, tail in zip(messages, tails):
-            total = total + decode(m[at], tail[j : j + 1])
-        out[at], scale = encode(total)
+    for at, total in added_up(base, messages, group, 0):
+        out[at.start - group[0] : at.stop - group[0]], scale = encode(total)
         scales.append(scale)
     write_scales(out, scales)
 
 
-def gather_kernel(n, base, *refs):
-    messages, out = refs[:n], refs[n]
-    rows = base.shape[0]
-    chunk = chunk_of(rows)
-    tails = [read_scales(m) for m in messages]
-    for j in range(rows // chunk):
-        at = slice(j * chunk, (j + 1) * chunk)
-        total = base[at]
-        for m, tail in zip(messages, tails):
-            total = total + decode(m[at], tail[j : j + 1])
+def gather_kernel(base, *refs):
+    messages, out = refs[:-1], refs[-1]
+    for at, total in added_up(base, messages, (0, base.shape[0]), 0):
         out[at] = total
 
 
-def final_kernel(n, n_before, base, *refs):
-    messages, refs = refs[:n], refs[n:]
-    before, (out, row_out, col_out) = refs[:n_before], refs[n_before:]
-    rows, half = base.shape
-    chunk = chunk_of(rows)
-    tails = [read_scales(m) for m in messages]
-    col_sum = jnp.zeros((1, half), jnp.float32)
-    for j in range(rows // chunk):
-        at = slice(j * chunk, (j + 1) * chunk)
-        row_sum = jnp.zeros((chunk, 128), jnp.float32)
-        total = base[at]
-        for m, tail in zip(messages, tails):
-            total = total + decode(m[at], tail[j : j + 1])
-        out[at] = total
+def final_kernel(n, group, has_rows, has_cols, base, *refs):
+    refs = list(refs)
+    messages = [refs.pop(0) for _ in range(n)]
+    rows_in = refs.pop(0)[...] if has_rows else None
+    cols_in = refs.pop(0)[...] if has_cols else 0.0
+    out, row_out, col_out = refs
+    chunk, half = chunk_of(base.shape[0]), base.shape[1]
+    row_out[...] = rows_in if has_rows else jnp.zeros(row_out.shape, jnp.float32)
+    col_sum = jnp.zeros((1, half), jnp.float32) + cols_in
+    for at, total in added_up(base, messages, group, group[0]):
+        out[at.start - group[0] : at.stop - group[0]] = total
         squares = total * total
         col_sum = col_sum + jnp.sum(squares, axis=0, keepdims=True)
+        row_sum = jnp.zeros((chunk, 128), jnp.float32)
         for k in range(half // 128):
             row_sum = row_sum + squares[:, k * 128 : (k + 1) * 128]
         row_sum = jnp.sum(row_sum.T, axis=0, keepdims=True)
-        for row in before:
-            row_sum = row_sum + row[j : j + 1]
-        row_out[j : j + 1] = row_sum
+        j = at.start // chunk
+        row_out[j : j + 1] = row_sum + (rows_in[j : j + 1] if has_rows else 0.0)
     col_out[...] = col_sum
 
 
-def columns_of(halves):
-    half = halves[0].shape[1]
-    for part in (0, 1):
-        for k in range(0, half, 128):
-            yield halves[part], slice(k, k + 128), slice(part * half + k, part * half + k + 128)
+def tiles_of(pieces, first, last):
+    half, begin = pieces[0].shape[1], 0
+    for low, high in zip(pieces[::2], pieces[1::2]):
+        end = begin + low.shape[0]
+        if begin <= first < end:
+            for part, ref in enumerate((low, high)):
+                for k in range(0, half, 128):
+                    tile = ref[first - begin : last - begin, k : k + 128]
+                    yield tile, slice(part * half + k, part * half + k + 128)
+        begin = end
 
 
 def as_column(row):
@@ -177,7 +182,9 @@
     return terms[0]
 
 
-def rows_kernel(n, all_cols, low, high, row_prev, low_col, high_col, *refs):
+def rows_kernel(n, n_pieces, all_cols, *refs):
+    pieces, refs = refs[:n_pieces], refs[n_pieces:]
+    (row_prev, low_col, high_col), refs = refs[:3], refs[3:]
     parts, (rows_out, by_row_out, both_out) = refs[:n], refs[n:]
     total = tree_sum([p[...] for p in parts])
     total = total + small_term * all_cols
@@ -186,17 +193,16 @@
     by_row_out[...] = 1.0 / jnp.sqrt(new_rows)
     inverse = 1.0 / new_rows
     n_chunks, chunk = new_rows.shape
-    half = low.shape[1]
+    half = low_col.shape[1]
     sums = [jnp.zeros((1, 128), jnp.float32)] * (2 * half // 128)
     for j in range(n_chunks):
         weight = as_column(inverse[j : j + 1])
-        for k, (grads, at, _) in enumerate(columns_of((low, high))):
-            g = grads[j * chunk : (j + 1) * chunk, at]
+        for k, (g, _) in enumerate(tiles_of(pieces, j * chunk, (j + 1) * chunk)):
             sums[k] = sums[k] + jnp.sum(g * g * weight, axis=0, keepdims=True)
     both_out[0:1, :half] = low_col[...]
     both_out[0:1, half:] = high_col[...]
-    for k, (_, _, there) in enumerate(columns_of((low, high))):
-        both_out[1:2, there] = sums[k]
+    for k, total in enumerate(sums):
+        both_out[1:2, k * 128 : (k + 1) * 128] = total
 
 
 def cols_kernel(n, all_rows, col_prev, *refs):
@@ -218,7 +224,9 @@
     return by_row[...] / clip, by_col[...]
 
 
-def fresh_kernel(n, elements, low, high, weight, row_factor, col_factor, *refs):
+def fresh_kernel(n, n_pieces, elements, *refs):
+    pieces, refs = refs[:n_pieces], refs[n_pieces:]
+    (weight, row_factor, col_factor), refs = refs[:3], refs[3:]
     parts, outs = refs[:n], refs[n:]
     by_row, by_col = factors(elements, parts, row_factor, col_factor)
     n_chunks, chunk = by_row.shape
@@ -226,8 +234,8 @@
     for j in range(n_chunks):
         column = as_column(by_row[j : j + 1])
         first, last = j * chunk, (j + 1) * chunk
-        for grads, here, there in columns_of((low, high)):
-            update = grads[first:last, here] * column * by_col[:, there]
+        for grads, there in tiles_of(pieces, first, last):
+            update = grads * column * by_col[:, there]
             fresh = (weight[first:last, there] - learn_rate * update).astype(jnp.bfloat16)
             if first < split:
                 outs[0][first : min(last, split), there] = fresh[: min(last, split) - first]
@@ -236,15 +244,17 @@
                 outs[1][cut - split : last - split, there] = fresh[cut - first :]
 
 
-def update_kernel(n, elements, low, high, row_factor, col_factor, *refs):
+def update_kernel(n, n_pieces, elements, *refs):
+    pieces, refs = refs[:n_pieces], refs[n_pieces:]
+    (row_factor, col_factor), refs = refs[:2], refs[2:]
     parts, out = refs[:n], refs[n]
     by_row, by_col = factors(elements, parts, row_factor, col_factor)
     n_chunks, chunk = by_row.shape
     for j in range(n_chunks):
         column = as_column(by_row[j : j + 1])
-        for grads, here, there in columns_of((low, high)):
-            at = slice(j * chunk, (j + 1) * chunk)
-            out[at, there] = grads[at, here] * column * by_col[:, there]
+        first, last = j * chunk, (j + 1) * chunk
+        for grads, there in tiles_of(pieces, first, last):
+            out[first:last, there] = grads * column * by_col[:, there]
 
 
 def place_kernel(rows_of, *refs):
@@ -333,25 +343,30 @@
     )
 
 
-def relay(base, messages):
-    rows, half = base.shape
-    shape = shape_of(rows + TAIL, half, dtype=jnp.bfloat16)
-    return call(functools.partial(relay_kernel, len(messages)), shape, base, *messages)
+def relay(base, messages, group):
+    shape = shape_of(group[1] - group[0] + TAIL, base.shape[1], dtype=jnp.bfloat16)
+    return call(functools.partial(relay_kernel, len(messages), group), shape, base, *messages)
 
 
 def gather(base, messages):
     if not messages:
         return base
-    shape = shape_of(*base.shape)
-    return call(functools.partial(gather_kernel, len(messages)), shape, base, *messages)
-
-
-def final(base, messages, before=()):
+    return call(gather_kernel, shape_of(*base.shape), base, *messages)
+
+
+def final(base, messages, group, rows_in, cols_in):
     rows, half = base.shape
     chunk = chunk_of(rows)
-    shapes = [shape_of(rows, half), shape_of(rows // chunk, chunk), shape_of(1, half)]
-    kernel = functools.partial(final_kernel, len(messages), len(before))
-    return call(kernel, shapes, base, *messages, *before)
+    shapes = [
+        shape_of(group[1] - group[0], half),
+        shape_of(rows // chunk, chunk),
+        shape_of(1, half),
+    ]
+    kernel = functools.partial(
+        final_kernel, len(messages), group, rows_in is not None, cols_in is not None
+    )
+    more = [x for x in (rows_in, cols_in) if x is not None]
+    return call(kernel, shapes, base, *messages, *more)
 
 
 def place(pieces, rows_of, out):
@@ -451,7 +466,7 @@
             if n_dp > 1:
                 coded = product(None, None, rows, blocks[hi, lo], gs[1:], (True, True), bases)
             else:
-                coded = [relay(x, []) for x in bases]
+                coded = [relay(x, [], (0, rows)) for x in bases]
             far[0][hi, lo] = shift(coded[0], lo=lo)
             far[1][hi, lo] = shift(coded[1], hi=hi)
 
@@ -467,27 +482,33 @@
             base[0][hi], second = whole_product(hi, 0, (False, True))
             near[1][hi] = shift(second, hi=hi)
         own = whole_product(0, 0, (False, False))
+        groups = groups_of(rows)
         last = [{}, {}]
-        for hi in his:
-            message = relay(base[0][hi], [far[0][hi, lo] for lo in los])
-            last[0][hi] = shift(message, hi=hi)
-        for lo in los:
-            message = relay(base[1][lo], [far[1][hi, lo] for hi in his])
-            last[1][lo] = shift(message, lo=lo)
+        for group in groups:
+            for hi in his:
+                message = relay(base[0][hi], [far[0][hi, lo] for lo in los], group)
+                last[0].setdefault(group, []).append(shift(message, hi=hi))
+            for lo in los:
+                message = relay(base[1][lo], [far[1][hi, lo] for hi in his], group)
+                last[1].setdefault(group, []).append(shift(message, lo=lo))
         own = [gather(own[part], list(near[part].values())) for part in (0, 1)]
-        low, row_part, low_col = final(own[0], list(last[0].values()))
-        high, row_part, high_col = final(own[1], list(last[1].values()), [row_part])
+        grads, row_part, col_part = [], None, [None, None]
+        for group in groups:
+            for part in (0, 1):
+                messages = last[part].get(group, [])
+                piece, row_part, col_part[part] = final(
+                    own[part], messages, group, row_part, col_part[part]
+                )
+                grads.append(piece)
 
         chunks = row_part.shape
         parts = exchange([row_part], "tensor", n_tensor)
         new_rows, by_row, both = call(
-            functools.partial(rows_kernel, len(parts), all_cols),
+            functools.partial(rows_kernel, len(parts), len(grads), all_cols),
             [shape_of(*chunks), shape_of(*chunks), shape_of(2, cols)],
-            low,
-            high,
+            *grads,
             row_prev.reshape(chunks),
-            low_col,
-            high_col,
+            *col_part,
             *parts,
         )
         parts = exchange([both], "dp", n_dp)
@@ -508,10 +529,9 @@
         elements = all_rows * all_cols
 
         pair = call(
-            functools.partial(fresh_kernel, len(parts), elements),
+            functools.partial(fresh_kernel, len(parts), len(grads), elements),
             [shape_of(part_rows, cols, dtype=jnp.bfloat16)] * 2,
-            low,
-            high,
+            *grads,
             master_weight,
             by_row,
             by_col,
@@ -533,10 +553,10 @@
                 onward.append((shift(along_lo[0, lo], hi=hi), row_of(0, hi, lo)))
                 onward.append((shift(along_hi[1, hi], lo=lo), row_of(1, hi, lo)))
         update = call(
-            functools.partial(update_kernel, len(parts), elements),
+            functools.partial(update_kernel, len(parts), len(grads), elements),
             shape_of(rows, cols),
-            after(low, *along_lo.values()),
-            high,
+            after(grads[0], *along_lo.values()),
+            *grads[1:],
             by_row,
             by_col,
             *parts,

time: 163 us -> 162 us (level)
  starting transfers between devices: 26.7 us -> 29.1 us
  waiting for transfers between devices: 104 us -> 102 us
    ppermute x5, waiting for transfers between devices: 4.44 us -> 0.01 us  [turn(): return lax.ppermute(x, axis, [(a, (a + step) % n) for a in range(n)])]
    ppermute x15 -> x17, starting transfers between devices: 17.1 us -> 19.5 us  [shift(): return lax.ppermute(x, 'seq', pairs)]
    ppermute x15 -> x17, waiting for transfers between devices: 91.1 us -> 92.6 us  [shift(): return lax.ppermute(x, 'seq', pairs)]
    pallas_call x20 -> x24, Pallas kernels: 28.3 us -> 28.7 us  [call(): pl.pallas_call(kernel, out_shape=out_shape, in_specs=specs or [NEAR] * le...]
  transfers between devices with their start and end apart: 25 -> 27, of which waited for: 18 -> 16; matrix products, arithmetic and copies ran while one was open for 0% -> 0% of each run, Pallas kernels for 13% -> 15%
where the time goes in v4:
time: 162 us
  waiting for transfers between devices  102 us (63%)
  starting transfers between devices  29.1 us (18%)
  Pallas kernels  28.7 us (18%)
  local copies, waits for them, and re-layouts  1.89 us (1%)
    ppermute x17, waiting for transfers between devices, shift(): return lax.ppermute(x, 'seq', pairs)  92.6 us
    pallas_call x24, Pallas kernels, call(): pl.pallas_call(kernel, out_shape=out_shape, in_specs=specs or [NEAR] * le...  28.7 us
    ppermute x17, starting transfers between devices, shift(): return lax.ppermute(x, 'seq', pairs)  19.5 us
    ppermute x5, waiting for transfers between devices, exchange(): parts = [x, lax.ppermute(x, axis, [(a, a ^ d) for a in range(n)])]  8.92 us
    ppermute x5, starting transfers between devices, exchange(): parts = [x, lax.ppermute(x, axis, [(a, a ^ d) for a in range(n)])]  8.41 us
  transfers between devices with their start and end apart: 27, of which 16 were waited for; matrix products, arithmetic and copies ran while one was open for 0% of the time, Pallas kernels for 15%

profile of v4, /device:TPU:0, one launch (start us, length us, event | category | flops | bytes accessed | tf_op | source)
XLA Modules:
  0.0 162.2 jit_solution(5937109803808910580)
XLA Ops:
  3.0 1.9 %copy-done = bf16[512,7168]{1,0:T(8,128)(2,1)S(1)} copy-done((bf16[512,7168]{1,0:T(8,128)(2,1)S(1)}, bf16[512,7168]{1,0:T(8,128)(2,1)}, u32[]{:S(2)}) %copy-start) | copy-done | bytes 7340056
  6.8 2.2 %shard_map.91 = (bf16[912,512]{1,0:T(8,128)(2,1)S(1)}, bf16[912,512]{1,0:T(8,128)(2,1)S(1)}) custom-call(bf16[512,896]{1,0:T(8,128)(2,1)S(1)} %collective-permute-done.5.refs_0_, bf16[512,1024]{1,0:T(8,128)(2,1)S(1)} %collective-permute-done.1.refs_3_.refs_1_, f32[896,512]{1,0:T(8,128)S(1)} %get-tuple-element.48.refs_2_, ...), custom_call_target="tpu_custom_call" | custom-call | flops 939524096 | bytes 6586368 | tf_op jit(solution)/shard_map/pallas_call | solution.py:281
  9.0 2.6 %collective-permute-start.6 = (bf16[912,512]{1,0:T(8,128)(2,1)S(1)}, bf16[912,512]{1,0:T(8,128)(2,1)S(1)}, u32[]{:S(2)}, u32[]{:S(2)}) collective-permute-start(bf16[912,512]{1,0:T(8,128)(2,1)S(1)} %get-tuple-element.50), channel_id=1, source_target_pairs={{0,4},{4,0},{8,12},{12,8},{1,5},{5,1},{9,13},{13,9},{2,6},{6,2},{1... | collective-permute-start | bytes 2801672 | tf_op jit(solution)/shard_map/ppermute | solution.py:410
  13.2 2.6 %shard_map.87 = (bf16[912,512]{1,0:T(8,128)(2,1)S(1)}, f32[896,512]{1,0:T(8,128)S(1)}) custom-call(bf16[512,7168]{1,0:T(8,128)(2,1)S(1)} %copy-done, bf16[512,896]{1,0:T(8,128)(2,1)S(1)} %collective-permute-done.2.refs_1_, bf16[512,1024]{1,0:T(8,128)(2,1)S(1)} %get-tuple-element.41.refs_2_.refs_1_, bf16[512,1024]{1,0:T(8,128)(2,1)S(1)} %collective-permute-done.1.refs_3_.refs_1_), custom_call_target="tpu_custom_call" | custom-call | bytes 1 | tf_op jit(solution)/shard_map/pallas_call | solution.py:281
  16.4 2.6 %shard_map.89 = (f32[896,512]{1,0:T(8,128)S(1)}, bf16[912,512]{1,0:T(8,128)(2,1)S(1)}) custom-call(bf16[512,7168]{1,0:T(8,128)(2,1)S(1)} %copy-done, bf16[512,896]{1,0:T(8,128)(2,1)S(1)} %collective-permute-done.4.refs_1_, bf16[512,1024]{1,0:T(8,128)(2,1)S(1)} %get-tuple-element.41.refs_2_.refs_1_, bf16[512,1024]{1,0:T(8,128)(2,1)S(1)} %collective-permute-done.1.refs_3_.refs_1_), custom_call_target="tpu_custom_call" | custom-call | bytes 1 | tf_op jit(solution)/shard_map/pallas_call | solution.py:281
  19.2 14.0 %collective-permute-done.6.refs_0_ = bf16[912,512]{1,0:T(8,128)(2,1)S(1)} collective-permute-done((bf16[912,512]{1,0:T(8,128)(2,1)S(1)}, bf16[912,512]{1,0:T(8,128)(2,1)S(1)}, u32[]{:S(2)}, u32[]{:S(2)}) %collective-permute-start.6) | collective-permute-done | bytes 933920 | tf_op jit(solution)/shard_map/ppermute | solution.py:410
  34.0 2.1 %collective-permute-start.7 = (bf16[528,512]{1,0:T(8,128)(2,1)S(1)}, bf16[528,512]{1,0:T(8,128)(2,1)S(1)}, u32[]{:S(2)}, u32[]{:S(2)}) collective-permute-start(bf16[528,512]{1,0:T(8,128)(2,1)S(1)} %shard_map.92), channel_id=1, source_target_pairs={{0,8},{4,12},{8,0},{12,4},{1,9},{5,13},{9,1},{13,5},{2,10},{6,14},... | collective-permute-start | bytes 1622024 | tf_op jit(solution)/shard_map/ppermute | solution.py:410
  40.5 12.7 %collective-permute-done.3.refs_0_ = bf16[912,512]{1,0:T(8,128)(2,1)S(1)} collective-permute-done((bf16[912,512]{1,0:T(8,128)(2,1)S(1)}, bf16[912,512]{1,0:T(8,128)(2,1)S(1)}, u32[]{:S(2)}, u32[]{:S(2)}) %collective-permute-start.3) | collective-permute-done | bytes 933920 | tf_op jit(solution)/shard_map/ppermute | solution.py:410
  53.2 1.9 %collective-permute-start.12 = (bf16[400,512]{1,0:T(8,128)(2,1)S(1)}, bf16[400,512]{1,0:T(8,128)(2,1)S(1)}, u32[]{:S(2)}, u32[]{:S(2)}) collective-permute-start(bf16[400,512]{1,0:T(8,128)(2,1)S(1)} %shard_map.99), channel_id=1, source_target_pairs={{0,4},{4,0},{8,12},{12,8},{1,5},{5,1},{9,13},{13,9},{2,6},{6,2},{1... | collective-permute-start | bytes 1228808 | tf_op jit(solution)/shard_map/ppermute | solution.py:410
  55.1 2.1 %shard_map.86 = (f32[896,512]{1,0:T(8,128)S(1)}, f32[896,512]{1,0:T(8,128)S(1)}) custom-call(bf16[512,7168]{1,0:T(8,128)(2,1)S(1)} %copy-done, bf16[512,896]{1,0:T(8,128)(2,1)S(1)} %collective-permute-done.refs_1_, bf16[512,1024]{1,0:T(8,128)(2,1)S(1)} %get-tuple-element.41.refs_2_.refs_1_, bf16[512,1024]{1,0:T(8,128)(2,1)S(1)} %collective-permute-done.1.refs_3_.refs_1_), custom_call_target="tpu_custom_call" | custom-call | bytes 1 | tf_op jit(solution)/shard_map/pallas_call | solution.py:281
  59.1 7.7 %collective-permute-done.7.refs_0_ = bf16[528,512]{1,0:T(8,128)(2,1)S(1)} collective-permute-done((bf16[528,512]{1,0:T(8,128)(2,1)S(1)}, bf16[528,512]{1,0:T(8,128)(2,1)S(1)}, u32[]{:S(2)}, u32[]{:S(2)}) %collective-permute-start.7) | collective-permute-done | bytes 540704 | tf_op jit(solution)/shard_map/ppermute | solution.py:410
  68.2 6.6 %collective-permute-done.11.refs_0_ = bf16[400,512]{1,0:T(8,128)(2,1)S(1)} collective-permute-done((bf16[400,512]{1,0:T(8,128)(2,1)S(1)}, bf16[400,512]{1,0:T(8,128)(2,1)S(1)}, u32[]{:S(2)}, u32[]{:S(2)}) %collective-permute-start.11) | collective-permute-done | bytes 409632 | tf_op jit(solution)/shard_map/ppermute | solution.py:410
  77.5 2.0 %collective-permute-done.13 = f32[7,128]{1,0:T(8,128)S(1)} collective-permute-done((f32[7,128]{1,0:T(8,128)S(1)}, f32[7,128]{1,0:T(8,128)S(1)}, u32[]{:S(2)}, u32[]{:S(2)}) %collective-permute-start.13) | collective-permute-done | bytes 3616 | tf_op jit(solution)/shard_map/ppermute | solution.py:421
  79.6 2.6 %collective-permute-start.14 = (f32[7,128]{1,0:T(8,128)S(1)}, f32[7,128]{1,0:T(8,128)S(1)}, u32[]{:S(2)}, u32[]{:S(2)}) collective-permute-start(f32[7,128]{1,0:T(8,128)S(1)} %add.9.refs_7_), channel_id=1, source_target_pairs={{0,2},{1,3},{2,0},{3,1},{4,6},{5,7},{6,4},{7,5},{8,10},{9,11},{10,... | collective-permute-start | bytes 10760 | tf_op jit(solution)/shard_map/ppermute | solution.py:421
  82.2 1.9 %collective-permute-done.14.refs_8_ = f32[7,128]{1,0:T(8,128)S(1)} collective-permute-done((f32[7,128]{1,0:T(8,128)S(1)}, f32[7,128]{1,0:T(8,128)S(1)}, u32[]{:S(2)}, u32[]{:S(2)}) %collective-permute-start.14) | collective-permute-done | bytes 3616 | tf_op jit(solution)/shard_map/ppermute | solution.py:421
  89.9 2.6 %collective-permute-done.18.refs_3_ = f32[2,1024]{1,0:T(2,128)S(1)} collective-permute-done((f32[2,1024]{1,0:T(2,128)S(1)}, f32[2,1024]{1,0:T(2,128)S(1)}, u32[]{:S(2)}, u32[]{:S(2)}) %collective-permute-start.18) | collective-permute-done | bytes 8224 | tf_op jit(solution)/shard_map/ppermute | solution.py:410
  94.7 1.9 %collective-permute-done.19 = f32[1,128]{1,0:T(1,128)S(1)} collective-permute-done((f32[1,128]{1,0:T(1,128)S(1)}, f32[1,128]{1,0:T(1,128)S(1)}, u32[]{:S(2)}, u32[]{:S(2)}) %collective-permute-start.19) | collective-permute-done | bytes 544 | tf_op jit(solution)/shard_map/ppermute | solution.py:421
  96.6 2.6 %collective-permute-start.20 = (f32[1,128]{1,0:T(1,128)S(1)}, f32[1,128]{1,0:T(1,128)S(1)}, u32[]{:S(2)}, u32[]{:S(2)}) collective-permute-start(f32[1,128]{1,0:T(1,128)S(1)} %add.11.refs_7_.refs_6_), channel_id=1, source_target_pairs={{0,2},{1,3},{2,0},{3,1},{4,6},{5,7},{6,4},{7,5},{8,10},{9,11},{10,... | collective-permute-start | bytes 1544 | tf_op jit(solution)/shard_map/ppermute | solution.py:421
  99.2 1.8 %collective-permute-done.20.refs_8_.refs_7_ = f32[1,128]{1,0:T(1,128)S(1)} collective-permute-done((f32[1,128]{1,0:T(1,128)S(1)}, f32[1,128]{1,0:T(1,128)S(1)}, u32[]{:S(2)}, u32[]{:S(2)}) %collective-permute-start.20) | collective-permute-done | bytes 544 | tf_op jit(solution)/shard_map/ppermute | solution.py:421
  105.9 19.2 %collective-permute-done.21.refs_0_ = bf16[448,1024]{1,0:T(8,128)(2,1)S(1)} collective-permute-done((bf16[448,1024]{1,0:T(8,128)(2,1)S(1)}, bf16[448,1024]{1,0:T(8,128)(2,1)S(1)}, u32[]{:S(2)}, u32[]{:S(2)}) %collective-permute-start.21) | collective-permute-done | bytes 917536 | tf_op jit(solution)/shard_map/ppermute | solution.py:410
  128.5 16.4 %collective-permute-done.25.refs_1_ = bf16[448,1024]{1,0:T(8,128)(2,1)S(1)} collective-permute-done((bf16[448,1024]{1,0:T(8,128)(2,1)S(1)}, bf16[448,1024]{1,0:T(8,128)(2,1)S(1)}, u32[]{:S(2)}, u32[]{:S(2)}) %collective-permute-start.25) | collective-permute-done | bytes 917536 | tf_op jit(solution)/shard_map/ppermute | solution.py:410
  144.8 2.3 %shard_map.107 = f32[896,1024]{1,0:T(8,128)} custom-call(f32[512,512]{1,0:T(8,128)S(1)} %get-tuple-element.73.refs_0_, f32[512,512]{1,0:T(8,128)S(1)} %get-tuple-element.57.refs_1_, f32[384,512]{1,0:T(8,128)S(1)} %get-tuple-element.60.refs_2_, f32[384,512]{1,0:T(8,128)S(1)} %get-tuple-element.63.refs_3_, f32[7,128]{1,0:T(8,128)S(1)} %get-tuple-element.67.refs_5_.refs_4_, ...), custom_call_target="tpu_custom_call" | custom-call | bytes 7348736 | tf_op jit(solution)/shard_map/pallas_call | solution.py:281
  147.1 1.9 %shard_map.105.refs_2_ = bf16[3584,1024]{1,0:T(8,128)(2,1)} custom-call(bf16[448,1024]{1,0:T(8,128)(2,1)S(1)} %collective-permute-done.21.refs_0_, bf16[448,1024]{1,0:T(8,128)(2,1)S(1)} %collective-permute-done.25.refs_1_, bf16[448,1024]{1,0:T(8,128)(2,1)S(1)} %collective-permute-done.23.refs_2_, ...), custom_call_target="tpu_custom_call", output_to_operand_aliasing={{}: (4, {})} | custom-call | bytes 7340032 | tf_op jit(solution)/shard_map/pallas_call | solution.py:281
  149.0 11.8 %collective-permute-done.22.refs_0_ = bf16[448,1024]{1,0:T(8,128)(2,1)S(1)} collective-permute-done((bf16[448,1024]{1,0:T(8,128)(2,1)S(1)}, bf16[448,1024]{1,0:T(8,128)(2,1)S(1)}, u32[]{:S(2)}, u32[]{:S(2)}) %collective-permute-start.22) | collective-permute-done | bytes 917536 | tf_op jit(solution)/shard_map/ppermute | solution.py:410
  (65 shorter events, 35.2 us)
Async XLA Ops:
  0.6 6.2 %collective-permute-start.1 = (bf16[512,1024]{1,0:T(8,128)(2,1)}, bf16[512,1024]{1,0:T(8,128)(2,1)S(1)}, u32[]{:S(2)}, u32[]{:S(2)}) collective-permute-start(bf16[512,1024]{1,0:T(8,128)(2,1)} %grad_out.1), channel_id=1, source_target_pairs={{0,16},{16,0},{1,17},{17,1},{2,18},{18,2},{3,19},{19,3},{4,20},{20... | collective-permute-start | bytes 3145736 | tf_op jit(solution)/shard_map/ppermute | solution.py:413
  2.8 4.0 %collective-permute-start.5 = (bf16[512,896]{1,0:T(8,128)(2,1)S(1)}, bf16[512,896]{1,0:T(8,128)(2,1)S(1)}, u32[]{:S(2)}, u32[]{:S(2)}) collective-permute-start(bf16[512,896]{1,0:T(8,128)(2,1)S(1)} %get-tuple-element.47), channel_id=1, source_target_pairs={{0,16},{16,0},{1,17},{17,1},{2,18},{18,2},{3,19},{19,3},{4,20},{20... | collective-permute-start | bytes 2752520 | tf_op jit(solution)/shard_map/ppermute | solution.py:413
  5.0 8.1 %collective-permute-start.2 = (bf16[512,896]{1,0:T(8,128)(2,1)S(1)}, bf16[512,896]{1,0:T(8,128)(2,1)S(1)}, u32[]{:S(2)}, u32[]{:S(2)}) collective-permute-start(bf16[512,896]{1,0:T(8,128)(2,1)S(1)} %get-tuple-element.43), channel_id=1, source_target_pairs={{0,16},{16,0},{1,17},{17,1},{2,18},{18,2},{3,19},{19,3},{4,20},{20... | collective-permute-start | bytes 2752520 | tf_op jit(solution)/shard_map/ppermute | solution.py:413
  5.2 11.2 %collective-permute-start.4 = (bf16[512,896]{1,0:T(8,128)(2,1)S(1)}, bf16[512,896]{1,0:T(8,128)(2,1)S(1)}, u32[]{:S(2)}, u32[]{:S(2)}) collective-permute-start(bf16[512,896]{1,0:T(8,128)(2,1)S(1)} %get-tuple-element.45), channel_id=1, source_target_pairs={{0,16},{16,0},{1,17},{17,1},{2,18},{18,2},{3,19},{19,3},{4,20},{20... | collective-permute-start | bytes 2752520 | tf_op jit(solution)/shard_map/ppermute | solution.py:413
  9.0 24.2 %collective-permute-start.6 = (bf16[912,512]{1,0:T(8,128)(2,1)S(1)}, bf16[912,512]{1,0:T(8,128)(2,1)S(1)}, u32[]{:S(2)}, u32[]{:S(2)}) collective-permute-start(bf16[912,512]{1,0:T(8,128)(2,1)S(1)} %get-tuple-element.50), channel_id=1, source_target_pairs={{0,4},{4,0},{8,12},{12,8},{1,5},{5,1},{9,13},{13,9},{2,6},{6,2},{1... | collective-permute-start | bytes 2801672 | tf_op jit(solution)/shard_map/ppermute | solution.py:410
  11.6 24.5 %collective-permute-start.9 = (bf16[912,512]{1,0:T(8,128)(2,1)S(1)}, bf16[912,512]{1,0:T(8,128)(2,1)S(1)}, u32[]{:S(2)}, u32[]{:S(2)}) collective-permute-start(bf16[912,512]{1,0:T(8,128)(2,1)S(1)} %get-tuple-element.55), channel_id=1, source_target_pairs={{0,8},{4,12},{8,0},{12,4},{1,9},{5,13},{9,1},{13,5},{2,10},{6,14},... | collective-permute-start | bytes 2801672 | tf_op jit(solution)/shard_map/ppermute | solution.py:410
  15.8 37.4 %collective-permute-start.3 = (bf16[912,512]{1,0:T(8,128)(2,1)S(1)}, bf16[912,512]{1,0:T(8,128)(2,1)S(1)}, u32[]{:S(2)}, u32[]{:S(2)}) collective-permute-start(bf16[912,512]{1,0:T(8,128)(2,1)S(1)} %get-tuple-element.44), channel_id=1, source_target_pairs={{0,4},{4,0},{8,12},{12,8},{1,5},{5,1},{9,13},{13,9},{2,6},{6,2},{1... | collective-permute-start | bytes 2801672 | tf_op jit(solution)/shard_map/ppermute | solution.py:410
  16.4 22.7 %collective-permute-start = (bf16[512,896]{1,0:T(8,128)(2,1)S(1)}, bf16[512,896]{1,0:T(8,128)(2,1)S(1)}, u32[]{:S(2)}, u32[]{:S(2)}) collective-permute-start(bf16[512,896]{1,0:T(8,128)(2,1)S(1)} %get-tuple-element.40), channel_id=1, source_target_pairs={{0,16},{16,0},{1,17},{17,1},{2,18},{18,2},{3,19},{19,3},{4,20},{20... | collective-permute-start | bytes 2752520 | tf_op jit(solution)/shard_map/ppermute | solution.py:413
  19.0 39.1 %collective-permute-start.8 = (bf16[912,512]{1,0:T(8,128)(2,1)S(1)}, bf16[912,512]{1,0:T(8,128)(2,1)S(1)}, u32[]{:S(2)}, u32[]{:S(2)}) collective-permute-start(bf16[912,512]{1,0:T(8,128)(2,1)S(1)} %get-tuple-element.53), channel_id=1, source_target_pairs={{0,8},{4,12},{8,0},{12,4},{1,9},{5,13},{9,1},{13,5},{2,10},{6,14},... | collective-permute-start | bytes 2801672 | tf_op jit(solution)/shard_map/ppermute | solution.py:410
  34.0 32.7 %collective-permute-start.7 = (bf16[528,512]{1,0:T(8,128)(2,1)S(1)}, bf16[528,512]{1,0:T(8,128)(2,1)S(1)}, u32[]{:S(2)}, u32[]{:S(2)}) collective-permute-start(bf16[528,512]{1,0:T(8,128)(2,1)S(1)} %shard_map.92), channel_id=1, source_target_pairs={{0,8},{4,12},{8,0},{12,4},{1,9},{5,13},{9,1},{13,5},{2,10},{6,14},... | collective-permute-start | bytes 1622024 | tf_op jit(solution)/shard_map/ppermute | solution.py:410
  36.9 30.6 %collective-permute-start.10 = (bf16[528,512]{1,0:T(8,128)(2,1)S(1)}, bf16[528,512]{1,0:T(8,128)(2,1)S(1)}, u32[]{:S(2)}, u32[]{:S(2)}) collective-permute-start(bf16[528,512]{1,0:T(8,128)(2,1)S(1)} %shard_map.95), channel_id=1, source_target_pairs={{0,4},{4,0},{8,12},{12,8},{1,5},{5,1},{9,13},{13,9},{2,6},{6,2},{1... | collective-permute-start | bytes 1622024 | tf_op jit(solution)/shard_map/ppermute | solution.py:410
  39.1 35.6 %collective-permute-start.11 = (bf16[400,512]{1,0:T(8,128)(2,1)S(1)}, bf16[400,512]{1,0:T(8,128)(2,1)S(1)}, u32[]{:S(2)}, u32[]{:S(2)}) collective-permute-start(bf16[400,512]{1,0:T(8,128)(2,1)S(1)} %shard_map.97), channel_id=1, source_target_pairs={{0,8},{4,12},{8,0},{12,4},{1,9},{5,13},{9,1},{13,5},{2,10},{6,14},... | collective-permute-start | bytes 1228808 | tf_op jit(solution)/shard_map/ppermute | solution.py:410
  53.2 22.2 %collective-permute-start.12 = (bf16[400,512]{1,0:T(8,128)(2,1)S(1)}, bf16[400,512]{1,0:T(8,128)(2,1)S(1)}, u32[]{:S(2)}, u32[]{:S(2)}) collective-permute-start(bf16[400,512]{1,0:T(8,128)(2,1)S(1)} %shard_map.99), channel_id=1, source_target_pairs={{0,4},{4,0},{8,12},{12,8},{1,5},{5,1},{9,13},{13,9},{2,6},{6,2},{1... | collective-permute-start | bytes 1228808 | tf_op jit(solution)/shard_map/ppermute | solution.py:410
  75.9 3.7 %collective-permute-start.13 = (f32[7,128]{1,0:T(8,128)S(1)}, f32[7,128]{1,0:T(8,128)S(1)}, u32[]{:S(2)}, u32[]{:S(2)}) collective-permute-start(f32[7,128]{1,0:T(8,128)S(1)} %get-tuple-element.66), channel_id=1, source_target_pairs={{0,1},{1,0},{2,3},{3,2},{4,5},{5,4},{6,7},{7,6},{8,9},{9,8},{10,11... | collective-permute-start | bytes 10760 | tf_op jit(solution)/shard_map/ppermute | solution.py:421
  79.6 4.5 %collective-permute-start.14 = (f32[7,128]{1,0:T(8,128)S(1)}, f32[7,128]{1,0:T(8,128)S(1)}, u32[]{:S(2)}, u32[]{:S(2)}) collective-permute-start(f32[7,128]{1,0:T(8,128)S(1)} %add.9.refs_7_), channel_id=1, source_target_pairs={{0,2},{1,3},{2,0},{3,1},{4,6},{5,7},{6,4},{7,5},{8,10},{9,11},{10,... | collective-permute-start | bytes 10760 | tf_op jit(solution)/shard_map/ppermute | solution.py:421
  86.2 3.7 %collective-permute-start.17 = (f32[2,1024]{1,0:T(2,128)S(1)}, f32[2,1024]{1,0:T(2,128)S(1)}, u32[]{:S(2)}, u32[]{:S(2)}) collective-permute-start(f32[2,1024]{1,0:T(2,128)S(1)} %add.10.refs_0_), channel_id=1, source_target_pairs={{0,8},{4,12},{8,0},{12,4},{1,9},{5,13},{9,1},{13,5},{2,10},{6,14},... | collective-permute-start | bytes 24584 | tf_op jit(solution)/shard_map/ppermute | solution.py:410
  87.9 4.5 %collective-permute-start.18 = (f32[2,1024]{1,0:T(2,128)S(1)}, f32[2,1024]{1,0:T(2,128)S(1)}, u32[]{:S(2)}, u32[]{:S(2)}) collective-permute-start(f32[2,1024]{1,0:T(2,128)S(1)} %add.10.refs_0_), channel_id=1, source_target_pairs={{0,12},{4,8},{8,4},{12,0},{1,13},{5,9},{9,5},{13,1},{2,14},{6,10},... | collective-permute-start | bytes 24584 | tf_op jit(solution)/shard_map/ppermute | solution.py:410
  96.6 4.4 %collective-permute-start.20 = (f32[1,128]{1,0:T(1,128)S(1)}, f32[1,128]{1,0:T(1,128)S(1)}, u32[]{:S(2)}, u32[]{:S(2)}) collective-permute-start(f32[1,128]{1,0:T(1,128)S(1)} %add.11.refs_7_.refs_6_), channel_id=1, source_target_pairs={{0,2},{1,3},{2,0},{3,1},{4,6},{5,7},{6,4},{7,5},{8,10},{9,11},{10,... | collective-permute-start | bytes 1544 | tf_op jit(solution)/shard_map/ppermute | solution.py:421
  101.8 23.4 %collective-permute-start.21 = (bf16[448,1024]{1,0:T(8,128)(2,1)S(1)}, bf16[448,1024]{1,0:T(8,128)(2,1)S(1)}, u32[]{:S(2)}, u32[]{:S(2)}) collective-permute-start(bf16[448,1024]{1,0:T(8,128)(2,1)S(1)} %get-tuple-element.71.refs_0_), channel_id=1, source_target_pairs={{0,4},{4,0},{8,12},{12,8},{1,5},{5,1},{9,13},{13,9},{2,6},{6,2},{1... | collective-permute-start | bytes 2752520 | tf_op jit(solution)/shard_map/ppermute | solution.py:410
  103.4 23.3 %collective-permute-start.23 = (bf16[448,1024]{1,0:T(8,128)(2,1)S(1)}, bf16[448,1024]{1,0:T(8,128)(2,1)S(1)}, u32[]{:S(2)}, u32[]{:S(2)}) collective-permute-start(bf16[448,1024]{1,0:T(8,128)(2,1)S(1)} %get-tuple-element.72.refs_1_), channel_id=1, source_target_pairs={{0,8},{4,12},{8,0},{12,4},{1,9},{5,13},{9,1},{13,5},{2,10},{6,14},... | collective-permute-start | bytes 2752520 | tf_op jit(solution)/shard_map/ppermute | solution.py:410
  103.9 40.9 %collective-permute-start.25 = (bf16[448,1024]{1,0:T(8,128)(2,1)S(1)}, bf16[448,1024]{1,0:T(8,128)(2,1)S(1)}, u32[]{:S(2)}, u32[]{:S(2)}) collective-permute-start(bf16[448,1024]{1,0:T(8,128)(2,1)S(1)} %get-tuple-element.72.refs_1_), channel_id=1, source_target_pairs={{0,4},{4,0},{8,12},{12,8},{1,5},{5,1},{9,13},{13,9},{2,6},{6,2},{1... | collective-permute-start | bytes 2752520 | tf_op jit(solution)/shard_map/ppermute | solution.py:410
  104.3 42.9 %collective-permute-start.26 = (bf16[448,1024]{1,0:T(8,128)(2,1)S(1)}, bf16[448,1024]{1,0:T(8,128)(2,1)S(1)}, u32[]{:S(2)}, u32[]{:S(2)}) collective-permute-start(bf16[448,1024]{1,0:T(8,128)(2,1)S(1)} %get-tuple-element.71.refs_0_), channel_id=1, source_target_pairs={{0,8},{4,12},{8,0},{12,4},{1,9},{5,13},{9,1},{13,5},{2,10},{6,14},... | collective-permute-start | bytes 2752520 | tf_op jit(solution)/shard_map/ppermute | solution.py:410
  125.2 35.7 %collective-permute-start.22 = (bf16[448,1024]{1,0:T(8,128)(2,1)S(1)}, bf16[448,1024]{1,0:T(8,128)(2,1)S(1)}, u32[]{:S(2)}, u32[]{:S(2)}) collective-permute-start(bf16[448,1024]{1,0:T(8,128)(2,1)S(1)} %collective-permute-done.21.refs_0_), channel_id=1, source_target_pairs={{0,8},{4,12},{8,0},{12,4},{1,9},{5,13},{9,1},{13,5},{2,10},{6,14},... | collective-permute-start | bytes 2752520 | tf_op jit(solution)/shard_map/ppermute | solution.py:410
  126.7 34.2 %collective-permute-start.24 = (bf16[448,1024]{1,0:T(8,128)(2,1)S(1)}, bf16[448,1024]{1,0:T(8,128)(2,1)S(1)}, u32[]{:S(2)}, u32[]{:S(2)}) collective-permute-start(bf16[448,1024]{1,0:T(8,128)(2,1)S(1)} %collective-permute-done.23.refs_2_), channel_id=1, source_target_pairs={{0,4},{4,0},{8,12},{12,8},{1,5},{5,1},{9,13},{13,9},{2,6},{6,2},{1... | collective-permute-start | bytes 2752520 | tf_op jit(solution)/shard_map/ppermute | solution.py:410
  (7 other events, 46.7 us)

commit v5 on v4

--- a/solution.py
+++ b/solution.py
@@ -217,9 +217,7 @@
 
 
 def factors(elements, parts, by_row, by_col):
-    total = parts[0][0:1, 0:1]
-    for part in parts[1:]:
-        total = total + part[0:1, 0:1]
+    total = tree_sum([part[0:1, 0:1] for part in parts])
     clip = jnp.maximum(1.0, jnp.sqrt(total / elements))
     return by_row[...] / clip, by_col[...]
 
@@ -414,6 +412,10 @@
 
     def exchange(parts, axis, n, step=None):
         step = step or (lambda x, d: turn(x, axis, n, d))
+        if axis is not None and n == 4:
+            x = sum(parts[1:], parts[0])
+            swap = lambda d: lax.ppermute(x, axis, [(a, a ^ d) for a in range(n)])
+            return [x] + [swap(d) for d in range(1, n)]
         if axis is not None and n & (n - 1) == 0:
             d = 1
             while d < n:

time: 162 us -> 163 us (level)
    ppermute x0 -> x6, starting transfers between devices: none -> 8.83 us  [exchange(): swap = lambda d: lax.ppermute(x, axis, [(a, a ^ d) for a in range(n)])]
    ppermute x5 -> x1, starting transfers between devices: 8.41 us -> 0.01 us  [exchange(): parts = [x, lax.ppermute(x, axis, [(a, a ^ d) for a in range(n)])]]
    ppermute x5 -> x1, waiting for transfers between devices: 8.92 us -> 1.17 us  [exchange(): parts = [x, lax.ppermute(x, axis, [(a, a ^ d) for a in range(n)])]]
    ppermute x0 -> x6, waiting for transfers between devices: none -> 6.89 us  [exchange(): swap = lambda d: lax.ppermute(x, axis, [(a, a ^ d) for a in range(n)])]
  transfers between devices with their start and end apart: 27 -> 29, of which waited for: 16 -> 16; matrix products, arithmetic and copies ran while one was open for 0% -> 0% of each run, Pallas kernels for 15% -> 15%
where the time goes in v5:
time: 163 us
  waiting for transfers between devices  101 us (62%)
  starting transfers between devices  29.5 us (18%)
  Pallas kernels  28.7 us (18%)
  local copies, waits for them, and re-layouts  1.89 us (1%)
    ppermute x17, waiting for transfers between devices, shift(): return lax.ppermute(x, 'seq', pairs)  93.3 us
    pallas_call x24, Pallas kernels, call(): pl.pallas_call(kernel, out_shape=out_shape, in_specs=specs or [NEAR] * le...  28.7 us
    ppermute x17, starting transfers between devices, shift(): return lax.ppermute(x, 'seq', pairs)  19.5 us
    ppermute x6, starting transfers between devices, exchange(): swap = lambda d: lax.ppermute(x, axis, [(a, a ^ d) for a in range(n)])  8.83 us
    ppermute x6, waiting for transfers between devices, exchange(): swap = lambda d: lax.ppermute(x, axis, [(a, a ^ d) for a in range(n)])  6.89 us
  transfers between devices with their start and end apart: 29, of which 16 were waited for; matrix products, arithmetic and copies ran while one was open for 0% of the time, Pallas kernels for 15%

profile of v5, /device:TPU:0, one launch (start us, length us, event | category | flops | bytes accessed | tf_op | source)
XLA Modules:
  0.0 162.5 jit_solution(10189801200745896252)
XLA Ops:
  1.2 1.7 %shard_map.85 = (bf16[512,896]{1,0:T(8,128)(2,1)S(1)}, bf16[512,1024]{1,0:T(8,128)(2,1)S(1)}) custom-call(bf16[512,7168]{1,0:T(8,128)(2,1)} %refs_0_.7, bf16[512,1024]{1,0:T(8,128)(2,1)} %grad_out.1), custom_call_target="tpu_custom_call" | custom-call | bytes 3932160 | tf_op jit(solution)/shard_map/pallas_call | solution.py:279
  3.0 1.9 %copy-done = bf16[512,7168]{1,0:T(8,128)(2,1)S(1)} copy-done((bf16[512,7168]{1,0:T(8,128)(2,1)S(1)}, bf16[512,7168]{1,0:T(8,128)(2,1)}, u32[]{:S(2)}) %copy-start) | copy-done | bytes 7340056
  6.8 2.2 %shard_map.91 = (bf16[912,512]{1,0:T(8,128)(2,1)S(1)}, bf16[912,512]{1,0:T(8,128)(2,1)S(1)}) custom-call(bf16[512,896]{1,0:T(8,128)(2,1)S(1)} %collective-permute-done.5.refs_0_, bf16[512,1024]{1,0:T(8,128)(2,1)S(1)} %collective-permute-done.1.refs_3_.refs_1_, f32[896,512]{1,0:T(8,128)S(1)} %get-tuple-element.48.refs_2_, ...), custom_call_target="tpu_custom_call" | custom-call | flops 939524096 | bytes 6586368 | tf_op jit(solution)/shard_map/pallas_call | solution.py:279
  9.0 2.6 %collective-permute-start.6 = (bf16[912,512]{1,0:T(8,128)(2,1)S(1)}, bf16[912,512]{1,0:T(8,128)(2,1)S(1)}, u32[]{:S(2)}, u32[]{:S(2)}) collective-permute-start(bf16[912,512]{1,0:T(8,128)(2,1)S(1)} %get-tuple-element.50), channel_id=1, source_target_pairs={{0,4},{4,0},{8,12},{12,8},{1,5},{5,1},{9,13},{13,9},{2,6},{6,2},{1... | collective-permute-start | bytes 2801672 | tf_op jit(solution)/shard_map/ppermute | solution.py:408
  13.2 2.6 %shard_map.87 = (bf16[912,512]{1,0:T(8,128)(2,1)S(1)}, f32[896,512]{1,0:T(8,128)S(1)}) custom-call(bf16[512,7168]{1,0:T(8,128)(2,1)S(1)} %copy-done, bf16[512,896]{1,0:T(8,128)(2,1)S(1)} %collective-permute-done.2.refs_1_, bf16[512,1024]{1,0:T(8,128)(2,1)S(1)} %get-tuple-element.41.refs_2_.refs_1_, bf16[512,1024]{1,0:T(8,128)(2,1)S(1)} %collective-permute-done.1.refs_3_.refs_1_), custom_call_target="tpu_custom_call" | custom-call | bytes 1 | tf_op jit(solution)/shard_map/pallas_call | solution.py:279
  16.4 2.6 %shard_map.89 = (f32[896,512]{1,0:T(8,128)S(1)}, bf16[912,512]{1,0:T(8,128)(2,1)S(1)}) custom-call(bf16[512,7168]{1,0:T(8,128)(2,1)S(1)} %copy-done, bf16[512,896]{1,0:T(8,128)(2,1)S(1)} %collective-permute-done.4.refs_1_, bf16[512,1024]{1,0:T(8,128)(2,1)S(1)} %get-tuple-element.41.refs_2_.refs_1_, bf16[512,1024]{1,0:T(8,128)(2,1)S(1)} %collective-permute-done.1.refs_3_.refs_1_), custom_call_target="tpu_custom_call" | custom-call | bytes 1 | tf_op jit(solution)/shard_map/pallas_call | solution.py:279
  19.2 14.0 %collective-permute-done.6.refs_0_ = bf16[912,512]{1,0:T(8,128)(2,1)S(1)} collective-permute-done((bf16[912,512]{1,0:T(8,128)(2,1)S(1)}, bf16[912,512]{1,0:T(8,128)(2,1)S(1)}, u32[]{:S(2)}, u32[]{:S(2)}) %collective-permute-start.6) | collective-permute-done | bytes 933920 | tf_op jit(solution)/shard_map/ppermute | solution.py:408
  34.0 2.1 %collective-permute-start.7 = (bf16[528,512]{1,0:T(8,128)(2,1)S(1)}, bf16[528,512]{1,0:T(8,128)(2,1)S(1)}, u32[]{:S(2)}, u32[]{:S(2)}) collective-permute-start(bf16[528,512]{1,0:T(8,128)(2,1)S(1)} %shard_map.92), channel_id=1, source_target_pairs={{0,8},{4,12},{8,0},{12,4},{1,9},{5,13},{9,1},{13,5},{2,10},{6,14},... | collective-permute-start | bytes 1622024 | tf_op jit(solution)/shard_map/ppermute | solution.py:408
  40.5 12.7 %collective-permute-done.3.refs_0_ = bf16[912,512]{1,0:T(8,128)(2,1)S(1)} collective-permute-done((bf16[912,512]{1,0:T(8,128)(2,1)S(1)}, bf16[912,512]{1,0:T(8,128)(2,1)S(1)}, u32[]{:S(2)}, u32[]{:S(2)}) %collective-permute-start.3) | collective-permute-done | bytes 933920 | tf_op jit(solution)/shard_map/ppermute | solution.py:408
  53.2 1.9 %collective-permute-start.12 = (bf16[400,512]{1,0:T(8,128)(2,1)S(1)}, bf16[400,512]{1,0:T(8,128)(2,1)S(1)}, u32[]{:S(2)}, u32[]{:S(2)}) collective-permute-start(bf16[400,512]{1,0:T(8,128)(2,1)S(1)} %shard_map.99), channel_id=1, source_target_pairs={{0,4},{4,0},{8,12},{12,8},{1,5},{5,1},{9,13},{13,9},{2,6},{6,2},{1... | collective-permute-start | bytes 1228808 | tf_op jit(solution)/shard_map/ppermute | solution.py:408
  55.1 2.1 %shard_map.86 = (f32[896,512]{1,0:T(8,128)S(1)}, f32[896,512]{1,0:T(8,128)S(1)}) custom-call(bf16[512,7168]{1,0:T(8,128)(2,1)S(1)} %copy-done, bf16[512,896]{1,0:T(8,128)(2,1)S(1)} %collective-permute-done.refs_1_, bf16[512,1024]{1,0:T(8,128)(2,1)S(1)} %get-tuple-element.41.refs_2_.refs_1_, bf16[512,1024]{1,0:T(8,128)(2,1)S(1)} %collective-permute-done.1.refs_3_.refs_1_), custom_call_target="tpu_custom_call" | custom-call | bytes 1 | tf_op jit(solution)/shard_map/pallas_call | solution.py:279
  59.1 7.7 %collective-permute-done.7.refs_0_ = bf16[528,512]{1,0:T(8,128)(2,1)S(1)} collective-permute-done((bf16[528,512]{1,0:T(8,128)(2,1)S(1)}, bf16[528,512]{1,0:T(8,128)(2,1)S(1)}, u32[]{:S(2)}, u32[]{:S(2)}) %collective-permute-start.7) | collective-permute-done | bytes 540704 | tf_op jit(solution)/shard_map/ppermute | solution.py:408
  68.2 6.6 %collective-permute-done.11.refs_0_ = bf16[400,512]{1,0:T(8,128)(2,1)S(1)} collective-permute-done((bf16[400,512]{1,0:T(8,128)(2,1)S(1)}, bf16[400,512]{1,0:T(8,128)(2,1)S(1)}, u32[]{:S(2)}, u32[]{:S(2)}) %collective-permute-start.11) | collective-permute-done | bytes 409632 | tf_op jit(solution)/shard_map/ppermute | solution.py:408
  77.5 2.6 %collective-permute-start.14 = (f32[7,128]{1,0:T(8,128)S(1)}, f32[7,128]{1,0:T(8,128)S(1)}, u32[]{:S(2)}, u32[]{:S(2)}) collective-permute-start(f32[7,128]{1,0:T(8,128)S(1)} %get-tuple-element.66.refs_7_), channel_id=1, source_target_pairs={{0,2},{1,3},{2,0},{3,1},{4,6},{5,7},{6,4},{7,5},{8,10},{9,11},{10,... | collective-permute-start | bytes 10760 | tf_op jit(solution)/shard_map/ppermute | solution.py:417
  80.4 1.7 %collective-permute-done.14.refs_9_ = f32[7,128]{1,0:T(8,128)S(1)} collective-permute-done((f32[7,128]{1,0:T(8,128)S(1)}, f32[7,128]{1,0:T(8,128)S(1)}, u32[]{:S(2)}, u32[]{:S(2)}) %collective-permute-start.14) | collective-permute-done | bytes 3616 | tf_op jit(solution)/shard_map/ppermute | solution.py:417
  82.0 3.5 %collective-permute-done.15.refs_10_ = f32[7,128]{1,0:T(8,128)S(1)} collective-permute-done((f32[7,128]{1,0:T(8,128)S(1)}, f32[7,128]{1,0:T(8,128)S(1)}, u32[]{:S(2)}, u32[]{:S(2)}) %collective-permute-start.15) | collective-permute-done | bytes 3616 | tf_op jit(solution)/shard_map/ppermute | solution.py:417
  91.5 2.4 %collective-permute-done.19.refs_3_ = f32[2,1024]{1,0:T(2,128)S(1)} collective-permute-done((f32[2,1024]{1,0:T(2,128)S(1)}, f32[2,1024]{1,0:T(2,128)S(1)}, u32[]{:S(2)}, u32[]{:S(2)}) %collective-permute-start.19) | collective-permute-done | bytes 8224 | tf_op jit(solution)/shard_map/ppermute | solution.py:408
  95.3 3.6 %collective-permute-start.22 = (f32[1,128]{1,0:T(1,128)S(1)}, f32[1,128]{1,0:T(1,128)S(1)}, u32[]{:S(2)}, u32[]{:S(2)}) collective-permute-start(f32[1,128]{1,0:T(1,128)S(1)} %get-tuple-element.70.refs_7_.refs_6_), channel_id=1, source_target_pairs={{0,3},{1,2},{2,1},{3,0},{4,7},{5,6},{6,5},{7,4},{8,11},{9,10},{10,... | collective-permute-start | bytes 1544 | tf_op jit(solution)/shard_map/ppermute | solution.py:417
  103.9 1.7 %collective-permute-start.28 = (bf16[448,1024]{1,0:T(8,128)(2,1)S(1)}, bf16[448,1024]{1,0:T(8,128)(2,1)S(1)}, u32[]{:S(2)}, u32[]{:S(2)}) collective-permute-start(bf16[448,1024]{1,0:T(8,128)(2,1)S(1)} %get-tuple-element.71.refs_0_), channel_id=1, source_target_pairs={{0,8},{4,12},{8,0},{12,4},{1,9},{5,13},{9,1},{13,5},{2,10},{6,14},... | collective-permute-start | bytes 2752520 | tf_op jit(solution)/shard_map/ppermute | solution.py:408
  105.5 19.2 %collective-permute-done.23.refs_0_ = bf16[448,1024]{1,0:T(8,128)(2,1)S(1)} collective-permute-done((bf16[448,1024]{1,0:T(8,128)(2,1)S(1)}, bf16[448,1024]{1,0:T(8,128)(2,1)S(1)}, u32[]{:S(2)}, u32[]{:S(2)}) %collective-permute-start.23) | collective-permute-done | bytes 917536 | tf_op jit(solution)/shard_map/ppermute | solution.py:408
  128.1 16.4 %collective-permute-done.27.refs_1_ = bf16[448,1024]{1,0:T(8,128)(2,1)S(1)} collective-permute-done((bf16[448,1024]{1,0:T(8,128)(2,1)S(1)}, bf16[448,1024]{1,0:T(8,128)(2,1)S(1)}, u32[]{:S(2)}, u32[]{:S(2)}) %collective-permute-start.27) | collective-permute-done | bytes 917536 | tf_op jit(solution)/shard_map/ppermute | solution.py:408
  144.4 2.3 %shard_map.107 = f32[896,1024]{1,0:T(8,128)} custom-call(f32[512,512]{1,0:T(8,128)S(1)} %get-tuple-element.73.refs_0_, f32[512,512]{1,0:T(8,128)S(1)} %get-tuple-element.57.refs_1_, f32[384,512]{1,0:T(8,128)S(1)} %get-tuple-element.60.refs_2_, f32[384,512]{1,0:T(8,128)S(1)} %get-tuple-element.63.refs_3_, f32[7,128]{1,0:T(8,128)S(1)} %get-tuple-element.67.refs_5_.refs_4_, ...), custom_call_target="tpu_custom_call" | custom-call | bytes 7349760 | tf_op jit(solution)/shard_map/pallas_call | solution.py:279
  146.7 1.9 %shard_map.105.refs_2_ = bf16[3584,1024]{1,0:T(8,128)(2,1)} custom-call(bf16[448,1024]{1,0:T(8,128)(2,1)S(1)} %collective-permute-done.23.refs_0_, bf16[448,1024]{1,0:T(8,128)(2,1)S(1)} %collective-permute-done.27.refs_1_, bf16[448,1024]{1,0:T(8,128)(2,1)S(1)} %collective-permute-done.25.refs_2_, ...), custom_call_target="tpu_custom_call", output_to_operand_aliasing={{}: (4, {})} | custom-call | bytes 7340032 | tf_op jit(solution)/shard_map/pallas_call | solution.py:279
  148.6 12.5 %collective-permute-done.24.refs_0_ = bf16[448,1024]{1,0:T(8,128)(2,1)S(1)} collective-permute-done((bf16[448,1024]{1,0:T(8,128)(2,1)S(1)}, bf16[448,1024]{1,0:T(8,128)(2,1)S(1)}, u32[]{:S(2)}, u32[]{:S(2)}) %collective-permute-start.24) | collective-permute-done | bytes 917536 | tf_op jit(solution)/shard_map/ppermute | solution.py:408
  (67 shorter events, 33.1 us)
Async XLA Ops:
  0.6 6.2 %collective-permute-start.1 = (bf16[512,1024]{1,0:T(8,128)(2,1)}, bf16[512,1024]{1,0:T(8,128)(2,1)S(1)}, u32[]{:S(2)}, u32[]{:S(2)}) collective-permute-start(bf16[512,1024]{1,0:T(8,128)(2,1)} %grad_out.1), channel_id=1, source_target_pairs={{0,16},{16,0},{1,17},{17,1},{2,18},{18,2},{3,19},{19,3},{4,20},{20... | collective-permute-start | bytes 3145736 | tf_op jit(solution)/shard_map/ppermute | solution.py:411
  5.0 8.1 %collective-permute-start.2 = (bf16[512,896]{1,0:T(8,128)(2,1)S(1)}, bf16[512,896]{1,0:T(8,128)(2,1)S(1)}, u32[]{:S(2)}, u32[]{:S(2)}) collective-permute-start(bf16[512,896]{1,0:T(8,128)(2,1)S(1)} %get-tuple-element.43), channel_id=1, source_target_pairs={{0,16},{16,0},{1,17},{17,1},{2,18},{18,2},{3,19},{19,3},{4,20},{20... | collective-permute-start | bytes 2752520 | tf_op jit(solution)/shard_map/ppermute | solution.py:411
  5.2 11.2 %collective-permute-start.4 = (bf16[512,896]{1,0:T(8,128)(2,1)S(1)}, bf16[512,896]{1,0:T(8,128)(2,1)S(1)}, u32[]{:S(2)}, u32[]{:S(2)}) collective-permute-start(bf16[512,896]{1,0:T(8,128)(2,1)S(1)} %get-tuple-element.45), channel_id=1, source_target_pairs={{0,16},{16,0},{1,17},{17,1},{2,18},{18,2},{3,19},{19,3},{4,20},{20... | collective-permute-start | bytes 2752520 | tf_op jit(solution)/shard_map/ppermute | solution.py:411
  9.0 24.2 %collective-permute-start.6 = (bf16[912,512]{1,0:T(8,128)(2,1)S(1)}, bf16[912,512]{1,0:T(8,128)(2,1)S(1)}, u32[]{:S(2)}, u32[]{:S(2)}) collective-permute-start(bf16[912,512]{1,0:T(8,128)(2,1)S(1)} %get-tuple-element.50), channel_id=1, source_target_pairs={{0,4},{4,0},{8,12},{12,8},{1,5},{5,1},{9,13},{13,9},{2,6},{6,2},{1... | collective-permute-start | bytes 2801672 | tf_op jit(solution)/shard_map/ppermute | solution.py:408
  11.6 24.5 %collective-permute-start.9 = (bf16[912,512]{1,0:T(8,128)(2,1)S(1)}, bf16[912,512]{1,0:T(8,128)(2,1)S(1)}, u32[]{:S(2)}, u32[]{:S(2)}) collective-permute-start(bf16[912,512]{1,0:T(8,128)(2,1)S(1)} %get-tuple-element.55), channel_id=1, source_target_pairs={{0,8},{4,12},{8,0},{12,4},{1,9},{5,13},{9,1},{13,5},{2,10},{6,14},... | collective-permute-start | bytes 2801672 | tf_op jit(solution)/shard_map/ppermute | solution.py:408
  15.8 37.4 %collective-permute-start.3 = (bf16[912,512]{1,0:T(8,128)(2,1)S(1)}, bf16[912,512]{1,0:T(8,128)(2,1)S(1)}, u32[]{:S(2)}, u32[]{:S(2)}) collective-permute-start(bf16[912,512]{1,0:T(8,128)(2,1)S(1)} %get-tuple-element.44), channel_id=1, source_target_pairs={{0,4},{4,0},{8,12},{12,8},{1,5},{5,1},{9,13},{13,9},{2,6},{6,2},{1... | collective-permute-start | bytes 2801672 | tf_op jit(solution)/shard_map/ppermute | solution.py:408
  16.4 22.7 %collective-permute-start = (bf16[512,896]{1,0:T(8,128)(2,1)S(1)}, bf16[512,896]{1,0:T(8,128)(2,1)S(1)}, u32[]{:S(2)}, u32[]{:S(2)}) collective-permute-start(bf16[512,896]{1,0:T(8,128)(2,1)S(1)} %get-tuple-element.40), channel_id=1, source_target_pairs={{0,16},{16,0},{1,17},{17,1},{2,18},{18,2},{3,19},{19,3},{4,20},{20... | collective-permute-start | bytes 2752520 | tf_op jit(solution)/shard_map/ppermute | solution.py:411
  19.0 39.1 %collective-permute-start.8 = (bf16[912,512]{1,0:T(8,128)(2,1)S(1)}, bf16[912,512]{1,0:T(8,128)(2,1)S(1)}, u32[]{:S(2)}, u32[]{:S(2)}) collective-permute-start(bf16[912,512]{1,0:T(8,128)(2,1)S(1)} %get-tuple-element.53), channel_id=1, source_target_pairs={{0,8},{4,12},{8,0},{12,4},{1,9},{5,13},{9,1},{13,5},{2,10},{6,14},... | collective-permute-start | bytes 2801672 | tf_op jit(solution)/shard_map/ppermute | solution.py:408
  34.0 32.7 %collective-permute-start.7 = (bf16[528,512]{1,0:T(8,128)(2,1)S(1)}, bf16[528,512]{1,0:T(8,128)(2,1)S(1)}, u32[]{:S(2)}, u32[]{:S(2)}) collective-permute-start(bf16[528,512]{1,0:T(8,128)(2,1)S(1)} %shard_map.92), channel_id=1, source_target_pairs={{0,8},{4,12},{8,0},{12,4},{1,9},{5,13},{9,1},{13,5},{2,10},{6,14},... | collective-permute-start | bytes 1622024 | tf_op jit(solution)/shard_map/ppermute | solution.py:408
  36.9 30.6 %collective-permute-start.10 = (bf16[528,512]{1,0:T(8,128)(2,1)S(1)}, bf16[528,512]{1,0:T(8,128)(2,1)S(1)}, u32[]{:S(2)}, u32[]{:S(2)}) collective-permute-start(bf16[528,512]{1,0:T(8,128)(2,1)S(1)} %shard_map.95), channel_id=1, source_target_pairs={{0,4},{4,0},{8,12},{12,8},{1,5},{5,1},{9,13},{13,9},{2,6},{6,2},{1... | collective-permute-start | bytes 1622024 | tf_op jit(solution)/shard_map/ppermute | solution.py:408
  39.1 35.6 %collective-permute-start.11 = (bf16[400,512]{1,0:T(8,128)(2,1)S(1)}, bf16[400,512]{1,0:T(8,128)(2,1)S(1)}, u32[]{:S(2)}, u32[]{:S(2)}) collective-permute-start(bf16[400,512]{1,0:T(8,128)(2,1)S(1)} %shard_map.97), channel_id=1, source_target_pairs={{0,8},{4,12},{8,0},{12,4},{1,9},{5,13},{9,1},{13,5},{2,10},{6,14},... | collective-permute-start | bytes 1228808 | tf_op jit(solution)/shard_map/ppermute | solution.py:408
  53.2 22.2 %collective-permute-start.12 = (bf16[400,512]{1,0:T(8,128)(2,1)S(1)}, bf16[400,512]{1,0:T(8,128)(2,1)S(1)}, u32[]{:S(2)}, u32[]{:S(2)}) collective-permute-start(bf16[400,512]{1,0:T(8,128)(2,1)S(1)} %shard_map.99), channel_id=1, source_target_pairs={{0,4},{4,0},{8,12},{12,8},{1,5},{5,1},{9,13},{13,9},{2,6},{6,2},{1... | collective-permute-start | bytes 1228808 | tf_op jit(solution)/shard_map/ppermute | solution.py:408
  75.9 4.5 %collective-permute-start.13 = (f32[7,128]{1,0:T(8,128)S(1)}, f32[7,128]{1,0:T(8,128)S(1)}, u32[]{:S(2)}, u32[]{:S(2)}) collective-permute-start(f32[7,128]{1,0:T(8,128)S(1)} %get-tuple-element.66.refs_7_), channel_id=1, source_target_pairs={{0,1},{1,0},{2,3},{3,2},{4,5},{5,4},{6,7},{7,6},{8,9},{9,8},{10,11... | collective-permute-start | bytes 10760 | tf_op jit(solution)/shard_map/ppermute | solution.py:417
  77.5 4.5 %collective-permute-start.14 = (f32[7,128]{1,0:T(8,128)S(1)}, f32[7,128]{1,0:T(8,128)S(1)}, u32[]{:S(2)}, u32[]{:S(2)}) collective-permute-start(f32[7,128]{1,0:T(8,128)S(1)} %get-tuple-element.66.refs_7_), channel_id=1, source_target_pairs={{0,2},{1,3},{2,0},{3,1},{4,6},{5,7},{6,4},{7,5},{8,10},{9,11},{10,... | collective-permute-start | bytes 10760 | tf_op jit(solution)/shard_map/ppermute | solution.py:417
  80.1 5.4 %collective-permute-start.15 = (f32[7,128]{1,0:T(8,128)S(1)}, f32[7,128]{1,0:T(8,128)S(1)}, u32[]{:S(2)}, u32[]{:S(2)}) collective-permute-start(f32[7,128]{1,0:T(8,128)S(1)} %get-tuple-element.66.refs_7_), channel_id=1, source_target_pairs={{0,3},{1,2},{2,1},{3,0},{4,7},{5,6},{6,5},{7,4},{8,11},{9,10},{10,... | collective-permute-start | bytes 10760 | tf_op jit(solution)/shard_map/ppermute | solution.py:417
  89.4 4.5 %collective-permute-start.19 = (f32[2,1024]{1,0:T(2,128)S(1)}, f32[2,1024]{1,0:T(2,128)S(1)}, u32[]{:S(2)}, u32[]{:S(2)}) collective-permute-start(f32[2,1024]{1,0:T(2,128)S(1)} %add.3.refs_0_), channel_id=1, source_target_pairs={{0,12},{4,8},{8,4},{12,0},{1,13},{5,9},{9,5},{13,1},{2,14},{6,10},... | collective-permute-start | bytes 24584 | tf_op jit(solution)/shard_map/ppermute | solution.py:408
  94.6 4.4 %collective-permute-start.21 = (f32[1,128]{1,0:T(1,128)S(1)}, f32[1,128]{1,0:T(1,128)S(1)}, u32[]{:S(2)}, u32[]{:S(2)}) collective-permute-start(f32[1,128]{1,0:T(1,128)S(1)} %get-tuple-element.70.refs_7_.refs_6_), channel_id=1, source_target_pairs={{0,2},{1,3},{2,0},{3,1},{4,6},{5,7},{6,4},{7,5},{8,10},{9,11},{10,... | collective-permute-start | bytes 1544 | tf_op jit(solution)/shard_map/ppermute | solution.py:417
  95.3 5.3 %collective-permute-start.22 = (f32[1,128]{1,0:T(1,128)S(1)}, f32[1,128]{1,0:T(1,128)S(1)}, u32[]{:S(2)}, u32[]{:S(2)}) collective-permute-start(f32[1,128]{1,0:T(1,128)S(1)} %get-tuple-element.70.refs_7_.refs_6_), channel_id=1, source_target_pairs={{0,3},{1,2},{2,1},{3,0},{4,7},{5,6},{6,5},{7,4},{8,11},{9,10},{10,... | collective-permute-start | bytes 1544 | tf_op jit(solution)/shard_map/ppermute | solution.py:417
  101.4 23.4 %collective-permute-start.23 = (bf16[448,1024]{1,0:T(8,128)(2,1)S(1)}, bf16[448,1024]{1,0:T(8,128)(2,1)S(1)}, u32[]{:S(2)}, u32[]{:S(2)}) collective-permute-start(bf16[448,1024]{1,0:T(8,128)(2,1)S(1)} %get-tuple-element.71.refs_0_), channel_id=1, source_target_pairs={{0,4},{4,0},{8,12},{12,8},{1,5},{5,1},{9,13},{13,9},{2,6},{6,2},{1... | collective-permute-start | bytes 2752520 | tf_op jit(solution)/shard_map/ppermute | solution.py:408
  103.0 23.3 %collective-permute-start.25 = (bf16[448,1024]{1,0:T(8,128)(2,1)S(1)}, bf16[448,1024]{1,0:T(8,128)(2,1)S(1)}, u32[]{:S(2)}, u32[]{:S(2)}) collective-permute-start(bf16[448,1024]{1,0:T(8,128)(2,1)S(1)} %get-tuple-element.72.refs_1_), channel_id=1, source_target_pairs={{0,8},{4,12},{8,0},{12,4},{1,9},{5,13},{9,1},{13,5},{2,10},{6,14},... | collective-permute-start | bytes 2752520 | tf_op jit(solution)/shard_map/ppermute | solution.py:408
  103.5 40.9 %collective-permute-start.27 = (bf16[448,1024]{1,0:T(8,128)(2,1)S(1)}, bf16[448,1024]{1,0:T(8,128)(2,1)S(1)}, u32[]{:S(2)}, u32[]{:S(2)}) collective-permute-start(bf16[448,1024]{1,0:T(8,128)(2,1)S(1)} %get-tuple-element.72.refs_1_), channel_id=1, source_target_pairs={{0,4},{4,0},{8,12},{12,8},{1,5},{5,1},{9,13},{13,9},{2,6},{6,2},{1... | collective-permute-start | bytes 2752520 | tf_op jit(solution)/shard_map/ppermute | solution.py:408
  103.9 42.9 %collective-permute-start.28 = (bf16[448,1024]{1,0:T(8,128)(2,1)S(1)}, bf16[448,1024]{1,0:T(8,128)(2,1)S(1)}, u32[]{:S(2)}, u32[]{:S(2)}) collective-permute-start(bf16[448,1024]{1,0:T(8,128)(2,1)S(1)} %get-tuple-element.71.refs_0_), channel_id=1, source_target_pairs={{0,8},{4,12},{8,0},{12,4},{1,9},{5,13},{9,1},{13,5},{2,10},{6,14},... | collective-permute-start | bytes 2752520 | tf_op jit(solution)/shard_map/ppermute | solution.py:408
  124.8 36.3 %collective-permute-start.24 = (bf16[448,1024]{1,0:T(8,128)(2,1)S(1)}, bf16[448,1024]{1,0:T(8,128)(2,1)S(1)}, u32[]{:S(2)}, u32[]{:S(2)}) collective-permute-start(bf16[448,1024]{1,0:T(8,128)(2,1)S(1)} %collective-permute-done.23.refs_0_), channel_id=1, source_target_pairs={{0,8},{4,12},{8,0},{12,4},{1,9},{5,13},{9,1},{13,5},{2,10},{6,14},... | collective-permute-start | bytes 2752520 | tf_op jit(solution)/shard_map/ppermute | solution.py:408
  126.3 34.8 %collective-permute-start.26 = (bf16[448,1024]{1,0:T(8,128)(2,1)S(1)}, bf16[448,1024]{1,0:T(8,128)(2,1)S(1)}, u32[]{:S(2)}, u32[]{:S(2)}) collective-permute-start(bf16[448,1024]{1,0:T(8,128)(2,1)S(1)} %collective-permute-done.25.refs_2_), channel_id=1, source_target_pairs={{0,4},{4,0},{8,12},{12,8},{1,5},{5,1},{9,13},{13,9},{2,6},{6,2},{1... | collective-permute-start | bytes 2752520 | tf_op jit(solution)/shard_map/ppermute | solution.py:408
  (9 other events, 54.8 us)

commit v6 on v5

--- a/solution.py
+++ b/solution.py
@@ -24,7 +24,7 @@
 
 def groups_of(rows):
     n = rows // chunk_of(rows)
-    cuts = sorted({0, (n + 1) // 2, n})
+    cuts = sorted({0, n - 1, n})
     return [(a * chunk_of(rows), b * chunk_of(rows)) for a, b in zip(cuts, cuts[1:])]
 
 
@@ -415,7 +415,7 @@
         if axis is not None and n == 4:
             x = sum(parts[1:], parts[0])
             swap = lambda d: lax.ppermute(x, axis, [(a, a ^ d) for a in range(n)])
-            return [x] + [swap(d) for d in range(1, n)]
+            return [x] + [swap(d) for d in reversed(range(1, n))]
         if axis is not None and n & (n - 1) == 0:
             d = 1
             while d < n:
@@ -517,7 +517,7 @@
         x = sum(parts[1:], parts[0])
         if n_hi * n_lo <= 4:
             steps = [(hi, lo) for hi in range(n_hi) for lo in range(n_lo) if hi or lo]
-            parts = [x] + [shift(x, hi=hi, lo=lo) for hi, lo in steps]
+            parts = [x] + [shift(x, hi=hi, lo=lo) for hi, lo in reversed(steps)]
         else:
             parts = exchange([x], None, n_lo, lambda x, d: shift(x, lo=d))
             parts = exchange(parts, None, n_hi, lambda x, d: shift(x, hi=d))

time: 163 us -> 160 us (0.982)
  waiting for transfers between devices: 101 us -> 96.1 us
  starting transfers between devices: 29.5 us -> 31.7 us
    ppermute x17, waiting for transfers between devices: 93.3 us -> 89.7 us  [shift(): return lax.ppermute(x, 'seq', pairs)]
    ppermute x17, starting transfers between devices: 19.5 us -> 21.6 us  [shift(): return lax.ppermute(x, 'seq', pairs)]
    ppermute x6, waiting for transfers between devices: 6.89 us -> 5.24 us  [exchange(): swap = lambda d: lax.ppermute(x, axis, [(a, a ^ d) for a in range(n)])]
  transfers between devices with their start and end apart: 29 -> 29, of which waited for: 16 -> 15; matrix products, arithmetic and copies ran while one was open for 0% -> 0% of each run, Pallas kernels for 15% -> 16%
where the time goes in v6:
time: 160 us
  waiting for transfers between devices  96.1 us (60%)
  starting transfers between devices  31.7 us (20%)
  Pallas kernels  29.1 us (18%)
  local copies, waits for them, and re-layouts  1.89 us (1%)
    ppermute x17, waiting for transfers between devices, shift(): return lax.ppermute(x, 'seq', pairs)  89.7 us
    pallas_call x24, Pallas kernels, call(): pl.pallas_call(kernel, out_shape=out_shape, in_specs=specs or [NEAR] * le...  29.1 us
    ppermute x17, starting transfers between devices, shift(): return lax.ppermute(x, 'seq', pairs)  21.6 us
    ppermute x6, starting transfers between devices, exchange(): swap = lambda d: lax.ppermute(x, axis, [(a, a ^ d) for a in range(n)])  8.84 us
    ppermute x6, waiting for transfers between devices, exchange(): swap = lambda d: lax.ppermute(x, axis, [(a, a ^ d) for a in range(n)])  5.24 us
  transfers between devices with their start and end apart: 29, of which 15 were waited for; matrix products, arithmetic and copies ran while one was open for 0% of the time, Pallas kernels for 16%

profile of v6, /device:TPU:0, one launch (start us, length us, event | category | flops | bytes accessed | tf_op | source)
XLA Modules:
  0.0 159.8 jit_solution(1110943916799890928)
XLA Ops:
  1.2 1.7 %shard_map.85 = (bf16[512,896]{1,0:T(8,128)(2,1)S(1)}, bf16[512,1024]{1,0:T(8,128)(2,1)S(1)}) custom-call(bf16[512,7168]{1,0:T(8,128)(2,1)} %refs_0_.7, bf16[512,1024]{1,0:T(8,128)(2,1)} %grad_out.1), custom_call_target="tpu_custom_call" | custom-call | bytes 3932160 | tf_op jit(solution)/shard_map/pallas_call | solution.py:279
  3.0 1.9 %copy-done = bf16[512,7168]{1,0:T(8,128)(2,1)S(1)} copy-done((bf16[512,7168]{1,0:T(8,128)(2,1)S(1)}, bf16[512,7168]{1,0:T(8,128)(2,1)}, u32[]{:S(2)}) %copy-start) | copy-done | bytes 7340056
  6.8 2.2 %shard_map.91 = (bf16[912,512]{1,0:T(8,128)(2,1)S(1)}, bf16[912,512]{1,0:T(8,128)(2,1)S(1)}) custom-call(bf16[512,896]{1,0:T(8,128)(2,1)S(1)} %collective-permute-done.5.refs_0_, bf16[512,1024]{1,0:T(8,128)(2,1)S(1)} %collective-permute-done.1.refs_3_.refs_1_, f32[896,512]{1,0:T(8,128)S(1)} %get-tuple-element.48.refs_2_, ...), custom_call_target="tpu_custom_call" | custom-call | flops 939524096 | bytes 6586368 | tf_op jit(solution)/shard_map/pallas_call | solution.py:279
  9.0 2.6 %collective-permute-start.6 = (bf16[912,512]{1,0:T(8,128)(2,1)S(1)}, bf16[912,512]{1,0:T(8,128)(2,1)S(1)}, u32[]{:S(2)}, u32[]{:S(2)}) collective-permute-start(bf16[912,512]{1,0:T(8,128)(2,1)S(1)} %get-tuple-element.50), channel_id=1, source_target_pairs={{0,4},{4,0},{8,12},{12,8},{1,5},{5,1},{9,13},{13,9},{2,6},{6,2},{1... | collective-permute-start | bytes 2801672 | tf_op jit(solution)/shard_map/ppermute | solution.py:408
  11.6 1.6 collective-permute-start.9
  13.2 2.6 %shard_map.87 = (bf16[912,512]{1,0:T(8,128)(2,1)S(1)}, f32[896,512]{1,0:T(8,128)S(1)}) custom-call(bf16[512,7168]{1,0:T(8,128)(2,1)S(1)} %copy-done, bf16[512,896]{1,0:T(8,128)(2,1)S(1)} %collective-permute-done.2.refs_1_, bf16[512,1024]{1,0:T(8,128)(2,1)S(1)} %get-tuple-element.41.refs_2_.refs_1_, bf16[512,1024]{1,0:T(8,128)(2,1)S(1)} %collective-permute-done.1.refs_3_.refs_1_), custom_call_target="tpu_custom_call" | custom-call | bytes 1 | tf_op jit(solution)/shard_map/pallas_call | solution.py:279
  16.4 2.6 %shard_map.89 = (f32[896,512]{1,0:T(8,128)S(1)}, bf16[912,512]{1,0:T(8,128)(2,1)S(1)}) custom-call(bf16[512,7168]{1,0:T(8,128)(2,1)S(1)} %copy-done, bf16[512,896]{1,0:T(8,128)(2,1)S(1)} %collective-permute-done.4.refs_1_, bf16[512,1024]{1,0:T(8,128)(2,1)S(1)} %get-tuple-element.41.refs_2_.refs_1_, bf16[512,1024]{1,0:T(8,128)(2,1)S(1)} %collective-permute-done.1.refs_3_.refs_1_), custom_call_target="tpu_custom_call" | custom-call | bytes 1 | tf_op jit(solution)/shard_map/pallas_call | solution.py:279
  19.2 14.0 %collective-permute-done.6.refs_0_ = bf16[912,512]{1,0:T(8,128)(2,1)S(1)} collective-permute-done((bf16[912,512]{1,0:T(8,128)(2,1)S(1)}, bf16[912,512]{1,0:T(8,128)(2,1)S(1)}, u32[]{:S(2)}, u32[]{:S(2)}) %collective-permute-start.6) | collective-permute-done | bytes 933920 | tf_op jit(solution)/shard_map/ppermute | solution.py:408
  34.4 2.1 %collective-permute-start.7 = (bf16[784,512]{1,0:T(8,128)(2,1)S(1)}, bf16[784,512]{1,0:T(8,128)(2,1)S(1)}, u32[]{:S(2)}, u32[]{:S(2)}) collective-permute-start(bf16[784,512]{1,0:T(8,128)(2,1)S(1)} %shard_map.92), channel_id=1, source_target_pairs={{0,8},{4,12},{8,0},{12,4},{1,9},{5,13},{9,1},{13,5},{2,10},{6,14},... | collective-permute-start | bytes 2408456 | tf_op jit(solution)/shard_map/ppermute | solution.py:408
  37.7 1.6 collective-permute-start.10
  40.5 12.7 %collective-permute-done.3.refs_0_ = bf16[912,512]{1,0:T(8,128)(2,1)S(1)} collective-permute-done((bf16[912,512]{1,0:T(8,128)(2,1)S(1)}, bf16[912,512]{1,0:T(8,128)(2,1)S(1)}, u32[]{:S(2)}, u32[]{:S(2)}) %collective-permute-start.3) | collective-permute-done | bytes 933920 | tf_op jit(solution)/shard_map/ppermute | solution.py:408
  53.2 1.9 %collective-permute-start.12 = (bf16[144,512]{1,0:T(8,128)(2,1)S(1)}, bf16[144,512]{1,0:T(8,128)(2,1)S(1)}, u32[]{:S(2)}, u32[]{:S(2)}) collective-permute-start(bf16[144,512]{1,0:T(8,128)(2,1)S(1)} %shard_map.99), channel_id=1, source_target_pairs={{0,4},{4,0},{8,12},{12,8},{1,5},{5,1},{9,13},{13,9},{2,6},{6,2},{1... | collective-permute-start | bytes 442376 | tf_op jit(solution)/shard_map/ppermute | solution.py:408
  55.1 2.1 %shard_map.86 = (f32[896,512]{1,0:T(8,128)S(1)}, f32[896,512]{1,0:T(8,128)S(1)}) custom-call(bf16[512,7168]{1,0:T(8,128)(2,1)S(1)} %copy-done, bf16[512,896]{1,0:T(8,128)(2,1)S(1)} %collective-permute-done.refs_1_, bf16[512,1024]{1,0:T(8,128)(2,1)S(1)} %get-tuple-element.41.refs_2_.refs_1_, bf16[512,1024]{1,0:T(8,128)(2,1)S(1)} %collective-permute-done.1.refs_3_.refs_1_), custom_call_target="tpu_custom_call" | custom-call | bytes 1 | tf_op jit(solution)/shard_map/pallas_call | solution.py:279
  59.1 13.3 %collective-permute-done.7.refs_0_ = bf16[784,512]{1,0:T(8,128)(2,1)S(1)} collective-permute-done((bf16[784,512]{1,0:T(8,128)(2,1)S(1)}, bf16[784,512]{1,0:T(8,128)(2,1)S(1)}, u32[]{:S(2)}, u32[]{:S(2)}) %collective-permute-start.7) | collective-permute-done | bytes 802848 | tf_op jit(solution)/shard_map/ppermute | solution.py:408
  75.3 3.7 %collective-permute-start.13 = (f32[7,128]{1,0:T(8,128)S(1)}, f32[7,128]{1,0:T(8,128)S(1)}, u32[]{:S(2)}, u32[]{:S(2)}) collective-permute-start(f32[7,128]{1,0:T(8,128)S(1)} %get-tuple-element.66.refs_7_), channel_id=1, source_target_pairs={{0,3},{1,2},{2,1},{3,0},{4,7},{5,6},{6,5},{7,4},{8,11},{9,10},{10,... | collective-permute-start | bytes 10760 | tf_op jit(solution)/shard_map/ppermute | solution.py:417
  80.7 2.7 %collective-permute-done.14.refs_9_ = f32[7,128]{1,0:T(8,128)S(1)} collective-permute-done((f32[7,128]{1,0:T(8,128)S(1)}, f32[7,128]{1,0:T(8,128)S(1)}, u32[]{:S(2)}, u32[]{:S(2)}) %collective-permute-start.14) | collective-permute-done | bytes 3616 | tf_op jit(solution)/shard_map/ppermute | solution.py:417
  93.9 2.4 %collective-permute-start.22 = (f32[1,128]{1,0:T(1,128)S(1)}, f32[1,128]{1,0:T(1,128)S(1)}, u32[]{:S(2)}, u32[]{:S(2)}) collective-permute-start(f32[1,128]{1,0:T(1,128)S(1)} %get-tuple-element.70.refs_7_.refs_6_), channel_id=1, source_target_pairs={{0,1},{1,0},{2,3},{3,2},{4,5},{5,4},{6,7},{7,6},{8,9},{9,8},{10,11... | collective-permute-start | bytes 1544 | tf_op jit(solution)/shard_map/ppermute | solution.py:417
  98.5 1.6 collective-permute-start.23
  102.6 19.2 %collective-permute-done.23.refs_0_ = bf16[448,1024]{1,0:T(8,128)(2,1)S(1)} collective-permute-done((bf16[448,1024]{1,0:T(8,128)(2,1)S(1)}, bf16[448,1024]{1,0:T(8,128)(2,1)S(1)}, u32[]{:S(2)}, u32[]{:S(2)}) %collective-permute-start.23) | collective-permute-done | bytes 917536 | tf_op jit(solution)/shard_map/ppermute | solution.py:408
  121.9 1.5 collective-permute-start.24
  126.2 15.4 %collective-permute-done.27.refs_1_ = bf16[448,1024]{1,0:T(8,128)(2,1)S(1)} collective-permute-done((bf16[448,1024]{1,0:T(8,128)(2,1)S(1)}, bf16[448,1024]{1,0:T(8,128)(2,1)S(1)}, u32[]{:S(2)}, u32[]{:S(2)}) %collective-permute-start.27) | collective-permute-done | bytes 917536 | tf_op jit(solution)/shard_map/ppermute | solution.py:408
  141.5 2.3 %shard_map.107 = f32[896,1024]{1,0:T(8,128)} custom-call(f32[768,512]{1,0:T(8,128)S(1)} %get-tuple-element.73.refs_0_, f32[768,512]{1,0:T(8,128)S(1)} %get-tuple-element.57.refs_1_, f32[128,512]{1,0:T(8,128)S(1)} %get-tuple-element.60.refs_2_, f32[128,512]{1,0:T(8,128)S(1)} %get-tuple-element.63.refs_3_, f32[7,128]{1,0:T(8,128)S(1)} %get-tuple-element.67.refs_5_.refs_4_, ...), custom_call_target="tpu_custom_call" | custom-call | bytes 7349760 | tf_op jit(solution)/shard_map/pallas_call | solution.py:279
  143.8 1.9 %shard_map.105.refs_2_ = bf16[3584,1024]{1,0:T(8,128)(2,1)} custom-call(bf16[448,1024]{1,0:T(8,128)(2,1)S(1)} %collective-permute-done.23.refs_0_, bf16[448,1024]{1,0:T(8,128)(2,1)S(1)} %collective-permute-done.27.refs_1_, bf16[448,1024]{1,0:T(8,128)(2,1)S(1)} %collective-permute-done.25.refs_2_, ...), custom_call_target="tpu_custom_call", output_to_operand_aliasing={{}: (4, {})} | custom-call | bytes 7340032 | tf_op jit(solution)/shard_map/pallas_call | solution.py:279
  145.7 12.7 %collective-permute-done.24.refs_0_ = bf16[448,1024]{1,0:T(8,128)(2,1)S(1)} collective-permute-done((bf16[448,1024]{1,0:T(8,128)(2,1)S(1)}, bf16[448,1024]{1,0:T(8,128)(2,1)S(1)}, u32[]{:S(2)}, u32[]{:S(2)}) %collective-permute-start.24) | collective-permute-done | bytes 917536 | tf_op jit(solution)/shard_map/ppermute | solution.py:408
  (67 shorter events, 32.7 us)
Async XLA Ops:
  0.6 6.2 %collective-permute-start.1 = (bf16[512,1024]{1,0:T(8,128)(2,1)}, bf16[512,1024]{1,0:T(8,128)(2,1)S(1)}, u32[]{:S(2)}, u32[]{:S(2)}) collective-permute-start(bf16[512,1024]{1,0:T(8,128)(2,1)} %grad_out.1), channel_id=1, source_target_pairs={{0,16},{16,0},{1,17},{17,1},{2,18},{18,2},{3,19},{19,3},{4,20},{20... | collective-permute-start | bytes 3145736 | tf_op jit(solution)/shard_map/ppermute | solution.py:411
  5.0 8.1 %collective-permute-start.2 = (bf16[512,896]{1,0:T(8,128)(2,1)S(1)}, bf16[512,896]{1,0:T(8,128)(2,1)S(1)}, u32[]{:S(2)}, u32[]{:S(2)}) collective-permute-start(bf16[512,896]{1,0:T(8,128)(2,1)S(1)} %get-tuple-element.43), channel_id=1, source_target_pairs={{0,16},{16,0},{1,17},{17,1},{2,18},{18,2},{3,19},{19,3},{4,20},{20... | collective-permute-start | bytes 2752520 | tf_op jit(solution)/shard_map/ppermute | solution.py:411
  5.2 11.2 %collective-permute-start.4 = (bf16[512,896]{1,0:T(8,128)(2,1)S(1)}, bf16[512,896]{1,0:T(8,128)(2,1)S(1)}, u32[]{:S(2)}, u32[]{:S(2)}) collective-permute-start(bf16[512,896]{1,0:T(8,128)(2,1)S(1)} %get-tuple-element.45), channel_id=1, source_target_pairs={{0,16},{16,0},{1,17},{17,1},{2,18},{18,2},{3,19},{19,3},{4,20},{20... | collective-permute-start | bytes 2752520 | tf_op jit(solution)/shard_map/ppermute | solution.py:411
  9.0 24.2 %collective-permute-start.6 = (bf16[912,512]{1,0:T(8,128)(2,1)S(1)}, bf16[912,512]{1,0:T(8,128)(2,1)S(1)}, u32[]{:S(2)}, u32[]{:S(2)}) collective-permute-start(bf16[912,512]{1,0:T(8,128)(2,1)S(1)} %get-tuple-element.50), channel_id=1, source_target_pairs={{0,4},{4,0},{8,12},{12,8},{1,5},{5,1},{9,13},{13,9},{2,6},{6,2},{1... | collective-permute-start | bytes 2801672 | tf_op jit(solution)/shard_map/ppermute | solution.py:408
  11.6 24.9 %collective-permute-start.9 = (bf16[912,512]{1,0:T(8,128)(2,1)S(1)}, bf16[912,512]{1,0:T(8,128)(2,1)S(1)}, u32[]{:S(2)}, u32[]{:S(2)}) collective-permute-start(bf16[912,512]{1,0:T(8,128)(2,1)S(1)} %get-tuple-element.55), channel_id=1, source_target_pairs={{0,8},{4,12},{8,0},{12,4},{1,9},{5,13},{9,1},{13,5},{2,10},{6,14},... | collective-permute-start | bytes 2801672 | tf_op jit(solution)/shard_map/ppermute | solution.py:408
  15.8 37.4 %collective-permute-start.3 = (bf16[912,512]{1,0:T(8,128)(2,1)S(1)}, bf16[912,512]{1,0:T(8,128)(2,1)S(1)}, u32[]{:S(2)}, u32[]{:S(2)}) collective-permute-start(bf16[912,512]{1,0:T(8,128)(2,1)S(1)} %get-tuple-element.44), channel_id=1, source_target_pairs={{0,4},{4,0},{8,12},{12,8},{1,5},{5,1},{9,13},{13,9},{2,6},{6,2},{1... | collective-permute-start | bytes 2801672 | tf_op jit(solution)/shard_map/ppermute | solution.py:408
  16.4 23.2 %collective-permute-start = (bf16[512,896]{1,0:T(8,128)(2,1)S(1)}, bf16[512,896]{1,0:T(8,128)(2,1)S(1)}, u32[]{:S(2)}, u32[]{:S(2)}) collective-permute-start(bf16[512,896]{1,0:T(8,128)(2,1)S(1)} %get-tuple-element.40), channel_id=1, source_target_pairs={{0,16},{16,0},{1,17},{17,1},{2,18},{18,2},{3,19},{19,3},{4,20},{20... | collective-permute-start | bytes 2752520 | tf_op jit(solution)/shard_map/ppermute | solution.py:411
  19.0 39.1 %collective-permute-start.8 = (bf16[912,512]{1,0:T(8,128)(2,1)S(1)}, bf16[912,512]{1,0:T(8,128)(2,1)S(1)}, u32[]{:S(2)}, u32[]{:S(2)}) collective-permute-start(bf16[912,512]{1,0:T(8,128)(2,1)S(1)} %get-tuple-element.53), channel_id=1, source_target_pairs={{0,8},{4,12},{8,0},{12,4},{1,9},{5,13},{9,1},{13,5},{2,10},{6,14},... | collective-permute-start | bytes 2801672 | tf_op jit(solution)/shard_map/ppermute | solution.py:408
  34.4 37.9 %collective-permute-start.7 = (bf16[784,512]{1,0:T(8,128)(2,1)S(1)}, bf16[784,512]{1,0:T(8,128)(2,1)S(1)}, u32[]{:S(2)}, u32[]{:S(2)}) collective-permute-start(bf16[784,512]{1,0:T(8,128)(2,1)S(1)} %shard_map.92), channel_id=1, source_target_pairs={{0,8},{4,12},{8,0},{12,4},{1,9},{5,13},{9,1},{13,5},{2,10},{6,14},... | collective-permute-start | bytes 2408456 | tf_op jit(solution)/shard_map/ppermute | solution.py:408
  37.7 35.7 %collective-permute-start.10 = (bf16[784,512]{1,0:T(8,128)(2,1)S(1)}, bf16[784,512]{1,0:T(8,128)(2,1)S(1)}, u32[]{:S(2)}, u32[]{:S(2)}) collective-permute-start(bf16[784,512]{1,0:T(8,128)(2,1)S(1)} %shard_map.95), channel_id=1, source_target_pairs={{0,4},{4,0},{8,12},{12,8},{1,5},{5,1},{9,13},{13,9},{2,6},{6,2},{1... | collective-permute-start | bytes 2408456 | tf_op jit(solution)/shard_map/ppermute | solution.py:408
  39.6 35.2 %collective-permute-start.11 = (bf16[144,512]{1,0:T(8,128)(2,1)S(1)}, bf16[144,512]{1,0:T(8,128)(2,1)S(1)}, u32[]{:S(2)}, u32[]{:S(2)}) collective-permute-start(bf16[144,512]{1,0:T(8,128)(2,1)S(1)} %shard_map.97), channel_id=1, source_target_pairs={{0,8},{4,12},{8,0},{12,4},{1,9},{5,13},{9,1},{13,5},{2,10},{6,14},... | collective-permute-start | bytes 442376 | tf_op jit(solution)/shard_map/ppermute | solution.py:408
  53.2 21.8 %collective-permute-start.12 = (bf16[144,512]{1,0:T(8,128)(2,1)S(1)}, bf16[144,512]{1,0:T(8,128)(2,1)S(1)}, u32[]{:S(2)}, u32[]{:S(2)}) collective-permute-start(bf16[144,512]{1,0:T(8,128)(2,1)S(1)} %shard_map.99), channel_id=1, source_target_pairs={{0,4},{4,0},{8,12},{12,8},{1,5},{5,1},{9,13},{13,9},{2,6},{6,2},{1... | collective-permute-start | bytes 442376 | tf_op jit(solution)/shard_map/ppermute | solution.py:408
  75.3 5.5 %collective-permute-start.13 = (f32[7,128]{1,0:T(8,128)S(1)}, f32[7,128]{1,0:T(8,128)S(1)}, u32[]{:S(2)}, u32[]{:S(2)}) collective-permute-start(f32[7,128]{1,0:T(8,128)S(1)} %get-tuple-element.66.refs_7_), channel_id=1, source_target_pairs={{0,3},{1,2},{2,1},{3,0},{4,7},{5,6},{6,5},{7,4},{8,11},{9,10},{10,... | collective-permute-start | bytes 10760 | tf_op jit(solution)/shard_map/ppermute | solution.py:417
  78.9 4.5 %collective-permute-start.14 = (f32[7,128]{1,0:T(8,128)S(1)}, f32[7,128]{1,0:T(8,128)S(1)}, u32[]{:S(2)}, u32[]{:S(2)}) collective-permute-start(f32[7,128]{1,0:T(8,128)S(1)} %get-tuple-element.66.refs_7_), channel_id=1, source_target_pairs={{0,2},{1,3},{2,0},{3,1},{4,6},{5,7},{6,4},{7,5},{8,10},{9,11},{10,... | collective-permute-start | bytes 10760 | tf_op jit(solution)/shard_map/ppermute | solution.py:417
  78.9 4.5 %collective-permute-start.15 = (f32[7,128]{1,0:T(8,128)S(1)}, f32[7,128]{1,0:T(8,128)S(1)}, u32[]{:S(2)}, u32[]{:S(2)}) collective-permute-start(f32[7,128]{1,0:T(8,128)S(1)} %get-tuple-element.66.refs_7_), channel_id=1, source_target_pairs={{0,1},{1,0},{2,3},{3,2},{4,5},{5,4},{6,7},{7,6},{8,9},{9,8},{10,11... | collective-permute-start | bytes 10760 | tf_op jit(solution)/shard_map/ppermute | solution.py:417
  85.6 4.5 %collective-permute-start.17 = (f32[2,1024]{1,0:T(2,128)S(1)}, f32[2,1024]{1,0:T(2,128)S(1)}, u32[]{:S(2)}, u32[]{:S(2)}) collective-permute-start(f32[2,1024]{1,0:T(2,128)S(1)} %add.3.refs_0_), channel_id=1, source_target_pairs={{0,12},{4,8},{8,4},{12,0},{1,13},{5,9},{9,5},{13,1},{2,14},{6,10},... | collective-permute-start | bytes 24584 | tf_op jit(solution)/shard_map/ppermute | solution.py:408
  91.9 5.3 %collective-permute-start.20 = (f32[1,128]{1,0:T(1,128)S(1)}, f32[1,128]{1,0:T(1,128)S(1)}, u32[]{:S(2)}, u32[]{:S(2)}) collective-permute-start(f32[1,128]{1,0:T(1,128)S(1)} %get-tuple-element.70.refs_7_.refs_6_), channel_id=1, source_target_pairs={{0,3},{1,2},{2,1},{3,0},{4,7},{5,6},{6,5},{7,4},{8,11},{9,10},{10,... | collective-permute-start | bytes 1544 | tf_op jit(solution)/shard_map/ppermute | solution.py:417
  93.3 4.4 %collective-permute-start.21 = (f32[1,128]{1,0:T(1,128)S(1)}, f32[1,128]{1,0:T(1,128)S(1)}, u32[]{:S(2)}, u32[]{:S(2)}) collective-permute-start(f32[1,128]{1,0:T(1,128)S(1)} %get-tuple-element.70.refs_7_.refs_6_), channel_id=1, source_target_pairs={{0,2},{1,3},{2,0},{3,1},{4,6},{5,7},{6,4},{7,5},{8,10},{9,11},{10,... | collective-permute-start | bytes 1544 | tf_op jit(solution)/shard_map/ppermute | solution.py:417
  98.5 23.4 %collective-permute-start.23 = (bf16[448,1024]{1,0:T(8,128)(2,1)S(1)}, bf16[448,1024]{1,0:T(8,128)(2,1)S(1)}, u32[]{:S(2)}, u32[]{:S(2)}) collective-permute-start(bf16[448,1024]{1,0:T(8,128)(2,1)S(1)} %get-tuple-element.71.refs_0_), channel_id=1, source_target_pairs={{0,4},{4,0},{8,12},{12,8},{1,5},{5,1},{9,13},{13,9},{2,6},{6,2},{1... | collective-permute-start | bytes 2752520 | tf_op jit(solution)/shard_map/ppermute | solution.py:408
  100.1 23.3 %collective-permute-start.25 = (bf16[448,1024]{1,0:T(8,128)(2,1)S(1)}, bf16[448,1024]{1,0:T(8,128)(2,1)S(1)}, u32[]{:S(2)}, u32[]{:S(2)}) collective-permute-start(bf16[448,1024]{1,0:T(8,128)(2,1)S(1)} %get-tuple-element.72.refs_1_), channel_id=1, source_target_pairs={{0,8},{4,12},{8,0},{12,4},{1,9},{5,13},{9,1},{13,5},{2,10},{6,14},... | collective-permute-start | bytes 2752520 | tf_op jit(solution)/shard_map/ppermute | solution.py:408
  101.6 39.9 %collective-permute-start.27 = (bf16[448,1024]{1,0:T(8,128)(2,1)S(1)}, bf16[448,1024]{1,0:T(8,128)(2,1)S(1)}, u32[]{:S(2)}, u32[]{:S(2)}) collective-permute-start(bf16[448,1024]{1,0:T(8,128)(2,1)S(1)} %get-tuple-element.72.refs_1_), channel_id=1, source_target_pairs={{0,4},{4,0},{8,12},{12,8},{1,5},{5,1},{9,13},{13,9},{2,6},{6,2},{1... | collective-permute-start | bytes 2752520 | tf_op jit(solution)/shard_map/ppermute | solution.py:408
  102.2 41.7 %collective-permute-start.28 = (bf16[448,1024]{1,0:T(8,128)(2,1)S(1)}, bf16[448,1024]{1,0:T(8,128)(2,1)S(1)}, u32[]{:S(2)}, u32[]{:S(2)}) collective-permute-start(bf16[448,1024]{1,0:T(8,128)(2,1)S(1)} %get-tuple-element.71.refs_0_), channel_id=1, source_target_pairs={{0,8},{4,12},{8,0},{12,4},{1,9},{5,13},{9,1},{13,5},{2,10},{6,14},... | collective-permute-start | bytes 2752520 | tf_op jit(solution)/shard_map/ppermute | solution.py:408
  121.9 36.5 %collective-permute-start.24 = (bf16[448,1024]{1,0:T(8,128)(2,1)S(1)}, bf16[448,1024]{1,0:T(8,128)(2,1)S(1)}, u32[]{:S(2)}, u32[]{:S(2)}) collective-permute-start(bf16[448,1024]{1,0:T(8,128)(2,1)S(1)} %collective-permute-done.23.refs_0_), channel_id=1, source_target_pairs={{0,8},{4,12},{8,0},{12,4},{1,9},{5,13},{9,1},{13,5},{2,10},{6,14},... | collective-permute-start | bytes 2752520 | tf_op jit(solution)/shard_map/ppermute | solution.py:408
  123.4 35.0 %collective-permute-start.26 = (bf16[448,1024]{1,0:T(8,128)(2,1)S(1)}, bf16[448,1024]{1,0:T(8,128)(2,1)S(1)}, u32[]{:S(2)}, u32[]{:S(2)}) collective-permute-start(bf16[448,1024]{1,0:T(8,128)(2,1)S(1)} %collective-permute-done.25.refs_2_), channel_id=1, source_target_pairs={{0,4},{4,0},{8,12},{12,8},{1,5},{5,1},{9,13},{13,9},{2,6},{6,2},{1... | collective-permute-start | bytes 2752520 | tf_op jit(solution)/shard_map/ppermute | solution.py:408
  (9 other events, 50.8 us)
